TPU v7x, 32 devices: a whole 2x2x4 slice. The times are simulated.
32 devices in a mesh: section: 2 (over core), expert: 16 (over z, y, x).
Axes of the slice: x: 2, y: 2, z: 4, core: 2. Of those that a mesh axis runs over, the one named last changes fastest.
Arguments:
- block_input: bfloat16 [2, 6144, 768], P(None, 'expert'), may hold values from -6 to 6
- cotangent: bfloat16 [2, 6144, 768], P(None, 'expert'), may hold values from -6 to 6
- lengths: int32 [2, 16, 4], P(None, 'expert'), may hold values from 1 to 288, 384 in all within a row
- routes: int32 [2, 2, 6144, 1], P('section', None, 'expert'), may hold values from 0 to 15; in each aligned block of 384 rows (0 to 383, 384 to 767, ..., all dimensions but the last counted through in order) at most 36 rows name the same one
- norm_gain: float32 [2, 2, 768], P('section'), may hold values from 0.5 to 1.5
- attention_in: bfloat16 [2, 3, 768, 768], P('section', None, 'expert'), may hold values from -0.21875 to 0.21875
- attention_out: bfloat16 [2, 768, 768], P('section', 'expert'), may hold values from -0.875 to 0.875
- position_bias: float32 [2, 32, 12], P('section'), may hold values from -6 to 6
- router: bfloat16 [2, 768, 16], P('section', 'expert'), may hold values from -0.109375 to 0.109375
- expert_up: bfloat16 [2, 16, 768, 3072], P('section', 'expert'), may hold values from -0.21875 to 0.21875
- expert_down: bfloat16 [2, 16, 3072, 768], P('section', 'expert'), may hold values from -3.5 to 3.5
Outputs:
- layer_out: bfloat16 [2, 2, 6144, 768], P('section', None, 'expert')
- input_grad: float32 [2, 2, 6144, 768], P('section', None, 'expert')
- grad_gain: float32 [2, 2, 768], P('section')
- grad_attention_in: float32 [2, 3, 768, 768], P('section', None, 'expert')
- grad_attention_out: float32 [2, 768, 768], P('section', 'expert')
- grad_position_bias: float32 [2, 32, 12], P('section')
- grad_router: float32 [2, 768, 16], P('section', 'expert')
- grad_expert_up: float32 [2, 16, 768, 3072], P('section', 'expert')
- grad_expert_down: float32 [2, 16, 3072, 768], P('section', 'expert')
Inputs may be any that keep to these rules, and one draw needn't show every extreme that they name: Each row holds the lengths of the 4 sequences of one group of one micro-batch; they sum to 384, and the longest in each row is exactly 288. routes[s, m, t, 0] is the expert that token t of micro-batch m uses in section s. Among the 384 tokens of one group of one micro-batch (the rows of one device, aligned blocks), no expert is named more than 36 times, and in every draw some group names one expert exactly 36 times.
All inputs are finite; a program needn't handle non-finite values.
Results may differ from a plain program's by a relative error of at most 0.023.
Values may be sent and summed in bfloat16 or wider, within the bound.
No kernel may reach another device: no remote copies, remote signals or barrier semaphores. Data moves between devices by JAX's collectives and lax.ppermute only.
A program may use at most 320 MiB of HBM per device.

v0:
```python
import jax
import jax.numpy as jnp
from jax import lax
from jax.sharding import PartitionSpec as P

bucket_edges = (12, 16, 23, 32, 46, 64, 91)
norm_eps = 1e-06
gelu_c = 0.7978845608028654
gelu_cube = 0.044715
masked_score = -1e30
highest = lax.Precision.HIGHEST


def passed_along(block, axis, distance):
    devices = range(lax.axis_size(axis))
    route = [(i - distance, i) for i in devices if i - distance in devices]
    return lax.ppermute(block, axis, route)


def split_up(value, dim, devices):
    before, after = (value.shape[:dim], value.shape[dim + 1 :])
    return jnp.moveaxis(value.reshape(*before, devices, -1, *after), dim, 0)


def sent_and_summed(value, axis, dim):
    devices = lax.axis_size(axis)
    tiles = lax.all_to_all(split_up(value, dim, devices), axis, 0, 0, tiled=True)
    return jnp.sum(tiles.astype(jnp.float32), axis=0)


def in_one_piece(arrays, axis, dim, along):
    ends, at = ([], 0)
    for a in arrays[:-1]:
        at += a.shape[along]
        ends.append(at)
    both = jnp.concatenate(arrays, axis=along)
    return tuple(jnp.split(sent_and_summed(both, axis, dim), ends, axis=along))


def product(left, right):
    return jnp.dot(left, right, preferred_element_type=jnp.float32)


def product_lead(left, right):
    return lax.dot_general(
        left, right, (((0,), (0,)), ((), ())), preferred_element_type=jnp.float32
    )


def product_last(left, right):
    return lax.dot_general(
        left, right, (((1,), (1,)), ((), ())), preferred_element_type=jnp.float32
    )


def gelu_pair(value):
    inner = jnp.tanh(gelu_c * (value + gelu_cube * value * value * value))
    result = 0.5 * value * (1.0 + inner)
    slope = 0.5 * (1.0 + inner) + 0.5 * value * (1.0 - inner * inner) * gelu_c * (
        1.0 + 3.0 * gelu_cube * value * value
    )
    return (result, slope)


def bucket_of(offset):
    distance = jnp.abs(offset)
    found = 16 * (offset > 0).astype(jnp.int32) + jnp.minimum(distance, 8)
    for edge in bucket_edges:
        found = found + (distance >= edge).astype(jnp.int32)
    return found


def norm_scale(values):
    return lax.rsqrt(jnp.mean(values * values, axis=-1, keepdims=True) + norm_eps)


def norm_forward(values, gain):
    return values * norm_scale(values) * gain


def norm_backward(values, gain, grad_normed):
    scale = norm_scale(values)
    normal = values * scale
    inner = grad_normed * gain
    grad_values = scale * (inner - normal * jnp.mean(inner * normal, axis=-1, keepdims=True))
    return (grad_values, jnp.sum(grad_normed * normal, axis=0))


def spread_line(line, rows):
    heads = line.shape[0]
    tiled = jnp.broadcast_to(line[:, None, :], (heads, rows, 2 * rows - 1)).reshape(heads, -1)
    trimmed = tiled[:, rows - 1 : rows - 1 + rows * (2 * rows - 2)]
    return trimmed.reshape(heads, rows, 2 * rows - 2)[:, :, :rows]


def diagonal_sums(grid, rows):
    heads = grid.shape[0]
    padded = jnp.pad(grid, ((0, 0), (0, 0), (0, rows - 2))).reshape(heads, -1)
    padded = jnp.pad(padded, ((0, 0), (rows - 1, 1)))
    return jnp.sum(padded.reshape(heads, rows, 2 * rows - 1), axis=1, dtype=jnp.float32)


def attention_scores(queries, keys, bias, same):
    scale = queries.shape[-1] ** (-0.5)
    scores = (
        jnp.einsum("ihd,jhd->hij", queries, keys, preferred_element_type=jnp.float32) * scale + bias
    )
    return jnp.where(same[None], scores, masked_score)


def attention_forward(normed_low, project_in, project_out, bias, same):
    rows, width = normed_low.shape
    heads = bias.shape[0]
    queries = product(normed_low, project_in[0]).astype(jnp.bfloat16).reshape(rows, heads, -1)
    keys = product(normed_low, project_in[1]).astype(jnp.bfloat16).reshape(rows, heads, -1)
    values = product(normed_low, project_in[2]).astype(jnp.bfloat16).reshape(rows, heads, -1)
    scores = attention_scores(queries, keys, bias, same)
    top = jnp.max(scores, axis=-1, keepdims=True)
    raised = jnp.exp(scores - top)
    total = jnp.sum(raised, axis=-1, keepdims=True)
    shares = (raised / total).astype(jnp.bfloat16)
    mixed = jnp.einsum("hij,jhd->ihd", shares, values, preferred_element_type=jnp.float32)
    mixed = mixed.astype(jnp.bfloat16).reshape(rows, width)
    return (product(mixed, project_out), (queries, keys, values, mixed, top + jnp.log(total)))


def attention_backward(normed_low, grad_low, kept, project_in, project_out, bias, same):
    queries, keys, values, mixed, log_total = kept
    rows, width = normed_low.shape
    heads = bias.shape[0]
    scale = queries.shape[-1] ** (-0.5)
    grad_out_proj = product_lead(mixed, grad_low)
    grad_mixed = product_last(grad_low, project_out).astype(jnp.bfloat16).reshape(rows, heads, -1)
    shares = jnp.exp(attention_scores(queries, keys, bias, same) - log_total)
    grad_shares = jnp.einsum("ihd,jhd->hij", grad_mixed, values, preferred_element_type=jnp.float32)
    grad_scores = shares * (grad_shares - jnp.sum(shares * grad_shares, axis=-1, keepdims=True))
    grad_scores = grad_scores.astype(jnp.bfloat16)
    grad_values = jnp.einsum(
        "hij,ihd->jhd", shares.astype(jnp.bfloat16), grad_mixed, preferred_element_type=jnp.float32
    )
    grad_queries = (
        jnp.einsum("hij,jhd->ihd", grad_scores, keys, preferred_element_type=jnp.float32) * scale
    )
    grad_keys = (
        jnp.einsum("hij,ihd->jhd", grad_scores, queries, preferred_element_type=jnp.float32) * scale
    )
    grad_queries = grad_queries.astype(jnp.bfloat16).reshape(rows, width)
    grad_keys = grad_keys.astype(jnp.bfloat16).reshape(rows, width)
    grad_values = grad_values.astype(jnp.bfloat16).reshape(rows, width)
    grad_in_proj = jnp.stack(
        [
            product_lead(normed_low, grad_queries),
            product_lead(normed_low, grad_keys),
            product_lead(normed_low, grad_values),
        ]
    )
    grad_normed = (
        product_last(grad_queries, project_in[0])
        + product_last(grad_keys, project_in[1])
        + product_last(grad_values, project_in[2])
    )
    return (grad_normed, grad_in_proj, grad_out_proj, diagonal_sums(grad_scores, rows))


def body(
    block_input,
    cotangent,
    lengths,
    routes,
    norm_gain,
    attention_in,
    attention_out,
    position_bias,
    router,
    expert_up,
    expert_down,
):
    micro, rows, width = block_input.shape
    section = lax.axis_index("section")
    first = section == 0
    gains = norm_gain[0]
    table = position_bias[0]
    up_weight = expert_up[0, 0]
    down_weight = expert_down[0, 0]
    experts = router.shape[2]
    capacity = max(2, 3 * rows // (2 * experts))
    project_in, project_out, router_all = (
        lax.all_gather(attention_in, "expert", axis=2, tiled=True),
        lax.all_gather(attention_out, "expert", axis=1, tiled=True),
        lax.all_gather(router, "expert", axis=1, tiled=True),
    )
    project_in = project_in[0]
    project_out = project_out[0]
    router_all = router_all[0]
    offsets = jnp.arange(2 * rows - 1, dtype=jnp.int32) - (rows - 1)
    bucket_hot = (
        bucket_of(offsets)[:, None] == jnp.arange(table.shape[0], dtype=jnp.int32)[None, :]
    ).astype(jnp.float32)
    bias = spread_line(jnp.dot(bucket_hot, table, precision=highest).T, rows)
    positions = jnp.arange(rows, dtype=jnp.int32)
    slots = jnp.arange(experts * capacity, dtype=jnp.int32)
    expert_ids = jnp.arange(experts, dtype=jnp.int32)

    def layout(index):
        bounds = jnp.cumsum(lax.dynamic_index_in_dim(lengths, index, 0, keepdims=False)[0])
        segment = jnp.sum((positions[:, None] >= bounds[None, :]).astype(jnp.int32), axis=1)
        same = segment[:, None] == segment[None, :]
        route = lax.dynamic_index_in_dim(routes[0], index, 0, keepdims=False)[:, 0]
        chosen = route[:, None] == expert_ids[None, :]
        chosen_int = chosen.astype(jnp.int32)
        earlier = jnp.cumsum(chosen_int, axis=0) - chosen_int
        place = route * capacity + jnp.sum(jnp.where(chosen, earlier, 0), axis=1)
        dispatch = (place[:, None] == slots[None, :]).astype(jnp.bfloat16)
        return (same, chosen, dispatch)

    def masked(tree, live):
        return jax.tree.map(lambda leaf: jnp.where(live, leaf, jnp.zeros_like(leaf)), tree)

    def added(left, right):
        if left is None:
            return right
        return jax.tree.map(jnp.add, left, right)

    outputs = []
    kept_all = []
    received = jnp.zeros((rows, width), jnp.bfloat16)
    for tick in range(micro + 1):
        index = jnp.clip(tick - section, 0, micro - 1)
        layer_in = jnp.where(first, block_input[min(tick, micro - 1)], received)
        forward_same, forward_chosen, forward_dispatch = layout(index)
        wide = layer_in.astype(jnp.float32)
        forward_normed_one = norm_forward(wide, gains[0]).astype(jnp.bfloat16)
        attended, forward_attention_kept = attention_forward(
            forward_normed_one, project_in, project_out, bias, forward_same
        )
        forward_middle = wide + attended
        forward_normed_two = norm_forward(forward_middle, gains[1]).astype(jnp.bfloat16)
        logits = product(forward_normed_two, router_all)
        top = jnp.max(logits, axis=1, keepdims=True)
        raised = jnp.exp(logits - top)
        forward_shares = raised / jnp.sum(raised, axis=1, keepdims=True)
        forward_gate = jnp.sum(
            jnp.where(forward_chosen, forward_shares, 0.0), axis=1, keepdims=True
        )
        send = (
            product_lead(forward_dispatch, forward_normed_two)
            .astype(jnp.bfloat16)
            .reshape(experts, capacity, width)
        )
        expert_arrived = lax.all_to_all(send, "expert", split_axis=0, concat_axis=0, tiled=True)
        expert_flat = expert_arrived.reshape(-1, width)
        pre_gelu = product(expert_flat, up_weight)
        expert_active, expert_slope = gelu_pair(pre_gelu)
        result = product(expert_active.astype(jnp.bfloat16), down_weight).astype(jnp.bfloat16)
        returned = result.reshape(expert_arrived.shape)
        forward_pre_gelu = pre_gelu.reshape(expert_arrived.shape[0], expert_arrived.shape[1], -1)
        came_back = lax.all_to_all(returned, "expert", split_axis=0, concat_axis=0, tiled=True)
        forward_combined = product(forward_dispatch, came_back.reshape(-1, width))
        output = forward_middle + forward_gate * forward_combined
        result = output
        kept = (
            layer_in,
            forward_normed_one,
            forward_attention_kept,
            forward_middle,
            forward_normed_two,
            forward_shares,
            forward_gate,
            forward_combined,
            expert_arrived,
            forward_pre_gelu,
        )
        result = result.astype(jnp.bfloat16)
        outputs.append(result)
        kept_all.append(kept)
        if tick < micro:
            received = passed_along(result, "section", 1)
    input_grads = []
    shared_total = None
    small_total = None
    owned_total = None
    arrived_grad = jnp.zeros((rows, width), jnp.bfloat16)
    for tick in range(micro + 1):
        number = tick - 1 + section
        index = jnp.clip(number, 0, micro - 1)
        live = (number >= 0) & (number < micro)
        earlier_kept = kept_all[max(tick - 1, 0)]
        later_kept = kept_all[min(tick + 1, micro)]
        kept = tuple(
            (
                jax.tree.map(
                    lambda left, right: jnp.where(first, left, right),
                    earlier_kept[place_at],
                    later_kept[place_at],
                )
                for place_at in range(len(earlier_kept))
            )
        )
        grad_output = jnp.where(
            first,
            arrived_grad.astype(jnp.float32),
            cotangent[min(tick, micro - 1)].astype(jnp.float32),
        )
        (
            backward_layer_in,
            normed_one,
            attention_kept,
            middle,
            normed_two,
            shares,
            gate,
            combined,
            arrived,
            pre_kept,
        ) = kept
        backward_same, backward_chosen, backward_dispatch = layout(index)
        grad_combined = (gate * grad_output).astype(jnp.bfloat16)
        grad_gate = jnp.sum(grad_output * combined, axis=1, keepdims=True)
        grad_logits = (grad_gate * gate * (backward_chosen.astype(jnp.float32) - shares)).astype(
            jnp.bfloat16
        )
        grad_router = product_lead(normed_two, grad_logits)
        grad_send = (
            product_lead(backward_dispatch, grad_combined)
            .astype(jnp.bfloat16)
            .reshape(experts, capacity, width)
        )
        grad_arrived = lax.all_to_all(
            grad_send, "expert", split_axis=0, concat_axis=0, tiled=True
        ).reshape(-1, width)
        flat = arrived.reshape(-1, width)
        pre_flat = pre_kept.reshape(flat.shape[0], -1)
        active, slope = gelu_pair(pre_flat)
        grad_down = product_lead(active.astype(jnp.bfloat16), grad_arrived)
        grad_pre = (product_last(grad_arrived, down_weight) * slope).astype(jnp.bfloat16)
        grad_up = product_lead(flat, grad_pre)
        grad_flat = product_last(grad_pre, up_weight).astype(jnp.bfloat16).reshape(arrived.shape)
        grad_back = lax.all_to_all(grad_flat, "expert", split_axis=0, concat_axis=0, tiled=True)
        grad_two = product(backward_dispatch, grad_back.reshape(-1, width)) + product_last(
            grad_logits, router_all
        )
        grad_middle, gain_two = norm_backward(middle, gains[1], grad_two)
        grad_middle = grad_middle + grad_output
        grad_one, grad_in_proj, grad_out_proj, grad_line = attention_backward(
            normed_one,
            grad_middle.astype(jnp.bfloat16),
            attention_kept,
            project_in,
            project_out,
            bias,
            backward_same,
        )
        grad_inputs, gain_one = norm_backward(
            backward_layer_in.astype(jnp.float32), gains[0], grad_one
        )
        shared = (grad_in_proj, grad_out_proj, grad_router)
        small = (jnp.stack([gain_one, gain_two]), grad_line)
        grad_inputs, shared, small, owned = (
            grad_inputs + grad_middle,
            shared,
            small,
            (grad_up, grad_down),
        )
        input_grads.append(grad_inputs)
        shared = masked(shared, live)
        shared_total = added(shared_total, shared)
        small_total = added(small_total, masked(small, live))
        owned_total = added(owned_total, masked(owned, live))
        if tick < micro:
            arrived_grad = passed_along(grad_inputs.astype(jnp.bfloat16), "section", -1)
    shared_total = (
        sent_and_summed(shared_total[0].astype(jnp.bfloat16), "expert", 1),
        *in_one_piece(
            (shared_total[1].astype(jnp.bfloat16), shared_total[2].astype(jnp.bfloat16)),
            "expert",
            0,
            1,
        ),
    )
    table_grad = lax.dot_general(
        bucket_hot, small_total[1], (((0,), (1,)), ((), ())), precision=highest
    )
    grad_gain, grad_table = lax.psum((small_total[0], table_grad), "expert")
    layer_out = jnp.stack(
        [jnp.where(first, outputs[which], outputs[which + 1]) for which in range(micro)]
    )[None]
    input_grad = jnp.stack(
        [jnp.where(first, input_grads[which + 1], input_grads[which]) for which in range(micro)]
    )[None]
    return (
        layer_out,
        input_grad,
        grad_gain[None],
        shared_total[0][None],
        shared_total[1][None],
        grad_table[None],
        shared_total[2][None],
        owned_total[0][None, None],
        owned_total[1][None, None],
    )


def solution(mesh):
    in_specs = (
        P(None, "expert", None),
        P(None, "expert", None),
        P(None, "expert", None),
        P("section", None, "expert", None),
        P("section", None, None),
        P("section", None, "expert", None),
        P("section", "expert", None),
        P("section", None, None),
        P("section", "expert", None),
        P("section", "expert", None, None),
        P("section", "expert", None, None),
    )
    out_specs = (
        P("section", None, "expert", None),
        P("section", None, "expert", None),
        P("section", None, None),
        P("section", None, "expert", None),
        P("section", "expert", None),
        P("section", None, None),
        P("section", "expert", None),
        P("section", "expert", None, None),
        P("section", "expert", None, None),
    )
    return jax.shard_map(body, mesh=mesh, in_specs=in_specs, out_specs=out_specs, check_vma=False)
```

profile of v0, /device:TPU:0, one launch (start us, length us, event | category | flops | bytes accessed | tf_op | source)
XLA Modules:
  0.0 1167.2 jit_solution(18155459836187180459)
XLA Ops:
  18.5 23.2 %reshape.1070 = f32[12,294528]{1,0:T(8,128)} reshape(f32[12,384,767]{2,1,0:T(8,128)} %broadcast_in_dim.78) | data formatting | bytes 28274688 | tf_op jit(solution)/shard_map/reshape | solution.py:91
  41.7 16.6 %slice.127 = f32[12,294144]{1,0:T(8,128)} slice(f32[12,294528]{1,0:T(8,128)} %reshape.1070), slice={[0:12], [383:294527]} | slice | bytes 28237824 | tf_op jit(solution)/shard_map/slice | solution.py:92
  58.3 30.7 %reshape.1071 = f32[12,384,766]{2,1,0:T(8,128)} reshape(f32[12,294144]{1,0:T(8,128)} %slice.127) | data formatting | bytes 28237824 | tf_op jit(solution)/shard_map/reshape | solution.py:93
  95.5 8.2 copy.353
  125.3 16.9 %all-gather.5.cloned.1.call-done = bf16[1,768,768]{2,1,0:T(8,128)(2,1)} async-done(((bf16[1,48,768]{2,1,0:T(8,128)(2,1)}), bf16[1,768,768]{2,1,0:T(8,128)(2,1)}) %all-gather.5.cloned.1.call-update) | async-done | bytes 1179664 | tf_op jit(solution)/shard_map/all_gather | solution.py:189
  146.4 27.9 %all_to_all.70 = bf16[16,36,768]{2,1,0:T(8,128)(2,1)S(1)} all-to-all(bf16[16,36,768]{2,1,0:T(8,128)(2,1)S(1)} %reshape.1074), channel_id=1, replica_groups=mesh['section'=2,'expert'=16] {'expert'}, dimensions={0} | all-to-all | bytes 1769472 | tf_op jit(solution)/shard_map/all_to_all | solution.py:250
  196.1 50.8 %all_gather.11 = bf16[1,768,16]{2,0,1:T(2,128)(2,1)S(1)} all-gather(bf16[1,48,16]{2,0,1:T(2,128)(2,1)S(1)} %copy.269), channel_id=1, replica_groups=mesh['section'=2,'expert'=16] {'expert'}, dimensions={1}, use_global_device_ids=true | all-gather | bytes 26112 | tf_op jit(solution)/shard_map/all_gather | solution.py:190
  302.2 15.2 %all-to-all-done.2 = bf16[16,36,768]{2,1,0:T(8,128)(2,1)S(1)} async-done(((bf16[16,36,768]{2,1,0:T(8,128)(2,1)}), bf16[16,36,768]{2,1,0:T(8,128)(2,1)S(1)}, u32[]{:S(2)}, u32[]{:S(2)}) %all-to-all-start.2) | async-done | bytes 884768 | tf_op jit(solution)/shard_map/all_to_all | solution.py:250
  326.4 7.5 fusion.122
  349.9 12.0 %all-to-all-done.3 = bf16[16,36,768]{2,1,0:T(8,128)(2,1)} async-done(((bf16[16,36,768]{2,1,0:T(8,128)(2,1)}), bf16[16,36,768]{2,1,0:T(8,128)(2,1)}, u32[]{:S(2)}, u32[]{:S(2)}) %all-to-all-start.3) | async-done | bytes 884768 | tf_op jit(solution)/shard_map/all_to_all | solution.py:257
  432.9 9.3 fusion.21
  452.3 12.0 %fusion.63 = f32[3072,768]{1,0:T(8,128)} fusion(bf16[576,768]{1,0:T(8,128)(2,1)} %reshape.1107, f32[576,3072]{1,0:T(8,128)} %copy-done.259, f32[576,3072]{1,0:T(8,128)} %copy-done.260, pred[]{:T(512)S(6)} %eq.346), kind=kOutput, calls=%fused_computation.102 | convolution fusion | flops 2735603712 | bytes 24477696 | tf_op jit(solution)/shard_map/dot_general | solution.py:45
  480.4 7.5 fusion.127
  560.5 23.2 %reshape.1137 = bf16[12,294144]{1,0:T(8,128)(2,1)} reshape(bf16[12,384,766]{2,1,0:T(8,128)(2,1)} %pad.20.clone) | data formatting | bytes 14118912 | tf_op jit(solution)/shard_map/reshape | solution.py:98
  600.9 11.5 pad_convert_fusion.2
  613.6 30.0 %reshape.1144 = f32[12,384,767]{2,1,0:T(8,128)} reshape(f32[12,294528]{1,0:T(8,128)} %pad_convert_fusion.2) | data formatting | bytes 28274688 | tf_op jit(solution)/shard_map/convert_element_type | solution.py:100
  661.9 9.8 fusion.28
  681.9 7.5 all-to-all-start.9
  691.5 12.0 %fusion.64 = f32[3072,768]{1,0:T(8,128)} fusion(bf16[576,768]{1,0:T(8,128)(2,1)S(1)} %copy-done.143, f32[576,3072]{1,0:T(8,128)} %copy-done.259, f32[576,3072]{1,0:T(8,128)} %copy-done.261, pred[]{:T(512)S(6)} %eq.346), kind=kOutput, calls=%fused_computation.103 | convolution fusion | flops 2735603712 | bytes 24477696 | tf_op jit(solution)/shard_map/dot_general | solution.py:45
  703.5 9.1 all-to-all-done.9
  765.2 23.2 %reshape.1138 = bf16[12,294144]{1,0:T(8,128)(2,1)} reshape(bf16[12,384,766]{2,1,0:T(8,128)(2,1)} %pad.22.clone) | data formatting | bytes 14118912 | tf_op jit(solution)/shard_map/reshape | solution.py:98
  799.0 11.5 pad_convert_fusion.1
  811.7 30.2 %reshape.1145 = f32[12,384,767]{2,1,0:T(8,128)} reshape(f32[12,294528]{1,0:T(8,128)} %pad_convert_fusion.1) | data formatting | bytes 28274688 | tf_op jit(solution)/shard_map/convert_element_type | solution.py:100
  859.8 9.8 fusion.35
  887.0 11.9 %add_bitcast_fusion = f32[1,1,3072,768]{3,2,1,0:T(8,128)} fusion(f32[3072,768]{1,0:T(8,128)} %fusion.64, f32[3072,768]{1,0:T(8,128)} %fusion.63, bf16[576,768]{1,0:T(8,128)(2,1)} %copy-done.144, pred[]{:T(512)S(6)} %and.12, pred[]{:T(512)S(6)} %and.11, pred[]{:T(512)S(6)} %and.10, f32[576,3072]{1,0:T(8,128)} %copy-done.260, f32[576,3072]{1,0:T(8,128)} %copy-done.261, ...), kind=kOutput, calls=%fused_computation.9 | convolution fusion | flops 2747400192 | bytes 43352068 | tf_op jit(solution)/shard_map/dot_general | solution.py:45
  899.0 11.2 add_bitcast_fusion.1
  939.8 23.4 %reshape.1139 = bf16[12,294144]{1,0:T(8,128)(2,1)} reshape(bf16[12,384,766]{2,1,0:T(8,128)(2,1)} %pad.24.clone) | data formatting | bytes 14118912 | tf_op jit(solution)/shard_map/reshape | solution.py:98
  988.0 17.6 %all-to-all-done.13 = bf16[16,48,784]{2,1,0:T(8,128)(2,1)} async-done(((bf16[16,48,784]{2,1,0:T(8,128)(2,1)}), bf16[16,48,784]{2,1,0:T(8,128)(2,1)}, u32[]{:S(2)}, u32[]{:S(2)}) %all-to-all-start.13) | async-done | bytes 1204256 | tf_op jit(solution)/shard_map/all_to_all | solution.py:27
  1005.6 8.2 all-to-all-start.12
  1013.9 11.6 pad_convert_fusion
  1030.1 30.1 %reshape.1146 = f32[12,384,767]{2,1,0:T(8,128)} reshape(f32[12,294528]{1,0:T(8,128)} %pad_convert_fusion) | data formatting | bytes 28274688 | tf_op jit(solution)/shard_map/convert_element_type | solution.py:100
  1066.8 83.1 %all-reduce.6 = (f32[1,2,768]{2,1,0:T(2,128)}, f32[1,32,12]{1,2,0:T(8,128)S(1)}) all-reduce(f32[1,2,768]{2,1,0:T(2,128)S(1)} %fusion.310, f32[1,32,12]{1,2,0:T(8,128)S(1)} %convolution_bitcast_fusion.10), channel_id=1, replica_groups=mesh['section'=2,'expert'=16] {'expert'}, use_global_device_ids=true, to_apply=%region_75.76 | all-reduce | flops 1920 | bytes 15360 | tf_op jit(solution)/shard_map/psum | solution.py:383
  (852 shorter events, 537.0 us)
Async XLA Ops:
  7.2 101.2 %all-gather.3.cloned.1.call-start = ((), (), s32[]{:S(2)}) async-start(), calls=%async_computation.14 | async-start | bytes 3760128 | tf_op jit(solution)/shard_map/all_gather | solution.py:188
  7.9 134.3 %all-gather.5.cloned.1.call-start = ((), (), s32[]{:S(2)}) async-start(), calls=%async_computation.15 | async-start | bytes 1253376 | tf_op jit(solution)/shard_map/all_gather | solution.py:189
  11.4 101.8 %copy-start.226 = (f32[384]{0:T(512)}, f32[384]{0:T(512)S(1)}, u32[]{:S(2)}) copy-start(f32[384]{0:T(512)S(1)} %add_rsqrt_fusion.11) | copy-start | bytes 4612
  105.3 143.2 %copy-start.185 = (s32[384]{0:T(512)}, s32[384]{0:T(512)S(1)}, u32[]{:S(2)}) copy-start(s32[384]{0:T(512)S(1)} %get-tuple-element.73) | copy-start | bytes 4612
  105.3 195.7 %copy-start.183 = (s32[384]{0:T(512)}, s32[384]{0:T(512)S(1)}, u32[]{:S(2)}) copy-start(s32[384]{0:T(512)S(1)} %get-tuple-element.69) | copy-start | bytes 4612
  105.3 196.3 %copy-start.181 = (s32[384]{0:T(512)}, s32[384]{0:T(512)S(1)}, u32[]{:S(2)}) copy-start(s32[384]{0:T(512)S(1)} %get-tuple-element.68) | copy-start | bytes 4612
  144.2 111.9 %copy-start.47 = (f32[384,768]{1,0:T(8,128)}, f32[384,768]{1,0:T(8,128)S(1)}, u32[]{:S(2)}) copy-start(f32[384,768]{1,0:T(8,128)S(1)} %get-tuple-element.124) | copy-start | bytes 3538948
  192.0 63.9 %all-to-all-start.1 = ((bf16[16,36,768]{2,1,0:T(8,128)(2,1)}), bf16[16,36,768]{2,1,0:T(8,128)(2,1)S(1)}, u32[]{:S(2)}, u32[]{:S(2)}) async-start(bf16[16,36,768]{2,1,0:T(8,128)(2,1)} %reshape.1076), calls=%async_computation.1 | async-start | bytes 1966080 | tf_op jit(solution)/shard_map/all_to_all | solution.py:257
  258.4 11.5 collective-permute-start
  285.2 235.0 %copy-start.8 = (bf16[384,768]{0,1:T(8,128)(2,1)}, bf16[384,768]{0,1:T(8,128)(2,1)S(1)}, u32[]{:S(2)}) copy-start(bf16[384,768]{0,1:T(8,128)(2,1)S(1)} %copy.274) | copy-start | bytes 1769476
  296.2 21.1 %all-to-all-start.2 = ((bf16[16,36,768]{2,1,0:T(8,128)(2,1)}), bf16[16,36,768]{2,1,0:T(8,128)(2,1)S(1)}, u32[]{:S(2)}, u32[]{:S(2)}) async-start(bf16[16,36,768]{2,1,0:T(8,128)(2,1)} %reshape.1085), calls=%async_computation.2 | async-start | bytes 1966080 | tf_op jit(solution)/shard_map/all_to_all | solution.py:250
  301.0 109.6 %copy-start.230 = (s32[384]{0:T(512)}, s32[384]{0:T(512)S(1)}, u32[]{:S(2)}) copy-start(s32[384]{0:T(512)S(1)} %multiply_add_fusion.11) | copy-start | bytes 4612
  336.0 25.9 %all-to-all-start.3 = ((bf16[16,36,768]{2,1,0:T(8,128)(2,1)}), bf16[16,36,768]{2,1,0:T(8,128)(2,1)}, u32[]{:S(2)}, u32[]{:S(2)}) async-start(bf16[16,36,768]{2,1,0:T(8,128)(2,1)} %reshape.1087), calls=%async_computation.3 | async-start | bytes 1966080 | tf_op jit(solution)/shard_map/all_to_all | solution.py:257
  349.2 160.7 %copy-start.145 = (f32[384,16]{0,1:T(8,128)}, f32[384,16]{0,1:T(8,128)S(1)}, u32[]{:S(2)}) copy-start(f32[384,16]{0,1:T(8,128)S(1)} %get-tuple-element.134) | copy-start | bytes 73732
  349.2 160.7 %copy-start.177 = (f32[384]{0:T(512)}, f32[384]{0:T(512)S(1)}, u32[]{:S(2)}) copy-start(f32[384]{0:T(512)S(1)} %get-tuple-element.133) | copy-start | bytes 4612
  349.2 160.7 %copy-start.197 = (f32[384]{0:T(512)}, f32[384]{0:T(512)S(1)}, u32[]{:S(2)}) copy-start(f32[384]{0:T(512)S(1)} %fusion.303) | copy-start | bytes 4612
  369.1 13.0 %collective-permute-start.1 = (bf16[384,768]{1,0:T(8,128)(2,1)}, bf16[384,768]{1,0:T(8,128)(2,1)}, u32[]{:S(2)}, u32[]{:S(2)}) collective-permute-start(bf16[384,768]{1,0:T(8,128)(2,1)} %get-tuple-element.99), channel_id=1, source_target_pairs={{0,16},{1,17},{2,18},{3,19},{4,20},{5,21},{6,22},{7,23},{8,24},{9,... | collective-permute-start | bytes 1769480 | tf_op jit(solution)/shard_map/ppermute | solution.py:17
  375.2 48.1 %all-to-all-start.6 = ((bf16[16,36,768]{2,1,0:T(8,128)(2,1)}), bf16[16,36,768]{2,1,0:T(8,128)(2,1)}, u32[]{:S(2)}, u32[]{:S(2)}) async-start(bf16[16,36,768]{2,1,0:T(8,128)(2,1)} %reshape.1106), calls=%async_computation.6 | async-start | bytes 1966080 | tf_op jit(solution)/shard_map/all_to_all | solution.py:328
  410.6 99.3 %copy-start.56 = (f32[384,768]{1,0:T(8,128)}, f32[384,768]{1,0:T(8,128)S(1)}, u32[]{:S(2)}) copy-start(f32[384,768]{1,0:T(8,128)S(1)} %get-tuple-element.106) | copy-start | bytes 3538948
  420.3 239.0 %copy-start.195 = (f32[384]{0:T(512)}, f32[384]{0:T(512)S(1)}, u32[]{:S(2)}) copy-start(f32[384]{0:T(512)S(1)} %select_reduce_fusion) | copy-start | bytes 4612
  423.3 41.0 %all-to-all-start.4 = ((bf16[16,36,768]{2,1,0:T(8,128)(2,1)}), bf16[16,36,768]{2,1,0:T(8,128)(2,1)S(1)}, u32[]{:S(2)}, u32[]{:S(2)}) async-start(bf16[16,36,768]{2,1,0:T(8,128)(2,1)} %reshape.1096), calls=%async_computation.4 | async-start | bytes 1966080 | tf_op jit(solution)/shard_map/all_to_all | solution.py:250
  464.3 34.5 %all-to-all-start.7 = ((bf16[16,36,768]{2,1,0:T(8,128)(2,1)}), bf16[16,36,768]{2,1,0:T(8,128)(2,1)}, u32[]{:S(2)}, u32[]{:S(2)}) async-start(bf16[16,36,768]{2,1,0:T(8,128)(2,1)} %reshape.1108), calls=%async_computation.7 | async-start | bytes 1966080 | tf_op jit(solution)/shard_map/all_to_all | solution.py:338
  498.8 85.0 %all-to-all-start.5 = ((bf16[16,36,768]{2,1,0:T(8,128)(2,1)}), bf16[16,36,768]{2,1,0:T(8,128)(2,1)}, u32[]{:S(2)}, u32[]{:S(2)}) async-start(bf16[16,36,768]{2,1,0:T(8,128)(2,1)} %reshape.1098), calls=%async_computation.5 | async-start | bytes 1966080 | tf_op jit(solution)/shard_map/all_to_all | solution.py:257
  543.4 42.5 %collective-permute-start.2 = (bf16[384,768]{1,0:T(8,128)(2,1)}, bf16[384,768]{1,0:T(8,128)(2,1)}, u32[]{:S(2)}, u32[]{:S(2)}) collective-permute-start(bf16[384,768]{1,0:T(8,128)(2,1)} %fusion.361), channel_id=1, source_target_pairs={{16,0},{17,1},{18,2},{19,3},{20,4},{21,5},{22,6},{23,7},{24,8},{25... | collective-permute-start | bytes 1769480 | tf_op jit(solution)/shard_map/ppermute | solution.py:17
  593.9 66.8 %all-to-all-start.8 = ((bf16[16,36,768]{2,1,0:T(8,128)(2,1)}), bf16[16,36,768]{2,1,0:T(8,128)(2,1)}, u32[]{:S(2)}, u32[]{:S(2)}) async-start(bf16[16,36,768]{2,1,0:T(8,128)(2,1)} %reshape.1114), calls=%async_computation.8 | async-start | bytes 1966080 | tf_op jit(solution)/shard_map/all_to_all | solution.py:328
  681.9 30.8 %all-to-all-start.9 = ((bf16[16,36,768]{2,1,0:T(8,128)(2,1)}), bf16[16,36,768]{2,1,0:T(8,128)(2,1)}, u32[]{:S(2)}, u32[]{:S(2)}) async-start(bf16[16,36,768]{2,1,0:T(8,128)(2,1)} %reshape.1116), calls=%async_computation.9 | async-start | bytes 1966080 | tf_op jit(solution)/shard_map/all_to_all | solution.py:338
  748.2 40.2 %collective-permute-start.3 = (bf16[384,768]{1,0:T(8,128)(2,1)}, bf16[384,768]{1,0:T(8,128)(2,1)}, u32[]{:S(2)}, u32[]{:S(2)}) collective-permute-start(bf16[384,768]{1,0:T(8,128)(2,1)} %convert_element_type.595), channel_id=1, source_target_pairs={{16,0},{17,1},{18,2},{19,3},{20,4},{21,5},{22,6},{23,7},{24,8},{25... | collective-permute-start | bytes 1769480 | tf_op jit(solution)/shard_map/ppermute | solution.py:17
  793.3 65.3 %all-to-all-start.10 = ((bf16[16,36,768]{2,1,0:T(8,128)(2,1)}), bf16[16,36,768]{2,1,0:T(8,128)(2,1)}, u32[]{:S(2)}, u32[]{:S(2)}) async-start(bf16[16,36,768]{2,1,0:T(8,128)(2,1)} %reshape.1125), calls=%async_computation.10 | async-start | bytes 1966080 | tf_op jit(solution)/shard_map/all_to_all | solution.py:328
  879.8 31.6 %all-to-all-start.11 = ((bf16[16,36,768]{2,1,0:T(8,128)(2,1)}), bf16[16,36,768]{2,1,0:T(8,128)(2,1)}, u32[]{:S(2)}, u32[]{:S(2)}) async-start(bf16[16,36,768]{2,1,0:T(8,128)(2,1)} %reshape.1127), calls=%async_computation.11 | async-start | bytes 1966080 | tf_op jit(solution)/shard_map/all_to_all | solution.py:338
  969.5 36.1 %all-to-all-start.13 = ((bf16[16,48,784]{2,1,0:T(8,128)(2,1)}), bf16[16,48,784]{2,1,0:T(8,128)(2,1)}, u32[]{:S(2)}, u32[]{:S(2)}) async-start(bf16[16,48,784]{2,1,0:T(8,128)(2,1)} %bitcast.551), calls=%async_computation.13 | async-start | bytes 2752512 | tf_op jit(solution)/shard_map/all_to_all | solution.py:27
  1005.6 151.1 %all-to-all-start.12 = ((bf16[16,3,48,768]{3,2,1,0:T(8,128)(2,1)}), bf16[16,3,48,768]{3,2,1,0:T(8,128)(2,1)}, u32[]{:S(2)}, u32[]{:S(2)}) async-start(bf16[16,3,48,768]{3,2,1,0:T(8,128)(2,1)} %copy.309), calls=%async_computation.12 | async-start | bytes 7077888 | tf_op jit(solution)/shard_map/all_to_all | solution.py:27
  1060.4 90.1 %copy-start.44 = (f32[384,768]{1,0:T(8,128)S(1)}, f32[384,768]{1,0:T(8,128)}, u32[]{:S(2)}) copy-start(f32[384,768]{1,0:T(8,128)} %copy-done.43) | copy-start | bytes 3538948
  (257 other events, 1989.5 us)
Sparse Core Ops, SparseCore 0:
  10.7 73.9 all-gather.2
  87.5 54.6 all-gather.4
where the time goes:
time: 1180 us; the launch traced here: 1170 us
  local copies, waits for them, and re-layouts  394 us (33%)
  matrix products  292 us (25%)
  blocking collectives  162 us (14%)
  other arithmetic  139 us (12%)
  starting transfers between devices  88.7 us (8%)
  waiting for transfers between devices  73.4 us (6%)
  between operations  17.4 us (1%)
    dot_general x27, matrix products, product_lead(): lax.dot_general(left, right, (((0,), (0,)), ((), ())), preferred_element_...  96.6 us
    convert_element_type x3, local copies, waits for them, and re-layouts, diagonal_sums(): jnp.sum(padded.reshape(heads, rows, 2 * rows - 1), axis=1, dtype=jnp.floa...  90.4 us
    psum x1, blocking collectives, body(): grad_gain, grad_table = lax.psum((small_total[0], table_grad), 'expert')  83.1 us
    dot_general x27, matrix products, product(): return jnp.dot(left, right, preferred_element_type=jnp.float32)  77.2 us
    reshape x3, local copies, waits for them, and re-layouts, diagonal_sums(): padded = jnp.pad(grid, ((0, 0), (0, 0), (0, rows - 2))).reshape(heads, -1)  69.8 us
    dot_general x21, matrix products, product_last(): lax.dot_general(left, right, (((1,), (1,)), ((), ())), preferred_element_...  64.3 us
    unnamed x547, local copies, waits for them, and re-layouts  55.3 us
    all_gather x1, blocking collectives, body(): lax.all_gather(router, 'expert', axis=1, tiled=True)  50.8 us
  transfers between devices with their start and end apart: 19, of which 6 were waited for; matrix products, arithmetic and copies ran while one was open for 50% of the time, Pallas kernels for 0%

commit v1 on v0

v1 whole, which is shorter than its diff:
```python
import functools

import jax
import jax.numpy as jnp
from jax import lax
from jax.experimental import pallas as pl
from jax.experimental.pallas import tpu as pltpu
from jax.sharding import PartitionSpec as P

bucket_edges = (12, 16, 23, 32, 46, 64, 91)
norm_eps = 1e-06
gelu_c = 0.7978845608028654
gelu_cube = 0.044715
masked_score = -1e30
highest = lax.Precision.HIGHEST
f32 = jnp.float32
bf16 = jnp.bfloat16
vmem_bytes = 56 * 2**20
pieces = 3


def dot(left, right):
    return jnp.dot(left, right, preferred_element_type=f32)


def dot_lead(left, right):
    return lax.dot_general(left, right, (((0,), (0,)), ((), ())), preferred_element_type=f32)


def dot_last(left, right):
    return lax.dot_general(left, right, (((1,), (1,)), ((), ())), preferred_element_type=f32)


def gelu_pair(value):
    square = value * value
    inner = jnp.tanh(gelu_c * value * (1.0 + gelu_cube * square))
    half = 0.5 * (1.0 + inner)
    slope = half + 0.5 * value * (1.0 - inner * inner) * (
        gelu_c * (1.0 + 3.0 * gelu_cube * square)
    )
    return (value * half, slope)


def bucket_of(offset):
    distance = jnp.abs(offset)
    found = 16 * (offset > 0).astype(jnp.int32) + jnp.minimum(distance, 8)
    for edge in bucket_edges:
        found = found + (distance >= edge).astype(jnp.int32)
    return found


def norm_scale(values):
    return lax.rsqrt(jnp.mean(values * values, axis=-1, keepdims=True) + norm_eps)


def norm_backward(values, gain, grad_normed):
    scale = norm_scale(values)
    normal = values * scale
    inner = grad_normed * gain
    grad_values = scale * (inner - normal * jnp.mean(inner * normal, axis=-1, keepdims=True))
    return (grad_values, jnp.sum(grad_normed * normal, axis=0, keepdims=True))


def weight_copies(core, own, other, weights, sems):
    copies = []
    step = weights.shape[2] // len(own)
    for p in range(len(own)):
        columns = pl.ds(p * step, step)
        for which, (ref, at) in enumerate(((own[p], 2 * core), (other[p], 2 - 2 * core))):
            copies.append(
                pltpu.make_async_copy(
                    ref, weights.at[pl.ds(at, 2), :, columns], sems.at[2 * p + which]
                )
            )
    for copy in copies:
        copy.start()
    return copies


def head_masks():
    lane = lax.broadcasted_iota(jnp.int32, (1, 128), 1)
    low = (lane < 64).astype(f32)
    return (low, 1.0 - low)


def bias_of(line_ref, head, rows):
    line = jnp.broadcast_to(line_ref[pl.ds(head, 1), :], (rows, 2 * rows))
    return pltpu.roll(line, rows + 1, 1, stride=1, stride_axis=0)[:, :rows]


def one_hot_columns(place_col, slots):
    rows = place_col.shape[0]
    return (place_col == lax.broadcasted_iota(jnp.int32, (rows, slots), 1)).astype(f32).astype(bf16)


def one_hot_rows(place_row, slots):
    rows = place_row.shape[1]
    return (place_row == lax.broadcasted_iota(jnp.int32, (slots, rows), 0)).astype(f32).astype(bf16)


def forward_kernel(second, core_ref, *refs):
    own, refs = refs[:pieces], refs[pieces:]
    other, refs = refs[:pieces], refs[pieces:]
    if second:
        (before_ref, gate_before_ref, place_before_ref, back_ref, cot_ref), refs = refs[:5], refs[5:]
    else:
        (x_ref,), refs = refs[:1], refs[1:]
    (gain_ref, router_ref, line_ref, seg_col_ref, seg_row_ref, route_ref, place_ref), refs = (
        refs[:7],
        refs[7:],
    )
    (q_ref, k_ref, v_ref, o_ref, lse_ref, mid_ref, h2_ref, share_ref, gate_ref, send_ref), refs = (
        refs[:10],
        refs[10:],
    )
    if second:
        (x_out_ref, combined_ref, grad_send_ref), refs = refs[:3], refs[3:]
    weights, sems = refs
    copies = weight_copies(core_ref[0], own, other, weights, sems)
    slots = send_ref.shape[0]
    rows = q_ref.shape[0]
    if second:
        scatter = one_hot_columns(place_before_ref[...], slots)
        combined = dot(scatter, back_ref[...])
        combined_ref[...] = combined.astype(bf16)
        low = (before_ref[...] + gate_before_ref[...] * combined).astype(bf16)
        x_out_ref[...] = low
        wide = low.astype(f32)
    else:
        wide = x_ref[...].astype(f32)
    h1 = (wide * norm_scale(wide) * gain_ref[0:1, :]).astype(bf16)
    for copy in copies:
        copy.wait()
    q_ref[...] = dot(h1, weights[0]).astype(bf16)
    k_ref[...] = dot(h1, weights[1]).astype(bf16)
    v_ref[...] = dot(h1, weights[2]).astype(bf16)
    same = seg_col_ref[...] == seg_row_ref[...]
    masks = head_masks()
    lanes = lax.broadcasted_iota(jnp.int32, (rows, 128), 1)

    def pair(p, lse):
        columns = pl.ds(pl.multiple_of(p * 128, 128), 128)
        queries, keys, values = q_ref[:, columns], k_ref[:, columns], v_ref[:, columns]
        mixed = jnp.zeros((rows, 128), f32)
        for half in range(2):
            head = 2 * p + half
            low_mask = masks[half].astype(bf16)
            scores = dot_last(queries * low_mask, keys) * 0.125 + bias_of(line_ref, head, rows)
            scores = jnp.where(same, scores, masked_score)
            top = jnp.max(scores, axis=-1, keepdims=True)
            raised = jnp.exp(scores - top)
            total = jnp.sum(raised, axis=-1, keepdims=True)
            shares = (raised * (1.0 / total)).astype(bf16)
            mixed = mixed + dot(shares, values * low_mask)
            lse = jnp.where(lanes == head, top + jnp.log(total), lse)
        o_ref[:, columns] = mixed.astype(bf16)
        return lse

    lse_ref[...] = lax.fori_loop(0, line_ref.shape[0] // 2, pair, jnp.zeros((rows, 128), f32))
    middle = wide + dot(o_ref[...], weights[3])
    mid_ref[...] = middle
    h2 = (middle * norm_scale(middle) * gain_ref[1:2, :]).astype(bf16)
    h2_ref[...] = h2
    logits = dot(h2, router_ref[...])
    raised = jnp.exp(logits - jnp.max(logits, axis=-1, keepdims=True))
    shares = raised / jnp.sum(raised, axis=-1, keepdims=True)
    share_ref[...] = shares
    chosen = route_ref[...] == lax.broadcasted_iota(jnp.int32, shares.shape, 1)
    gate = jnp.sum(jnp.where(chosen, shares, 0.0), axis=-1, keepdims=True)
    gate_ref[...] = gate
    gather = one_hot_rows(place_ref[...], slots)
    send_ref[...] = dot(gather, h2).astype(bf16)
    if second:
        grad_out = (gate * cot_ref[...].astype(f32)).astype(bf16)
        grad_send_ref[...] = dot(gather, grad_out).astype(bf16)


def backward_kernel(second, core_ref, *refs):
    own, refs = refs[:pieces], refs[pieces:]
    other, refs = refs[:pieces], refs[pieces:]
    (
        x_ref, q_ref, k_ref, v_ref, o_ref, lse_ref, mid_ref, h2_ref, share_ref, gate_ref,
        dy_ref, dback_ref, out_ref, gain_ref, router_ref, line_ref, seg_col_ref, seg_row_ref,
        route_ref, place_ref,
    ), refs = refs[:20], refs[20:]
    if second:
        (gate_next_ref, place_next_ref), refs = refs[:2], refs[2:]
    (dx_ref, keep_ref, give_ref, router_grad_ref, gain_grad_ref, line_grad_ref), refs = (
        refs[:6],
        refs[6:],
    )
    if second:
        (y_ref, grad_send_ref), refs = refs[:2], refs[2:]
    weights, do_ref, dq_ref, dk_ref, dv_ref, dx1_ref, sems = refs
    core = core_ref[0]
    copies = weight_copies(core, own, other, weights, sems)
    rows = q_ref.shape[0]
    slots = dback_ref.shape[0]

    def put(matrix, value):
        value = value.astype(bf16)

        @pl.when(core == matrix // 2)
        def _():
            keep_ref[matrix % 2] = value

        @pl.when(core != matrix // 2)
        def _():
            give_ref[matrix % 2] = value

    dy = dy_ref[...].astype(f32)
    gate = gate_ref[...]
    middle = mid_ref[...]
    scatter = one_hot_columns(place_ref[...], slots)
    if second:
        combined = dot(scatter, out_ref[...])
        y_ref[...] = (middle + gate * combined).astype(bf16)
    else:
        combined = out_ref[...].astype(f32)
    grad_gate = jnp.sum(dy * combined, axis=-1, keepdims=True)
    shares = share_ref[...]
    chosen = route_ref[...] == lax.broadcasted_iota(jnp.int32, shares.shape, 1)
    grad_logits = (grad_gate * gate * (chosen.astype(f32) - shares)).astype(bf16)
    router_grad_ref[...] = dot_lead(h2_ref[...], grad_logits)
    grad_two = dot(scatter, dback_ref[...]) + dot_last(grad_logits, router_ref[...])
    grad_middle, gain_two = norm_backward(middle, gain_ref[1:2, :], grad_two)
    grad_middle = grad_middle + dy
    dx1_ref[...] = grad_middle
    low = grad_middle.astype(bf16)
    for copy in copies:
        copy.wait()
    put(3, dot_lead(o_ref[...], low))
    do_ref[...] = dot_last(low, weights[3]).astype(bf16)
    same = seg_col_ref[...] == seg_row_ref[...]
    masks = head_masks()
    lanes = lax.broadcasted_iota(jnp.int32, (rows, 128), 1)
    flip = (
        lax.broadcasted_iota(jnp.int32, (rows, rows), 0)
        + lax.broadcasted_iota(jnp.int32, (rows, rows), 1)
        == rows - 1
    )
    flip = flip.astype(f32).astype(bf16)

    def pair(p, carry):
        columns = pl.ds(pl.multiple_of(p * 128, 128), 128)
        queries, keys, values = q_ref[:, columns], k_ref[:, columns], v_ref[:, columns]
        grad_mixed = do_ref[:, columns]
        dq = jnp.zeros((rows, 128), f32)
        dk = jnp.zeros((rows, 128), f32)
        dv = jnp.zeros((rows, 128), f32)
        for half in range(2):
            head = 2 * p + half
            low_mask = masks[half].astype(bf16)
            own_queries = queries * low_mask
            own_mixed = grad_mixed * low_mask
            lse = jnp.sum(jnp.where(lanes == head, lse_ref[...], 0.0), axis=-1, keepdims=True)
            scores = dot_last(own_queries, keys) * 0.125 + bias_of(line_ref, head, rows)
            shares = jnp.exp(jnp.where(same, scores, masked_score) - lse)
            grad_shares = dot_last(own_mixed, values)
            mean = jnp.sum(shares * grad_shares, axis=-1, keepdims=True)
            grad_scores = (shares * (grad_shares - mean)).astype(bf16)
            dv = dv + dot_lead(shares.astype(bf16), own_mixed)
            dq = dq + dot(grad_scores, keys * low_mask)
            dk = dk + dot_lead(grad_scores, own_queries)
            flipped = dot(flip, grad_scores)
            wide = jnp.concatenate([flipped, jnp.zeros_like(flipped)], axis=1)
            turned = pltpu.roll(wide, 0, 1, stride=1, stride_axis=0)
            line_grad_ref[pl.ds(head, 1), :] = jnp.sum(turned, axis=0, keepdims=True)
        dq_ref[:, columns] = (dq * 0.125).astype(bf16)
        dk_ref[:, columns] = (dk * 0.125).astype(bf16)
        dv_ref[:, columns] = dv.astype(bf16)
        return carry

    lax.fori_loop(0, line_ref.shape[0] // 2, pair, 0)
    wide = x_ref[...].astype(f32)
    grad_one = (
        dot_last(dq_ref[...], weights[0])
        + dot_last(dk_ref[...], weights[1])
        + dot_last(dv_ref[...], weights[2])
    )
    grad_inputs, gain_one = norm_backward(wide, gain_ref[0:1, :], grad_one)
    grad_inputs = grad_inputs + dx1_ref[...]
    dx_ref[...] = grad_inputs
    gain_grad_ref[0:1, :] = gain_one
    gain_grad_ref[1:2, :] = gain_two
    if second:
        grad_out = (gate_next_ref[...] * grad_inputs.astype(bf16).astype(f32)).astype(bf16)
        gather = one_hot_rows(place_next_ref[...], slots)
        grad_send_ref[...] = dot(gather, grad_out).astype(bf16)
    h1 = (wide * norm_scale(wide) * gain_ref[0:1, :]).astype(bf16)
    put(0, dot_lead(h1, dq_ref[...]))
    put(1, dot_lead(h1, dk_ref[...]))
    put(2, dot_lead(h1, dv_ref[...]))


def expert_copies(mine, tiles, up_refs, down_refs, up, down, sems, start):
    width = up.shape[2]

    def copies(which):
        found = []
        for j in range(tiles):
            at = pl.ds(j * width, width)
            found.append(
                (
                    pltpu.make_async_copy(up_refs[which].at[:, at], up.at[j], sems.at[0, j]),
                    pltpu.make_async_copy(down_refs[which].at[at, :], down.at[j], sems.at[1, j]),
                )
            )
        return found

    if start:
        for which in range(2):

            @pl.when(mine == 1 - which)
            def _():
                for couple in copies(which):
                    for copy in couple:
                        copy.start()


def expert_wait(j, up_ref, down_ref, up, down, sems):
    width = up.shape[2]
    at = pl.ds(0, width)
    pltpu.make_async_copy(up_ref.at[:, at], up.at[j], sems.at[0, j]).wait()
    pltpu.make_async_copy(down_ref.at[at, :], down.at[j], sems.at[1, j]).wait()


def expert_forward_kernel(
    mine_ref, x_ref, up_own, up_other, down_own, down_other, act_ref, slope_ref, out_ref,
    up, down, total, sems,
):
    j = pl.program_id(0)
    tiles = up.shape[0]

    @pl.when(j == 0)
    def _():
        expert_copies(
            mine_ref[0], tiles, (up_own, up_other), (down_own, down_other), up, down, sems, True
        )
        total[...] = jnp.zeros_like(total)

    expert_wait(j, up_own, down_own, up, down, sems)
    active, slope = gelu_pair(dot(x_ref[...], up[j]))
    active = active.astype(bf16)
    act_ref[...] = active
    slope_ref[...] = slope.astype(bf16)
    total[...] += dot(active, down[j])

    @pl.when(j == tiles - 1)
    def _():
        out_ref[...] = total[...].astype(bf16)


def expert_backward_kernel(
    mine_ref, dout_ref, slope_ref, up_own, up_other, down_own, down_other, dpre_ref, dbuf_ref,
    up, down, total, sems,
):
    j = pl.program_id(0)
    tiles = up.shape[0]

    @pl.when(j == 0)
    def _():
        expert_copies(
            mine_ref[0], tiles, (up_own, up_other), (down_own, down_other), up, down, sems, True
        )
        total[...] = jnp.zeros_like(total)

    expert_wait(j, up_own, down_own, up, down, sems)
    grad_pre = (dot_last(dout_ref[...], down[j]) * slope_ref[...].astype(f32)).astype(bf16)
    dpre_ref[...] = grad_pre
    total[...] += dot_last(grad_pre, up[j])

    @pl.when(j == tiles - 1)
    def _():
        dbuf_ref[...] = total[...].astype(bf16)


def up_grad_kernel(buf_a, buf_b, dpre_a, dpre_b, grad_ref):
    grad_ref[...] = dot_lead(buf_a[...], dpre_a[...]) + dot_lead(buf_b[...], dpre_b[...])


def down_grad_kernel(dout_a, dout_b, act_a, act_b, grad_ref):
    grad_ref[...] = dot_lead(act_a[...], dout_a[...]) + dot_lead(act_b[...], dout_b[...])


def shape(dims, kind=bf16):
    return jax.ShapeDtypeStruct(dims, kind)


def params():
    return pltpu.CompilerParams(vmem_limit_bytes=vmem_bytes)


def cost(us):
    return pl.CostEstimate(flops=int(us * 1e9), bytes_accessed=0, transcendentals=0)


smem = pl.BlockSpec(memory_space=pltpu.SMEM)
vmem = pl.BlockSpec(memory_space=pltpu.VMEM)
anywhere = pl.BlockSpec(memory_space=pl.ANY)


def run_forward(second, core, own, other, inputs, slots, experts):
    rows, width = inputs[0].shape
    outs = [shape((rows, width))] * 4 + [
        shape((rows, 128), f32),
        shape((rows, width), f32),
        shape((rows, width)),
        shape((rows, experts), f32),
        shape((rows, 1), f32),
        shape((slots, width)),
    ]
    if second:
        outs += [shape((rows, width)), shape((rows, width)), shape((slots, width))]
    return pl.pallas_call(
        functools.partial(forward_kernel, second),
        out_shape=outs,
        in_specs=[smem] + [anywhere] * (2 * pieces) + [vmem] * len(inputs),
        out_specs=[vmem] * len(outs),
        scratch_shapes=[
            pltpu.VMEM((4, width, width), bf16),
            pltpu.SemaphoreType.DMA((2 * pieces,)),
        ],
        compiler_params=params(),
        cost_estimate=cost(18),
        name="attention_forward",
    )(core, *own, *other, *inputs)


def run_backward(second, core, own, other, inputs, slots, experts, heads):
    rows, width = inputs[0].shape
    outs = [
        shape((rows, width), f32),
        shape((2, width, width)),
        shape((2, width, width)),
        shape((width, experts), f32),
        shape((2, width), f32),
        shape((heads, 2 * rows), f32),
    ]
    if second:
        outs += [shape((rows, width)), shape((slots, width))]
    return pl.pallas_call(
        functools.partial(backward_kernel, second),
        out_shape=outs,
        in_specs=[smem] + [anywhere] * (2 * pieces) + [vmem] * len(inputs),
        out_specs=[vmem] * len(outs),
        scratch_shapes=[pltpu.VMEM((4, width, width), bf16)]
        + [pltpu.VMEM((rows, width), bf16)] * 4
        + [pltpu.VMEM((rows, width), f32), pltpu.SemaphoreType.DMA((2 * pieces,))],
        compiler_params=params(),
        cost_estimate=cost(30),
        name="attention_backward",
    )(core, *own, *other, *inputs)


def run_expert(kernel, mine, tall, middles, ups, downs, n_middle, us, name):
    slots, width = tall.shape
    inner = ups[0].shape[1]
    tiles = 6 if inner % 768 == 0 else 1
    tile = inner // tiles
    whole = pl.BlockSpec((slots, width), lambda j: (0, 0))
    part = pl.BlockSpec((slots, tile), lambda j: (0, j))
    return pl.pallas_call(
        kernel,
        grid=(tiles,),
        out_shape=[shape((slots, inner))] * n_middle + [shape((slots, width))],
        in_specs=[smem, whole] + [part] * len(middles) + [anywhere] * 4,
        out_specs=[part] * n_middle + [whole],
        scratch_shapes=[
            pltpu.VMEM((tiles, width, tile), bf16),
            pltpu.VMEM((tiles, tile, width), bf16),
            pltpu.VMEM((slots, width), f32),
            pltpu.SemaphoreType.DMA((2, tiles)),
        ],
        compiler_params=params(),
        cost_estimate=cost(us),
        name=name,
    )(mine, tall, *middles, *ups, *downs)


def run_up_grad(buf_a, buf_b, dpre_a, dpre_b):
    slots, width = buf_a.shape
    inner = dpre_a.shape[1]
    tile = inner // 6
    whole = pl.BlockSpec((slots, width), lambda j: (0, 0))
    part = pl.BlockSpec((slots, tile), lambda j: (0, j))
    return pl.pallas_call(
        up_grad_kernel,
        grid=(6,),
        out_shape=shape((width, inner), f32),
        in_specs=[whole, whole, part, part],
        out_specs=pl.BlockSpec((width, tile), lambda j: (0, j)),
        compiler_params=params(),
        cost_estimate=cost(10),
        name="up_gradient",
    )(buf_a, buf_b, dpre_a, dpre_b)


def run_down_grad(dout_a, dout_b, act_a, act_b):
    slots, width = dout_a.shape
    inner = act_a.shape[1]
    tile = inner // 6
    whole = pl.BlockSpec((slots, width), lambda j: (0, 0))
    part = pl.BlockSpec((slots, tile), lambda j: (0, j))
    return pl.pallas_call(
        down_grad_kernel,
        grid=(6,),
        out_shape=shape((inner, width), f32),
        in_specs=[whole, whole, part, part],
        out_specs=pl.BlockSpec((tile, width), lambda j: (j, 0)),
        compiler_params=params(),
        cost_estimate=cost(10),
        name="down_gradient",
    )(dout_a, dout_b, act_a, act_b)


def swap(block):
    return lax.ppermute(block, "section", [(0, 1), (1, 0)])


def moved(block, source):
    return lax.ppermute(block, "section", [(source, 1 - source)])


def across(block, bit, devices):
    return lax.ppermute(block, "expert", [(i, i ^ (1 << bit)) for i in range(devices)])


def bit_orders(bits):
    if bits == 4:
        return [(3, 2, 0, 1), (0, 1, 3, 2), (1, 3, 2, 0)]
    names = list(range(bits))
    return [tuple(names[(i + r * bits // pieces) % bits] for i in names) for r in range(pieces)]


def split_lanes(block):
    step = block.shape[-1] // pieces
    return [block[..., p * step : (p + 1) * step] for p in range(pieces)]


def gathered(shard, device, devices):
    bits = devices.bit_length() - 1
    count, rows = shard.shape[:2]
    found = [
        p.reshape((count,) + (1,) * bits + p.shape[1:]) for p in split_lanes(shard)
    ]
    orders = bit_orders(bits)
    for step in range(bits):
        for p in range(pieces):
            bit = orders[p][step]
            axis = bits - bit
            got = across(found[p], bit, devices)
            high = (device >> bit) & 1 == 1
            found[p] = jnp.where(
                high,
                jnp.concatenate([got, found[p]], axis),
                jnp.concatenate([found[p], got], axis),
            )
    return [p.reshape(count, devices * rows, -1) for p in found]


def halved(block, bit, bits, lead, device, devices):
    axis = lead + bits - 1 - bit
    low = lax.index_in_dim(block, 0, axis, keepdims=True)
    high = lax.index_in_dim(block, 1, axis, keepdims=True)
    up = (device >> bit) & 1 == 1
    got = across(jnp.where(up, low, high), bit, devices)
    return jnp.where(up, high, low).astype(f32) + got.astype(f32)


def scattered(total, device, devices):
    bits = devices.bit_length() - 1
    count = total.shape[0]
    found = [
        p.reshape((count,) + (2,) * bits + (total.shape[1] // devices, -1))
        for p in split_lanes(total)
    ]
    orders = [order[::-1] for order in bit_orders(bits)]
    for step in range(bits):
        for p in range(pieces):
            value = halved(found[p], orders[p][step], bits, 1, device, devices)
            found[p] = value if step == bits - 1 else value.astype(bf16)
    return jnp.concatenate([p.reshape(count, total.shape[1] // devices, -1) for p in found], 2)


def body(
    block_input,
    cotangent,
    lengths,
    routes,
    norm_gain,
    attention_in,
    attention_out,
    position_bias,
    router,
    expert_up,
    expert_down,
):
    _, rows, width = block_input.shape
    section = lax.axis_index("section")
    device = lax.axis_index("expert")
    devices = lax.axis_size("expert")
    bits = devices.bit_length() - 1
    first = section == 0
    core = section.astype(jnp.int32).reshape(1)
    mine = [(section == which).astype(jnp.int32).reshape(1) for which in range(2)]
    experts = router.shape[2]
    shard_rows = router.shape[1]
    buckets, heads = position_bias.shape[1:]
    capacity = max(2, 3 * rows // (2 * experts))
    capacity = -(-capacity // 8) * 8
    slots = experts * capacity

    def both(own, other):
        return (jnp.where(first, own, other), jnp.where(first, other, own))

    def own_micro(block):
        return jnp.where(first, block[0], block[1])

    def other_micro(block):
        return jnp.where(first, block[1], block[0])

    queries_keys = attention_in[0, :2]
    values_out = jnp.stack([attention_in[0, 2], attention_out[0]])
    given = swap(jnp.where(first, values_out, queries_keys))
    shards = (
        jnp.where(first, queries_keys, given),
        jnp.where(first, given, values_out),
    )
    small_parts = (
        norm_gain[0].reshape(-1),
        position_bias[0].reshape(-1),
        router[0].astype(f32).reshape(-1),
        other_micro(routes[0])[:, 0].astype(f32),
    )
    small = jnp.concatenate(small_parts).reshape(-1, 128)
    small_given = swap(small).reshape(-1)
    split_at, at = [], 0
    for part in small_parts[:-1]:
        at += part.shape[0]
        split_at.append(at)
    gain_other, table_other, router_other, route_other = jnp.split(small_given, split_at)
    gains = both(norm_gain[0], gain_other.reshape(2, width))
    tables = both(position_bias[0], table_other.reshape(buckets, heads))
    route_pair = both(own_micro(routes[0])[:, 0], route_other.astype(jnp.int32))
    router_pair = both(router[0], router_other.reshape(shard_rows, experts).astype(bf16))

    first_weights = gathered(shards[0], device, devices)
    first_other = [swap(p) for p in first_weights]
    up_other = swap(expert_up[0, 0])
    down_other = swap(expert_down[0, 0])

    routers = jnp.concatenate(router_pair, axis=1)
    routers = jnp.pad(routers, ((0, 0), (0, -routers.shape[1] % 128)))
    routers = routers.reshape((1,) * bits + routers.shape)
    for bit in range(bits):
        axis = bits - 1 - bit
        got = across(routers, bit, devices)
        routers = jnp.where(
            (device >> bit) & 1 == 1,
            jnp.concatenate([got, routers], axis),
            jnp.concatenate([routers, got], axis),
        )
    routers = routers.reshape(width, -1)
    router_all = (routers[:, :experts], routers[:, experts : 2 * experts])

    late, first_weights = lax.optimization_barrier((shards[1], first_weights))
    second_weights = gathered(late, device, devices)
    second_other = [swap(p) for p in second_weights]
    owns, others = (first_weights, second_weights), (first_other, second_other)

    positions = jnp.arange(rows, dtype=jnp.int32)
    bounds = jnp.cumsum(own_micro(lengths)[0])
    segment = jnp.sum((positions[:, None] >= bounds[None, :]).astype(jnp.int32), axis=1)
    seg_col, seg_row = segment[:, None], segment[None, :]
    offsets = jnp.arange(2 * rows, dtype=jnp.int32) - (rows - 1)
    bucket_hot = (
        bucket_of(offsets)[:, None] == jnp.arange(buckets, dtype=jnp.int32)[None, :]
    ).astype(f32)
    lines = [
        lax.dot_general(table, bucket_hot, (((0,), (1,)), ((), ())), precision=highest)
        for table in tables
    ]
    before = (positions[:, None] > positions[None, :]).astype(bf16)
    places = []
    for route in route_pair:
        chosen = route[:, None] == jnp.arange(experts, dtype=jnp.int32)[None, :]
        earlier = dot(before, chosen.astype(bf16))
        slot = jnp.sum(jnp.where(chosen, earlier, 0.0), axis=1).astype(jnp.int32)
        places.append(route * capacity + slot)
    route_cols = [route[:, None] for route in route_pair]
    place_cols = [place[:, None] for place in places]
    place_rows = [place[None, :] for place in places]
    ups, downs = (expert_up[0, 0], up_other), (expert_down[0, 0], down_other)

    def exchanged(block):
        return lax.all_to_all(block, "expert", split_axis=0, concat_axis=0, tiled=True)

    def expert_forward(which, arrived):
        return run_expert(
            expert_forward_kernel, mine[which], arrived, (), ups, downs, 2, 11, "expert_forward"
        )

    def expert_backward(which, arrived, slope):
        return run_expert(
            expert_backward_kernel, mine[which], arrived, (slope,), ups, downs, 1, 11,
            "expert_backward",
        )

    def shared_inputs(which):
        return (
            gains[which], router_all[which], lines[which], seg_col, seg_row, route_cols[which],
        )

    inputs = own_micro(block_input)
    cot = own_micro(cotangent)
    q0, k0, v0, o0, lse0, mid0, h20, share0, gate0, send0 = run_forward(
        False, core, owns[0], others[0], (inputs, *shared_inputs(0), place_rows[0]), slots, experts
    )
    buf0 = exchanged(send0)
    act0, slope0, result0 = expert_forward(0, buf0)
    back0 = exchanged(result0)
    q1, k1, v1, o1, lse1, mid1, h21, share1, gate1, send1, between, combined0, grad_send1 = (
        run_forward(
            True, core, owns[1], others[1],
            (mid0, gate0, place_cols[0], back0, cot, *shared_inputs(1), place_rows[1]),
            slots, experts,
        )
    )
    buf1 = exchanged(send1)
    grad_send1, _ = lax.optimization_barrier((grad_send1, buf1))
    dout1 = exchanged(grad_send1)
    act1, slope1, result1 = expert_forward(1, buf1)
    back1 = exchanged(result1)
    dpre1, dbuf1 = expert_backward(1, dout1, slope1)
    dback1 = exchanged(dbuf1)
    dx1, keep1, give1, router_grad1, gain_grad1, line_grad1, last, grad_send0 = run_backward(
        True, core, owns[1], others[1],
        (between, q1, k1, v1, o1, lse1, mid1, h21, share1, gate1, cot, dback1, back1,
         *shared_inputs(1), place_cols[1], gate0, place_rows[0]),
        slots, experts, heads,
    )
    dout0 = exchanged(grad_send0)
    dpre0, dbuf0 = expert_backward(0, dout0, slope0)
    dback0 = exchanged(dbuf0)
    dx0, keep0, give0, router_grad0, gain_grad0, line_grad0 = run_backward(
        False, core, owns[0], others[0],
        (inputs, q0, k0, v0, o0, lse0, mid0, h20, share0, gate0, dx1.astype(bf16), dback0,
         combined0, *shared_inputs(0), place_cols[0]),
        slots, experts, heads,
    )

    from_first = [moved(block, 0) for block in (buf1, act1, dout1, dpre1)]
    from_second = [moved(block, 1) for block in (buf0, act0, dout0, dpre0)]

    def up_of(bufs, dpres):
        return run_up_grad(*bufs, *dpres)

    def down_of(douts, acts):
        return run_down_grad(*douts, *acts)

    first_sets = ((buf0, from_second[0]), (dpre0, from_second[3]))
    second_sets = ((buf1, from_first[0]), (dpre1, from_first[3]))
    grad_up = lax.cond(
        first, lambda a, b: up_of(*a), lambda a, b: up_of(*b), first_sets, second_sets
    )
    first_sets = ((dout0, from_second[2]), (act0, from_second[1]))
    second_sets = ((dout1, from_first[2]), (act1, from_first[1]))
    grad_down = lax.cond(
        first, lambda a, b: down_of(*a), lambda a, b: down_of(*b), first_sets, second_sets
    )

    def reduced(keep, give):
        total = (keep.astype(f32) + swap(give).astype(f32)).astype(bf16)
        return scattered(total, device, devices)

    shared1 = reduced(keep1, give1)
    shared0 = reduced(keep0, give0)
    shared_other = swap(jnp.where(first, shared1, shared0))
    queries_keys = jnp.where(first, shared0, shared_other)
    values_out = jnp.where(first, shared_other, shared1)

    router_mine = jnp.where(first, router_grad0, router_grad1)
    router_given = jnp.where(first, router_grad1, router_grad0)
    router_sum = (router_mine + swap(router_given)).reshape((2,) * bits + (shard_rows, experts))
    little = [
        jnp.concatenate([gain, line], axis=0)
        for gain, line in ((gain_grad0, line_grad0), (gain_grad1, line_grad1))
    ]
    little_sum = jnp.where(first, little[0], little[1]) + swap(
        jnp.where(first, little[1], little[0])
    )
    for bit in range(bits):
        router_sum = halved(router_sum, bit, bits, 0, device, devices)
        little_sum = little_sum + across(little_sum, bit, devices)
    grad_table = jnp.dot(little_sum[2:], bucket_hot, precision=highest).T

    out_other = swap(jnp.where(first, last, between))
    layer_out = jnp.stack(
        [jnp.where(first, between, out_other), jnp.where(first, out_other, last)]
    )
    grad_other = swap(jnp.where(first, dx1, dx0))
    input_grad = jnp.stack([jnp.where(first, dx0, grad_other), jnp.where(first, grad_other, dx1)])
    return (
        layer_out[None],
        input_grad[None],
        little_sum[:2][None],
        jnp.concatenate([queries_keys, values_out[:1]], axis=0)[None],
        values_out[1][None],
        grad_table[None],
        router_sum.reshape(1, shard_rows, experts),
        grad_up[None, None],
        grad_down[None, None],
    )


def solution(mesh):
    in_specs = (
        P(None, "expert", None),
        P(None, "expert", None),
        P(None, "expert", None),
        P("section", None, "expert", None),
        P("section", None, None),
        P("section", None, "expert", None),
        P("section", "expert", None),
        P("section", None, None),
        P("section", "expert", None),
        P("section", "expert", None, None),
        P("section", "expert", None, None),
    )
    out_specs = (
        P("section", None, "expert", None),
        P("section", None, "expert", None),
        P("section", None, None),
        P("section", None, "expert", None),
        P("section", "expert", None),
        P("section", None, None),
        P("section", "expert", None),
        P("section", "expert", None, None),
        P("section", "expert", None, None),
    )
    return jax.shard_map(body, mesh=mesh, in_specs=in_specs, out_specs=out_specs, check_vma=False)
```

time: 1180 us -> 589 us (0.50)
  local copies, waits for them, and re-layouts: 394 us -> 15.6 us
  matrix products: 292 us -> 2.83 us
  Pallas kernels: 0 us -> 182 us
  blocking collectives: 162 us -> 31.3 us
  other arithmetic: 139 us -> 23.2 us
  waiting for transfers between devices: 73.4 us -> 189 us
  starting transfers between devices: 88.7 us -> 131 us
  between operations: 17.4 us -> 2.84 us
    dot_general x98 -> x5, matrix products: 292 us -> 2.83 us  [the longest x2 2.11 us: body(): lax.dot_general(table, bucket_hot, (((0,), (1,)), ((), ())), precision=hi...]
    pallas_call x0 -> x10, Pallas kernels: none -> 182 us  [the longest x2 67.3 us: run_backward(): pl.pallas_call(functools.partial(backward_kernel, second), out_shape=outs...]
    reshape x35 -> x3, local copies, waits for them, and re-layouts: 175 us -> 0.13 us  [the longest x1 0.1 us: body(): tables = both(position_bias[0], table_other.reshape(buckets, heads))]
    ppermute x4 -> x85, waiting for transfers between devices: 0.01 us -> 150 us  [the longest x60 145 us: across(): lax.ppermute(block, 'expert', [(i, i ^ 1 << bit) for i in range(devices)])]
    convert_element_type x15 -> x3, local copies, waits for them, and re-layouts: 103 us -> 0.93 us  [the longest x2 0.84 us: body(): router[0].astype(f32).reshape(-1)]
    ppermute x4 -> x85, starting transfers between devices: 7.03 us -> 92.9 us  [the longest x60 70.4 us: across(): lax.ppermute(block, 'expert', [(i, i ^ 1 << bit) for i in range(devices)])]
    psum x1 -> x0, blocking collectives: 83.1 us -> none  [body(): grad_gain, grad_table = lax.psum((small_total[0], table_grad), 'expert')]
    all_gather x1 -> x0, blocking collectives: 50.8 us -> none  [body(): lax.all_gather(router, 'expert', axis=1, tiled=True)]
  transfers between devices with their start and end apart: 19 -> 92, of which waited for: 6 -> 38; matrix products, arithmetic and copies ran while one was open for 50% -> 6% of each run, Pallas kernels for 0% -> 28%
where the time goes in v1:
time: 589 us; the launch traced here: 579 us
  waiting for transfers between devices  189 us (32%)
  Pallas kernels  182 us (31%)
  starting transfers between devices  131 us (22%)
  blocking collectives  31.3 us (5%)
  other arithmetic  23.2 us (4%)
  local copies, waits for them, and re-layouts  15.6 us (3%)
    ppermute x60, waiting for transfers between devices, across(): lax.ppermute(block, 'expert', [(i, i ^ 1 << bit) for i in range(devices)])  145 us
    ppermute x60, starting transfers between devices, across(): lax.ppermute(block, 'expert', [(i, i ^ 1 << bit) for i in range(devices)])  70.4 us
    pallas_call x2, Pallas kernels, run_backward(): pl.pallas_call(functools.partial(backward_kernel, second), out_shape=outs...  67.3 us
    pallas_call x4, Pallas kernels, run_expert(): pl.pallas_call(kernel, grid=(tiles,), out_shape=[shape((slots, inner))] *...  55 us
    all_to_all x7, waiting for transfers between devices, exchanged(): lax.all_to_all(block, 'expert', split_axis=0, concat_axis=0, tiled=True)  39.3 us
    all_to_all x7, starting transfers between devices, exchanged(): lax.all_to_all(block, 'expert', split_axis=0, concat_axis=0, tiled=True)  38.2 us
    pallas_call x2, Pallas kernels, run_forward(): pl.pallas_call(functools.partial(forward_kernel, second), out_shape=outs,...  34.8 us
    all_to_all x1, blocking collectives, exchanged(): lax.all_to_all(block, 'expert', split_axis=0, concat_axis=0, tiled=True)  31.3 us
  transfers between devices with their start and end apart: 92, of which 38 were waited for; matrix products, arithmetic and copies ran while one was open for 6% of the time, Pallas kernels for 28%

profile of v1, /device:TPU:0, one launch (start us, length us, event | category | flops | bytes accessed | tf_op | source)
XLA Modules:
  0.0 578.7 jit_solution(1691237200870516649)
XLA Ops:
  34.5 5.7 collective-permute-done.10
  62.6 16.6 %attention_forward.2 = (bf16[384,768]{1,0:T(8,128)(2,1)}, bf16[384,768]{1,0:T(8,128)(2,1)}, bf16[384,768]{1,0:T(8,128)(2,1)}, bf16[384,768]{1,0:T(8,128)(2,1)}, ...) custom-call(s32[1]{0:T(128)} %bitcast.4.core_ref, ...), custom_call_target="tpu_custom_call" | custom-call | flops 17999998976 | tf_op jit(solution)/shard_map/attention_forward/pallas_call | solution.py:415
  89.5 20.9 %collective-permute-done.13 = bf16[2,1,1,1,1,48,256]{6,5,0,1,4,3,2:T(8,128)(2,1)S(1)} collective-permute-done((bf16[2,1,1,1,1,48,256]{6,5,0,1,4,3,2:T(8,128)(2,1)S(1)}, bf16[2,1,1,1,1,48,256]{6,5,0,1,4,3,2:T(8,128)(2,1)S(1)}, u32[]{:S(2)}, u32[]{:S(2)}) %collective-permute-start.13) | collective-permute-done | bytes 49184 | tf_op jit(solution)/shard_map/ppermute | solution.py:526
  121.0 14.9 %expert_forward.2 = (bf16[640,3072]{1,0:T(8,128)(2,1)}, bf16[640,3072]{1,0:T(8,128)(2,1)}, bf16[640,768]{1,0:T(8,128)(2,1)}) custom-call(s32[1]{0:T(128)} %bitcast.92.mine_ref, bf16[640,768]{1,0:T(8,128)(2,1)} %bitcast.94.x_ref, bf16[768,3072]{1,0:T(8,128)(2,1)} %bitcast.326, bf16[768,3072]{1,0:T(8,128)(2,1)} %collective-permute-done.36.up_other, ...), custom_call_target="tpu_custom_call" | custom-call | flops 11000000512 | tf_op jit(solution)/shard_map/expert_forward/pallas_call | solution.py:463
  135.9 6.8 %all-to-all-start.1 = ((bf16[16,40,768]{2,1,0:T(8,128)(2,1)}), bf16[16,40,768]{2,1,0:T(8,128)(2,1)S(1)}, u32[]{:S(2)}, u32[]{:S(2)}) async-start(bf16[16,40,768]{2,1,0:T(8,128)(2,1)} %bitcast.279), calls=%async_computation.1 | async-start | bytes 1966080 | tf_op jit(solution)/shard_map/all_to_all | solution.py:697
  148.0 8.0 %collective-permute-done.16 = bf16[2,2,2,1,2,48,256]{6,5,0,1,2,4,3:T(8,128)(2,1)S(1)} collective-permute-done((bf16[2,2,2,1,2,48,256]{6,5,0,1,2,4,3:T(8,128)(2,1)S(1)}, bf16[2,2,2,1,2,48,256]{6,5,0,1,2,4,3:T(8,128)(2,1)S(1)}, u32[]{:S(2)}, u32[]{:S(2)}) %collective-permute-start.16) | collective-permute-done | bytes 393248 | tf_op jit(solution)/shard_map/ppermute | solution.py:526
  156.3 7.1 %collective-permute-done.20 = bf16[2,2,1,2,2,48,256]{6,5,0,4,3,2,1:T(8,128)(2,1)S(1)} collective-permute-done((bf16[2,2,1,2,2,48,256]{6,5,0,4,3,2,1:T(8,128)(2,1)S(1)}, bf16[2,2,1,2,2,48,256]{6,5,0,4,3,2,1:T(8,128)(2,1)S(1)}, u32[]{:S(2)}, u32[]{:S(2)}) %collective-permute-start.20) | collective-permute-done | bytes 393248 | tf_op jit(solution)/shard_map/ppermute | solution.py:526
  170.3 18.3 %attention_forward.3 = (bf16[384,768]{1,0:T(8,128)(2,1)}, bf16[384,768]{1,0:T(8,128)(2,1)}, bf16[384,768]{1,0:T(8,128)(2,1)}, bf16[384,768]{1,0:T(8,128)(2,1)}, ...) custom-call(s32[1]{0:T(128)} %bitcast.4.core_ref, ...), custom_call_target="tpu_custom_call" | custom-call | flops 17999998976 | tf_op jit(solution)/shard_map/attention_forward/pallas_call | solution.py:415
  188.5 31.3 %all_to_all.88 = bf16[16,40,768]{2,1,0:T(8,128)(2,1)} all-to-all(bf16[16,40,768]{2,1,0:T(8,128)(2,1)} %bitcast.286), channel_id=1, replica_groups=mesh['section'=2,'expert'=16] {'expert'}, dimensions={0} | all-to-all | bytes 1966080 | tf_op jit(solution)/shard_map/all_to_all | solution.py:697
  223.6 14.9 %expert_forward.3 = (bf16[640,3072]{1,0:T(8,128)(2,1)}, bf16[640,3072]{1,0:T(8,128)(2,1)}, bf16[640,768]{1,0:T(8,128)(2,1)}) custom-call(s32[1]{0:T(128)} %bitcast.100.mine_ref, bf16[640,768]{1,0:T(8,128)(2,1)} %bitcast.102.x_ref, bf16[768,3072]{1,0:T(8,128)(2,1)} %bitcast.327, bf16[768,3072]{1,0:T(8,128)(2,1)} %collective-permute-done.36.up_other, ...), custom_call_target="tpu_custom_call" | custom-call | flops 11000000512 | tf_op jit(solution)/shard_map/expert_forward/pallas_call | solution.py:463
  238.5 7.5 %all-to-all-done.3 = bf16[16,40,768]{2,1,0:T(8,128)(2,1)S(1)} async-done(((bf16[16,40,768]{2,1,0:T(8,128)(2,1)}), bf16[16,40,768]{2,1,0:T(8,128)(2,1)S(1)}, u32[]{:S(2)}, u32[]{:S(2)}) %all-to-all-start.3) | async-done | bytes 983072 | tf_op jit(solution)/shard_map/all_to_all | solution.py:697
  251.7 12.3 %expert_backward.2 = (bf16[640,3072]{1,0:T(8,128)(2,1)}, bf16[640,768]{1,0:T(8,128)(2,1)}) custom-call(s32[1]{0:T(128)} %bitcast.100.mine_ref, bf16[640,768]{1,0:T(8,128)(2,1)S(1)} %bitcast.273, bf16[640,3072]{1,0:T(8,128)(2,1)} %get-tuple-element.138.slope_ref, bf16[768,3072]{1,0:T(8,128)(2,1)} %bitcast.328, ...), custom_call_target="tpu_custom_call" | custom-call | flops 11000000512 | tf_op jit(solution)/shard_map/expert_backward/pallas_call | solution.py:463
  264.1 9.5 %all-to-all-done.5 = bf16[16,40,768]{2,1,0:T(8,128)(2,1)S(1)} async-done(((bf16[16,40,768]{2,1,0:T(8,128)(2,1)}), bf16[16,40,768]{2,1,0:T(8,128)(2,1)S(1)}, u32[]{:S(2)}, u32[]{:S(2)}) %all-to-all-start.5) | async-done | bytes 983072 | tf_op jit(solution)/shard_map/all_to_all | solution.py:697
  273.5 5.8 %all-to-all-start.4 = ((bf16[16,40,768]{2,1,0:T(8,128)(2,1)}), bf16[16,40,768]{2,1,0:T(8,128)(2,1)S(1)}, u32[]{:S(2)}, u32[]{:S(2)}) async-start(bf16[16,40,768]{2,1,0:T(8,128)(2,1)} %bitcast.284), calls=%async_computation.4 | async-start | bytes 1966080 | tf_op jit(solution)/shard_map/all_to_all | solution.py:697
  286.2 14.9 %all-to-all-done.4 = bf16[16,40,768]{2,1,0:T(8,128)(2,1)S(1)} async-done(((bf16[16,40,768]{2,1,0:T(8,128)(2,1)}), bf16[16,40,768]{2,1,0:T(8,128)(2,1)S(1)}, u32[]{:S(2)}, u32[]{:S(2)}) %all-to-all-start.4) | async-done | bytes 983072 | tf_op jit(solution)/shard_map/all_to_all | solution.py:697
  302.0 34.6 %attention_backward.2 = (f32[384,768]{1,0:T(8,128)}, bf16[2,768,768]{2,1,0:T(8,128)(2,1)}, bf16[2,768,768]{2,1,0:T(8,128)(2,1)}, f32[768,16]{1,0:T(8,128)}, f32[...) custom-call(s32[1]{0:T(128)} %bitcast.4.core_ref, ...), custom_call_target="tpu_custom_call" | custom-call | flops 30000001024 | tf_op jit(solution)/shard_map/attention_backward/pallas_call | solution.py:442
  336.7 6.0 %all-to-all-start.6 = ((bf16[16,40,768]{2,1,0:T(8,128)(2,1)}), bf16[16,40,768]{2,1,0:T(8,128)(2,1)}, u32[]{:S(2)}, u32[]{:S(2)}) async-start(bf16[16,40,768]{2,1,0:T(8,128)(2,1)} %bitcast.280), calls=%async_computation.6 | async-start | bytes 1966080 | tf_op jit(solution)/shard_map/all_to_all | solution.py:697
  349.5 6.3 %collective-permute-start.77 = (bf16[640,768]{1,0:T(8,128)(2,1)}, bf16[640,768]{1,0:T(8,128)(2,1)}, u32[]{:S(2)}, u32[]{:S(2)}) collective-permute-start(bf16[640,768]{1,0:T(8,128)(2,1)} %bitcast.102.x_ref), channel_id=1, source_target_pairs={{0,16},{1,17},{2,18},{3,19},{4,20},{5,21},{6,22},{7,23},{8,24},{9,... | collective-permute-start | bytes 2949128 | tf_op jit(solution)/shard_map/ppermute | solution.py:522
  357.0 7.4 %all-to-all-done.6 = bf16[16,40,768]{2,1,0:T(8,128)(2,1)} async-done(((bf16[16,40,768]{2,1,0:T(8,128)(2,1)}), bf16[16,40,768]{2,1,0:T(8,128)(2,1)}, u32[]{:S(2)}, u32[]{:S(2)}) %all-to-all-start.6) | async-done | bytes 983072 | tf_op jit(solution)/shard_map/all_to_all | solution.py:697
  364.5 12.8 %expert_backward.3 = (bf16[640,3072]{1,0:T(8,128)(2,1)}, bf16[640,768]{1,0:T(8,128)(2,1)}) custom-call(s32[1]{0:T(128)} %bitcast.92.mine_ref, bf16[640,768]{1,0:T(8,128)(2,1)} %bitcast.113.dout_ref, bf16[640,3072]{1,0:T(8,128)(2,1)} %get-tuple-element.151.slope_ref, bf16[768,3072]{1,0:T(8,128)(2,1)} %bitcast.329, ...), custom_call_target="tpu_custom_call" | custom-call | flops 11000000512 | tf_op jit(solution)/shard_map/expert_backward/pallas_call | solution.py:463
  377.3 5.9 %all-to-all-start.7 = ((bf16[16,40,768]{2,1,0:T(8,128)(2,1)}), bf16[16,40,768]{2,1,0:T(8,128)(2,1)}, u32[]{:S(2)}, u32[]{:S(2)}) async-start(bf16[16,40,768]{2,1,0:T(8,128)(2,1)} %bitcast.276), calls=%async_computation.7 | async-start | bytes 1966080 | tf_op jit(solution)/shard_map/all_to_all | solution.py:697
  390.7 14.7 %collective-permute-done.67 = bf16[2,2,2,2,1,48,256]{6,5,0,4,3,2,1:T(8,128)(2,1)S(1)} collective-permute-done((bf16[2,2,2,2,1,48,256]{6,5,0,4,3,2,1:T(8,128)(2,1)S(1)}, bf16[2,2,2,2,1,48,256]{6,5,0,4,3,2,1:T(8,128)(2,1)S(1)}, u32[]{:S(2)}, u32[]{:S(2)}) %collective-permute-start.67) | collective-permute-done | bytes 393248 | tf_op jit(solution)/shard_map/ppermute | solution.py:526
  409.9 8.8 %collective-permute-done.59 = bf16[2,2,2,1,2,48,256]{6,5,0,4,3,2,1:T(8,128)(2,1)S(1)} collective-permute-done((bf16[2,2,2,1,2,48,256]{6,5,0,4,3,2,1:T(8,128)(2,1)S(1)}, bf16[2,2,2,1,2,48,256]{6,5,0,4,3,2,1:T(8,128)(2,1)S(1)}, u32[]{:S(2)}, u32[]{:S(2)}) %collective-permute-start.59) | collective-permute-done | bytes 393248 | tf_op jit(solution)/shard_map/ppermute | solution.py:526
  424.9 12.7 %conditional.3 = (f32[1,1,3072,768]{3,2,1,0:T(8,128)}) conditional(s32[]{:T(128)} %convert_element_type.439, (bf16[640,768]{1,0:T(8,128)(2,1)S(1)}, bf16[640,768]{1,0:T(8,128)(2,1)S(1)}, bf16[640,3072]{1,0:T(8,128)(2,1)}, bf16[640,3072]{1,0:T(8,128)(2,1)}) %tuple.92, (bf16[640,768]{1,0:T(8,128)(2,1)}, bf16[640,768]{1,0:T(8,128)(2,1)}, ...), branch_computations={%region_6.7_spmd, %region_7.8_spmd} | conditional | flops 10000000000 | bytes 8 | solution.py:769
  424.9 12.7 %down_gradient.3 = f32[3072,768]{1,0:T(8,128)} custom-call(bf16[640,768]{1,0:T(8,128)(2,1)} %get-tuple-element.52.dout_a, bf16[640,768]{1,0:T(8,128)(2,1)} %get-tuple-element.53.dout_b, bf16[640,3072]{1,0:T(8,128)(2,1)} %get-tuple-element.54.act_a, bf16[640,3072]{1,0:T(8,128)(2,1)} %get-tuple-element.55.act_b), custom_call_target="tpu_custom_call" | custom-call | flops 10000000000 | tf_op jit(solution)/shard_map/cond/branch_1_fun/down_gradient/pallas_call | solution.py:505
  448.4 32.7 %attention_backward.3 = (f32[384,768]{1,0:T(8,128)}, bf16[2,768,768]{2,1,0:T(8,128)(2,1)}, bf16[2,768,768]{2,1,0:T(8,128)(2,1)}, f32[768,16]{1,0:T(8,128)}, f32[2,768]{1,0:T(2,128)}, /*index=5*/f32[12,768]{1,0:T(8,128)}) custom-call(s32[1]{0:T(128)} %bitcast.4.core_ref, bf16[2,768,256]{2,1,0:T(8,128)(2,1)} %bitcast.289, bf16[2,768,256]{2,1,0:T(8,128)(2,1)} %bitcast.292, ...), custom_call_target="tpu_custom_call" | custom-call | flops 30000001024 | tf_op jit(solution)/shard_map/attention_backward/pallas_call | solution.py:442
  514.7 9.6 %collective-permute-done.54 = bf16[2,2,2,2,1,48,256]{6,5,0,4,3,2,1:T(8,128)(2,1)S(1)} collective-permute-done((bf16[2,2,2,2,1,48,256]{6,5,0,4,3,2,1:T(8,128)(2,1)S(1)}, bf16[2,2,2,2,1,48,256]{6,5,0,4,3,2,1:T(8,128)(2,1)S(1)}, u32[]{:S(2)}, u32[]{:S(2)}) %collective-permute-start.54) | collective-permute-done | bytes 393248 | tf_op jit(solution)/shard_map/ppermute | solution.py:526
  526.2 8.4 %collective-permute-done.46 = bf16[2,2,2,1,2,48,256]{6,5,0,4,3,2,1:T(8,128)(2,1)S(1)} collective-permute-done((bf16[2,2,2,1,2,48,256]{6,5,0,4,3,2,1:T(8,128)(2,1)S(1)}, bf16[2,2,2,1,2,48,256]{6,5,0,4,3,2,1:T(8,128)(2,1)S(1)}, u32[]{:S(2)}, u32[]{:S(2)}) %collective-permute-start.46) | collective-permute-done | bytes 393248 | tf_op jit(solution)/shard_map/ppermute | solution.py:526
  535.7 7.7 %collective-permute-done.51 = bf16[2,1,1,2,2,48,256]{6,5,0,4,3,2,1:T(8,128)(2,1)S(1)} collective-permute-done((bf16[2,1,1,2,2,48,256]{6,5,0,4,3,2,1:T(8,128)(2,1)S(1)}, bf16[2,1,1,2,2,48,256]{6,5,0,4,3,2,1:T(8,128)(2,1)S(1)}, u32[]{:S(2)}, u32[]{:S(2)}) %collective-permute-start.51) | collective-permute-done | bytes 196640 | tf_op jit(solution)/shard_map/ppermute | solution.py:526
  545.1 5.8 collective-permute-done.56
  564.1 12.6 %conditional.2 = (f32[1,1,768,3072]{3,2,1,0:T(8,128)}) conditional(s32[]{:T(128)} %convert_element_type.439, (bf16[640,768]{1,0:T(8,128)(2,1)}, bf16[640,768]{1,0:T(8,128)(2,1)}, bf16[640,3072]{1,0:T(8,128)(2,1)S(1)}, bf16[640,3072]{1,0:T(8,128)(2,1)}) %tuple.91, (bf16[640,768]{1,0:T(8,128)(2,1)}, bf16[640,768]{1,0:T(8,128)(2,1)}, ...), branch_computations={%region_4.5_spmd, %region_5.6_spmd} | conditional | flops 10000000000 | bytes 8 | solution.py:764
  564.1 12.6 %up_gradient.3 = f32[768,3072]{1,0:T(8,128)} custom-call(bf16[640,768]{1,0:T(8,128)(2,1)} %get-tuple-element.44.buf_a, bf16[640,768]{1,0:T(8,128)(2,1)} %get-tuple-element.45.buf_b, bf16[640,3072]{1,0:T(8,128)(2,1)} %get-tuple-element.46.dpre_a, bf16[640,3072]{1,0:T(8,128)(2,1)} %get-tuple-element.47.dpre_b), custom_call_target="tpu_custom_call" | custom-call | flops 10000000000 | tf_op jit(solution)/shard_map/cond/branch_1_fun/up_gradient/pallas_call | solution.py:487
  (424 shorter events, 195.3 us)
Async XLA Ops:
  6.5 114.5 %collective-permute-start.36 = (bf16[768,3072]{1,0:T(8,128)(2,1)}, bf16[768,3072]{1,0:T(8,128)(2,1)}, u32[]{:S(2)}, u32[]{:S(2)}) collective-permute-start(bf16[768,3072]{1,0:T(8,128)(2,1)} %bitcast.325), channel_id=1, source_target_pairs={{0,16},{16,0},{1,17},{17,1},{2,18},{18,2},{3,19},{19,3},{4,20},{20... | collective-permute-start | bytes 14155784 | tf_op jit(solution)/shard_map/ppermute | solution.py:518
  21.9 25.5 %collective-permute-start.34 = (bf16[1,1,2,2,48,128]{5,4,3,2,1,0:T(8,128)(2,1)S(1)}, bf16[1,1,2,2,48,128]{5,4,3,2,1,0:T(8,128)(2,1)S(1)}, u32[]{:S(2)}, u32[]{:S(2)}) collective-permute-start(bf16[1,1,2,2,48,128]{5,4,3,2,1,0:T(8,128)(2,1)S(1)} %maximum_select_fusion.32), channel_id=1, source_target_pairs={{0,4},{1,5},{2,6},{3,7},{4,0},{5,1},{6,2},{7,3},{8,12},{9,13},{10,... | collective-permute-start | bytes 147464 | tf_op jit(solution)/shard_map/ppermute | solution.py:526
  47.4 73.6 %collective-permute-start.37 = (bf16[3072,768]{1,0:T(8,128)(2,1)}, bf16[3072,768]{1,0:T(8,128)(2,1)}, u32[]{:S(2)}, u32[]{:S(2)}) collective-permute-start(bf16[3072,768]{1,0:T(8,128)(2,1)} %bitcast.96.down_own), channel_id=1, source_target_pairs={{0,16},{16,0},{1,17},{17,1},{2,18},{18,2},{3,19},{19,3},{4,20},{20... | collective-permute-start | bytes 14155784 | tf_op jit(solution)/shard_map/ppermute | solution.py:518
  79.2 41.7 %all-to-all-start = ((bf16[16,40,768]{2,1,0:T(8,128)(2,1)}), bf16[16,40,768]{2,1,0:T(8,128)(2,1)}, u32[]{:S(2)}, u32[]{:S(2)}) async-start(bf16[16,40,768]{2,1,0:T(8,128)(2,1)} %bitcast.278), calls=%async_computation | async-start | bytes 1966080 | tf_op jit(solution)/shard_map/all_to_all | solution.py:697
  83.7 26.7 %collective-permute-start.13 = (bf16[2,1,1,1,1,48,256]{6,5,0,1,4,3,2:T(8,128)(2,1)S(1)}, bf16[2,1,1,1,1,48,256]{6,5,0,1,4,3,2:T(8,128)(2,1)S(1)}, u32[]{:S(2)}, u32[]{:S(2)}) collective-permute-start(bf16[2,1,1,1,1,48,256]{6,5,0,1,4,3,2:T(8,128)(2,1)S(1)} %get-tuple-element.255), channel_id=1, source_target_pairs={{0,8},{1,9},{2,10},{3,11},{4,12},{5,13},{6,14},{7,15},{8,0},{9,1},... | collective-permute-start | bytes 147464 | tf_op jit(solution)/shard_map/ppermute | solution.py:526
  86.5 23.9 %collective-permute-start.17 = (bf16[2,1,1,1,1,48,256]{6,5,0,4,3,2,1:T(8,128)(2,1)S(1)}, bf16[2,1,1,1,1,48,256]{6,5,0,4,3,2,1:T(8,128)(2,1)S(1)}, u32[]{:S(2)}, u32[]{:S(2)}) collective-permute-start(bf16[2,1,1,1,1,48,256]{6,5,0,4,3,2,1:T(8,128)(2,1)S(1)} %get-tuple-element.254), channel_id=1, source_target_pairs={{0,1},{1,0},{2,3},{3,2},{4,5},{5,4},{6,7},{7,6},{8,9},{9,8},{10,11... | collective-permute-start | bytes 147464 | tf_op jit(solution)/shard_map/ppermute | solution.py:526
  88.0 24.1 %collective-permute-start.21 = (bf16[2,1,1,1,1,48,256]{6,5,0,3,4,2,1:T(8,128)(2,1)S(1)}, bf16[2,1,1,1,1,48,256]{6,5,0,3,4,2,1:T(8,128)(2,1)S(1)}, u32[]{:S(2)}, u32[]{:S(2)}) collective-permute-start(bf16[2,1,1,1,1,48,256]{6,5,0,3,4,2,1:T(8,128)(2,1)S(1)} %get-tuple-element.251), channel_id=1, source_target_pairs={{0,2},{1,3},{2,0},{3,1},{4,6},{5,7},{6,4},{7,5},{8,10},{9,11},{10,... | collective-permute-start | bytes 147464 | tf_op jit(solution)/shard_map/ppermute | solution.py:526
  116.2 26.5 %collective-permute-start.15 = (bf16[2,2,2,1,1,48,256]{6,5,0,1,4,3,2:T(8,128)(2,1)S(1)}, bf16[2,2,2,1,1,48,256]{6,5,0,1,4,3,2:T(8,128)(2,1)S(1)}, u32[]{:S(2)}, u32[]{:S(2)}) collective-permute-start(bf16[2,2,2,1,1,48,256]{6,5,0,1,4,3,2:T(8,128)(2,1)S(1)} %maximum_select_fusion.17), channel_id=1, source_target_pairs={{0,1},{1,0},{2,3},{3,2},{4,5},{5,4},{6,7},{7,6},{8,9},{9,8},{10,11... | collective-permute-start | bytes 589832 | tf_op jit(solution)/shard_map/ppermute | solution.py:526
  117.7 27.1 %collective-permute-start.19 = (bf16[2,1,1,2,2,48,256]{6,5,0,4,3,2,1:T(8,128)(2,1)S(1)}, bf16[2,1,1,2,2,48,256]{6,5,0,4,3,2,1:T(8,128)(2,1)S(1)}, u32[]{:S(2)}, u32[]{:S(2)}) collective-permute-start(bf16[2,1,1,2,2,48,256]{6,5,0,4,3,2,1:T(8,128)(2,1)S(1)} %maximum_select_fusion.18), channel_id=1, source_target_pairs={{0,8},{1,9},{2,10},{3,11},{4,12},{5,13},{6,14},{7,15},{8,0},{9,1},... | collective-permute-start | bytes 589832 | tf_op jit(solution)/shard_map/ppermute | solution.py:526
  117.8 28.6 %collective-permute-start.23 = (bf16[2,2,1,2,1,48,256]{6,5,0,3,1,4,2:T(8,128)(2,1)S(1)}, bf16[2,2,1,2,1,48,256]{6,5,0,3,1,4,2:T(8,128)(2,1)S(1)}, u32[]{:S(2)}, u32[]{:S(2)}) collective-permute-start(bf16[2,2,1,2,1,48,256]{6,5,0,3,1,4,2:T(8,128)(2,1)S(1)} %fusion.11), channel_id=1, source_target_pairs={{0,4},{1,5},{2,6},{3,7},{4,0},{5,1},{6,2},{7,3},{8,12},{9,13},{10,... | collective-permute-start | bytes 589832 | tf_op jit(solution)/shard_map/ppermute | solution.py:526
  135.9 33.4 %all-to-all-start.1 = ((bf16[16,40,768]{2,1,0:T(8,128)(2,1)}), bf16[16,40,768]{2,1,0:T(8,128)(2,1)S(1)}, u32[]{:S(2)}, u32[]{:S(2)}) async-start(bf16[16,40,768]{2,1,0:T(8,128)(2,1)} %bitcast.279), calls=%async_computation.1 | async-start | bytes 1966080 | tf_op jit(solution)/shard_map/all_to_all | solution.py:697
  144.9 18.5 %collective-permute-start.20 = (bf16[2,2,1,2,2,48,256]{6,5,0,4,3,2,1:T(8,128)(2,1)S(1)}, bf16[2,2,1,2,2,48,256]{6,5,0,4,3,2,1:T(8,128)(2,1)S(1)}, u32[]{:S(2)}, u32[]{:S(2)}) collective-permute-start(bf16[2,2,1,2,2,48,256]{6,5,0,4,3,2,1:T(8,128)(2,1)S(1)} %maximum_select_fusion.10), channel_id=1, source_target_pairs={{0,4},{1,5},{2,6},{3,7},{4,0},{5,1},{6,2},{7,3},{8,12},{9,13},{10,... | collective-permute-start | bytes 1179656 | tf_op jit(solution)/shard_map/ppermute | solution.py:526
  219.8 26.2 %all-to-all-start.3 = ((bf16[16,40,768]{2,1,0:T(8,128)(2,1)}), bf16[16,40,768]{2,1,0:T(8,128)(2,1)S(1)}, u32[]{:S(2)}, u32[]{:S(2)}) async-start(bf16[16,40,768]{2,1,0:T(8,128)(2,1)} %bitcast.283), calls=%async_computation.3 | async-start | bytes 1966080 | tf_op jit(solution)/shard_map/all_to_all | solution.py:697
  246.1 27.5 %all-to-all-start.5 = ((bf16[16,40,768]{2,1,0:T(8,128)(2,1)}), bf16[16,40,768]{2,1,0:T(8,128)(2,1)S(1)}, u32[]{:S(2)}, u32[]{:S(2)}) async-start(bf16[16,40,768]{2,1,0:T(8,128)(2,1)} %bitcast.285), calls=%async_computation.5 | async-start | bytes 1966080 | tf_op jit(solution)/shard_map/all_to_all | solution.py:697
  273.5 27.5 %all-to-all-start.4 = ((bf16[16,40,768]{2,1,0:T(8,128)(2,1)}), bf16[16,40,768]{2,1,0:T(8,128)(2,1)S(1)}, u32[]{:S(2)}, u32[]{:S(2)}) async-start(bf16[16,40,768]{2,1,0:T(8,128)(2,1)} %bitcast.284), calls=%async_computation.4 | async-start | bytes 1966080 | tf_op jit(solution)/shard_map/all_to_all | solution.py:697
  279.3 68.2 %collective-permute-start.82 = (bf16[640,3072]{1,0:T(8,128)(2,1)}, bf16[640,3072]{1,0:T(8,128)(2,1)}, u32[]{:S(2)}, u32[]{:S(2)}) collective-permute-start(bf16[640,3072]{1,0:T(8,128)(2,1)} %get-tuple-element.167), channel_id=1, source_target_pairs={{0,16},{1,17},{2,18},{3,19},{4,20},{5,21},{6,22},{7,23},{8,24},{9,... | collective-permute-start | bytes 11796488 | tf_op jit(solution)/shard_map/ppermute | solution.py:522
  282.6 101.8 %collective-permute-start.78 = (bf16[640,3072]{1,0:T(8,128)(2,1)}, bf16[640,3072]{1,0:T(8,128)(2,1)}, u32[]{:S(2)}, u32[]{:S(2)}) collective-permute-start(bf16[640,3072]{1,0:T(8,128)(2,1)} %get-tuple-element.165), channel_id=1, source_target_pairs={{0,16},{1,17},{2,18},{3,19},{4,20},{5,21},{6,22},{7,23},{8,24},{9,... | collective-permute-start | bytes 11796488 | tf_op jit(solution)/shard_map/ppermute | solution.py:522
  336.7 27.8 %all-to-all-start.6 = ((bf16[16,40,768]{2,1,0:T(8,128)(2,1)}), bf16[16,40,768]{2,1,0:T(8,128)(2,1)}, u32[]{:S(2)}, u32[]{:S(2)}) async-start(bf16[16,40,768]{2,1,0:T(8,128)(2,1)} %bitcast.280), calls=%async_computation.6 | async-start | bytes 1966080 | tf_op jit(solution)/shard_map/all_to_all | solution.py:697
  344.0 40.5 %collective-permute-start.58 = (bf16[2,768,768]{2,1,0:T(8,128)(2,1)}, bf16[2,768,768]{2,1,0:T(8,128)(2,1)}, u32[]{:S(2)}, u32[]{:S(2)}) collective-permute-start(bf16[2,768,768]{2,1,0:T(8,128)(2,1)} %get-tuple-element.162), channel_id=1, source_target_pairs={{0,16},{16,0},{1,17},{17,1},{2,18},{18,2},{3,19},{19,3},{4,20},{20... | collective-permute-start | bytes 7077896 | tf_op jit(solution)/shard_map/ppermute | solution.py:518
  346.2 216.4 %collective-permute-start.79 = (bf16[640,768]{1,0:T(8,128)(2,1)}, bf16[640,768]{1,0:T(8,128)(2,1)}, u32[]{:S(2)}, u32[]{:S(2)}) collective-permute-start(bf16[640,768]{1,0:T(8,128)(2,1)} %bitcast.94.x_ref), channel_id=1, source_target_pairs={{16,0},{17,1},{18,2},{19,3},{20,4},{21,5},{22,6},{23,7},{24,8},{25... | collective-permute-start | bytes 2949128 | tf_op jit(solution)/shard_map/ppermute | solution.py:522
  347.5 71.3 %collective-permute-start.84 = (bf16[640,3072]{1,0:T(8,128)(2,1)}, bf16[640,3072]{1,0:T(8,128)(2,1)}, u32[]{:S(2)}, u32[]{:S(2)}) collective-permute-start(bf16[640,3072]{1,0:T(8,128)(2,1)} %get-tuple-element.168), channel_id=1, source_target_pairs={{16,0},{17,1},{18,2},{19,3},{20,4},{21,5},{22,6},{23,7},{24,8},{25... | collective-permute-start | bytes 11796488 | tf_op jit(solution)/shard_map/ppermute | solution.py:522
  349.5 33.7 %collective-permute-start.77 = (bf16[640,768]{1,0:T(8,128)(2,1)}, bf16[640,768]{1,0:T(8,128)(2,1)}, u32[]{:S(2)}, u32[]{:S(2)}) collective-permute-start(bf16[640,768]{1,0:T(8,128)(2,1)} %bitcast.102.x_ref), channel_id=1, source_target_pairs={{0,16},{1,17},{2,18},{3,19},{4,20},{5,21},{6,22},{7,23},{8,24},{9,... | collective-permute-start | bytes 2949128 | tf_op jit(solution)/shard_map/ppermute | solution.py:522
  377.3 71.1 %all-to-all-start.7 = ((bf16[16,40,768]{2,1,0:T(8,128)(2,1)}), bf16[16,40,768]{2,1,0:T(8,128)(2,1)}, u32[]{:S(2)}, u32[]{:S(2)}) async-start(bf16[16,40,768]{2,1,0:T(8,128)(2,1)} %bitcast.276), calls=%async_computation.7 | async-start | bytes 1966080 | tf_op jit(solution)/shard_map/all_to_all | solution.py:697
  383.2 40.2 %collective-permute-start.83 = (bf16[640,768]{1,0:T(8,128)(2,1)}, bf16[640,768]{1,0:T(8,128)(2,1)}, u32[]{:S(2)}, u32[]{:S(2)}) collective-permute-start(bf16[640,768]{1,0:T(8,128)(2,1)} %bitcast.113.dout_ref), channel_id=1, source_target_pairs={{16,0},{17,1},{18,2},{19,3},{20,4},{21,5},{22,6},{23,7},{24,8},{25... | collective-permute-start | bytes 2949128 | tf_op jit(solution)/shard_map/ppermute | solution.py:522
  389.1 19.1 %collective-permute-start.63 = (bf16[2,2,1,2,2,48,256]{6,5,0,4,3,2,1:T(8,128)(2,1)S(1)}, bf16[2,2,1,2,2,48,256]{6,5,0,4,3,2,1:T(8,128)(2,1)S(1)}, u32[]{:S(2)}, u32[]{:S(2)}) collective-permute-start(bf16[2,2,1,2,2,48,256]{6,5,0,4,3,2,1:T(8,128)(2,1)S(1)} %broadcast_select_fusion.4), channel_id=1, source_target_pairs={{0,4},{1,5},{2,6},{3,7},{4,0},{5,1},{6,2},{7,3},{8,12},{9,13},{10,... | collective-permute-start | bytes 1179656 | tf_op jit(solution)/shard_map/ppermute | solution.py:526
  405.4 157.2 %collective-permute-start.80 = (bf16[640,3072]{1,0:T(8,128)(2,1)}, bf16[640,3072]{1,0:T(8,128)(2,1)}, u32[]{:S(2)}, u32[]{:S(2)}) collective-permute-start(bf16[640,3072]{1,0:T(8,128)(2,1)} %get-tuple-element.166), channel_id=1, source_target_pairs={{16,0},{17,1},{18,2},{19,3},{20,4},{21,5},{22,6},{23,7},{24,8},{25... | collective-permute-start | bytes 11796488 | tf_op jit(solution)/shard_map/ppermute | solution.py:522
  418.7 19.0 %collective-permute-start.68 = (bf16[2,2,1,2,1,48,256]{6,5,0,4,3,2,1:T(8,128)(2,1)S(1)}, bf16[2,2,1,2,1,48,256]{6,5,0,4,3,2,1:T(8,128)(2,1)S(1)}, u32[]{:S(2)}, u32[]{:S(2)}) collective-permute-start(bf16[2,2,1,2,1,48,256]{6,5,0,4,3,2,1:T(8,128)(2,1)S(1)} %broadcast_select_fusion.9), channel_id=1, source_target_pairs={{0,4},{1,5},{2,6},{3,7},{4,0},{5,1},{6,2},{7,3},{8,12},{9,13},{10,... | collective-permute-start | bytes 589832 | tf_op jit(solution)/shard_map/ppermute | solution.py:526
  418.9 19.0 %collective-permute-start.64 = (bf16[2,1,1,2,2,48,256]{6,5,0,4,3,2,1:T(8,128)(2,1)S(1)}, bf16[2,1,1,2,2,48,256]{6,5,0,4,3,2,1:T(8,128)(2,1)S(1)}, u32[]{:S(2)}, u32[]{:S(2)}) collective-permute-start(bf16[2,1,1,2,2,48,256]{6,5,0,4,3,2,1:T(8,128)(2,1)S(1)} %broadcast_select_fusion.11), channel_id=1, source_target_pairs={{0,8},{1,9},{2,10},{3,11},{4,12},{5,13},{6,14},{7,15},{8,0},{9,1},... | collective-permute-start | bytes 589832 | tf_op jit(solution)/shard_map/ppermute | solution.py:526
  445.3 36.0 %collective-permute-start.66 = (bf16[2,1,1,1,1,48,256]{6,5,0,4,3,2,1:T(8,128)(2,1)S(1)}, bf16[2,1,1,1,1,48,256]{6,5,0,4,3,2,1:T(8,128)(2,1)S(1)}, u32[]{:S(2)}, u32[]{:S(2)}) collective-permute-start(bf16[2,1,1,1,1,48,256]{6,5,0,4,3,2,1:T(8,128)(2,1)S(1)} %broadcast_select_fusion.24), channel_id=1, source_target_pairs={{0,1},{1,0},{2,3},{3,2},{4,5},{5,4},{6,7},{7,6},{8,9},{9,8},{10,11... | collective-permute-start | bytes 147464 | tf_op jit(solution)/shard_map/ppermute | solution.py:526
  446.2 47.2 %collective-permute-start.62 = (bf16[2,1,1,1,1,48,256]{6,5,0,4,3,2,1:T(8,128)(2,1)S(1)}, bf16[2,1,1,1,1,48,256]{6,5,0,4,3,2,1:T(8,128)(2,1)S(1)}, u32[]{:S(2)}, u32[]{:S(2)}) collective-permute-start(bf16[2,1,1,1,1,48,256]{6,5,0,4,3,2,1:T(8,128)(2,1)S(1)} %broadcast_select_fusion.26), channel_id=1, source_target_pairs={{0,8},{1,9},{2,10},{3,11},{4,12},{5,13},{6,14},{7,15},{8,0},{9,1},... | collective-permute-start | bytes 147464 | tf_op jit(solution)/shard_map/ppermute | solution.py:526
  488.6 23.6 %collective-permute-start.45 = (bf16[2,768,768]{2,1,0:T(8,128)(2,1)}, bf16[2,768,768]{2,1,0:T(8,128)(2,1)S(1)}, u32[]{:S(2)}, u32[]{:S(2)}) collective-permute-start(bf16[2,768,768]{2,1,0:T(8,128)(2,1)} %get-tuple-element.160), channel_id=1, source_target_pairs={{0,16},{16,0},{1,17},{17,1},{2,18},{18,2},{3,19},{19,3},{4,20},{20... | collective-permute-start | bytes 7077896 | tf_op jit(solution)/shard_map/ppermute | solution.py:518
  505.1 55.8 %collective-permute-start.39 = (f32[384,768]{1,0:T(8,128)S(1)}, f32[384,768]{1,0:T(8,128)S(1)}, u32[]{:S(2)}, u32[]{:S(2)}) collective-permute-start(f32[384,768]{1,0:T(8,128)S(1)} %broadcast_select_fusion), channel_id=1, source_target_pairs={{0,16},{16,0},{1,17},{17,1},{2,18},{18,2},{3,19},{19,3},{4,20},{20... | collective-permute-start | bytes 3538952 | tf_op jit(solution)/shard_map/ppermute | solution.py:518
  (98 other events, 1025.3 us)

commit v2 on v1

v2 whole, which is shorter than its diff:
```python
import functools

import jax
import jax.numpy as jnp
from jax import lax
from jax.experimental import pallas as pl
from jax.experimental.pallas import tpu as pltpu
from jax.sharding import PartitionSpec as P

bucket_edges = (12, 16, 23, 32, 46, 64, 91)
norm_eps = 1e-06
gelu_c = 0.7978845608028654
gelu_cube = 0.044715
masked_score = -1e30
highest = lax.Precision.HIGHEST
f32 = jnp.float32
bf16 = jnp.bfloat16
vmem_bytes = 56 * 2**20
pieces = 3


def dot(left, right):
    return jnp.dot(left, right, preferred_element_type=f32)


def dot_lead(left, right):
    return lax.dot_general(left, right, (((0,), (0,)), ((), ())), preferred_element_type=f32)


def dot_last(left, right):
    return lax.dot_general(left, right, (((1,), (1,)), ((), ())), preferred_element_type=f32)


def gelu_pair(value):
    square = value * value
    inner = jnp.tanh(gelu_c * value * (1.0 + gelu_cube * square))
    half = 0.5 * (1.0 + inner)
    slope = half + 0.5 * value * (1.0 - inner * inner) * (
        gelu_c * (1.0 + 3.0 * gelu_cube * square)
    )
    return (value * half, slope)


def bucket_of(offset):
    distance = jnp.abs(offset)
    found = 16 * (offset > 0).astype(jnp.int32) + jnp.minimum(distance, 8)
    for edge in bucket_edges:
        found = found + (distance >= edge).astype(jnp.int32)
    return found


def norm_scale(values):
    return lax.rsqrt(jnp.mean(values * values, axis=-1, keepdims=True) + norm_eps)


def norm_backward(values, gain, grad_normed):
    scale = norm_scale(values)
    normal = values * scale
    inner = grad_normed * gain
    grad_values = scale * (inner - normal * jnp.mean(inner * normal, axis=-1, keepdims=True))
    return (grad_values, jnp.sum(grad_normed * normal, axis=0, keepdims=True))


def zero_token(token_ref):
    token_ref[0] = 0


def weight_copies(place_ref, layer, matrices, blocks, weights, router, sems):
    core, device = place_ref[0], place_ref[1]
    first, count = matrices
    copies = []
    for p in range(pieces):
        for (here, differ), (there, _) in zip(blocks[0][p], blocks[1][p]):
            rows, step = here.shape[2:]
            for at in range(here.shape[0]):
                target = pl.ds(pl.multiple_of((device ^ differ[at]) * rows, rows), rows)
                couples = [
                    (pl.ds(first, count), pl.ds(0, step), weights.at[:, target, pl.ds(p * step, step)])
                ]
                if p == 0 and router is not None:
                    couples.append((4, pl.ds(0, 128), router.at[target, :]))
                for which, lanes, goal in couples:
                    sem = sems.at[len(copies)]
                    own = pltpu.make_async_copy(here.at[at, which, :, lanes], goal, sem)
                    other = pltpu.make_async_copy(there.at[at, which, :, lanes], goal, sem)
                    copies.append(own)
                    pl.when(core == layer)(own.start)
                    pl.when(core != layer)(other.start)
    return copies


def laid_out(layout, refs):
    blocks, at = [], 0
    for _ in range(2):
        blocks.append([])
        for piece in layout:
            blocks[-1].append([(refs[at + i], differ) for i, differ in enumerate(piece)])
            at += len(piece)
    return blocks, refs[at:]


def join_kernel(place_ref, *refs):
    olds, gots, outs = refs[:pieces], refs[pieces : 2 * pieces], refs[2 * pieces :]
    token_ref, outs = outs[0], outs[1:]
    zero_token(token_ref)
    for old, got, out in zip(olds, gots, outs):
        half = old.shape[0]
        out[:half] = old[...]
        out[half:] = got[...]


def head_masks():
    lane = lax.broadcasted_iota(jnp.int32, (1, 128), 1)
    low = (lane < 64).astype(f32)
    return (low.astype(bf16), (1.0 - low).astype(bf16))


def bias_kernel(line_ref, base_ref):
    heads, _, reach = base_ref.shape
    wide = line_ref.shape[1]

    def one(head, carry):
        line = jnp.broadcast_to(line_ref[pl.ds(head, 1), :], (128, wide))
        turned = pltpu.roll(line, wide - 127, 1, stride=1, stride_axis=0)
        base_ref[head] = turned[:, :reach]
        return carry

    lax.fori_loop(0, heads, one, 0)


def bias_of(base_ref, head, rows):
    blocks = rows // 128
    return jnp.concatenate(
        [base_ref[head, :, 128 * (blocks - 1 - a) : 128 * (blocks - 1 - a) + rows] for a in range(blocks)],
        axis=0,
    )


def diagonal_line(grad_scores, flip, wide):
    blocks = grad_scores.shape[0] // 128
    parts = [None] * (wide // 128)
    for a in range(blocks):
        flipped = dot(flip, grad_scores[128 * a : 128 * (a + 1), :])
        for j in range(blocks):
            piece = flipped[:, 128 * j : 128 * (j + 1)]
            at = j + blocks - 1 - a
            parts[at] = piece if parts[at] is None else parts[at] + piece
    empty = jnp.zeros((128, 128), f32)
    sums = jnp.concatenate([empty if part is None else part for part in parts], axis=1)
    turned = pltpu.roll(sums, 0, 1, stride=1, stride_axis=0)
    return jnp.sum(turned, axis=0, keepdims=True)


def one_hot_columns(place_col, slots):
    rows = place_col.shape[0]
    return (place_col == lax.broadcasted_iota(jnp.int32, (rows, slots), 1)).astype(f32).astype(bf16)


def one_hot_rows(place_row, slots):
    rows = place_row.shape[1]
    return (place_row == lax.broadcasted_iota(jnp.int32, (slots, rows), 0)).astype(f32).astype(bf16)


def forward_kernel(second, experts, layout, core_ref, *refs):
    blocks, refs = laid_out(layout, refs)
    if second:
        (before_ref, gate_before_ref, place_before_ref, back_ref, cot_ref), refs = refs[:5], refs[5:]
    else:
        (x_ref,), refs = refs[:1], refs[1:]
    (gain_ref, base_ref, seg_col_ref, seg_row_ref, route_ref, place_ref), refs = (
        refs[:6],
        refs[6:],
    )
    (
        token_ref, q_ref, k_ref, v_ref, o_ref, p_ref, mid_ref, h2_ref, share_ref, gate_ref, send_ref,
    ), refs = refs[:11], refs[11:]
    if second:
        (x_out_ref, combined_ref, grad_send_ref), refs = refs[:3], refs[3:]
    weights, router_ref, mask_ref, sems = refs
    zero_token(token_ref)
    copies = weight_copies(core_ref, int(second), (0, 4), blocks, weights, router_ref, sems)
    slots = send_ref.shape[0]
    rows = q_ref.shape[0]
    if second:
        scatter = one_hot_columns(place_before_ref[...], slots)
        combined = dot(scatter, back_ref[...])
        combined_ref[...] = combined.astype(bf16)
        low = (before_ref[...] + gate_before_ref[...] * combined).astype(bf16)
        x_out_ref[...] = low
        wide = low.astype(f32)
    else:
        wide = x_ref[...].astype(f32)
    h1 = (wide * norm_scale(wide) * gain_ref[0:1, :]).astype(bf16)
    mask_ref[...] = jnp.where(seg_col_ref[...] == seg_row_ref[...], 0.0, masked_score)
    for copy in copies:
        copy.wait()
    q_ref[...] = dot(h1, weights[0]).astype(bf16)
    k_ref[...] = dot(h1, weights[1]).astype(bf16)
    v_ref[...] = dot(h1, weights[2]).astype(bf16)
    masks = head_masks()

    def pair(p, carry):
        columns = pl.ds(pl.multiple_of(p * 128, 128), 128)
        queries, keys, values = q_ref[:, columns], k_ref[:, columns], v_ref[:, columns]
        mixed = jnp.zeros((rows, 128), f32)
        for half in range(2):
            head = 2 * p + half
            scores = dot_last(queries * masks[half], keys) * 0.125 + bias_of(base_ref, head, rows)
            scores = scores + mask_ref[...]
            raised = jnp.exp(scores - jnp.max(scores, axis=-1, keepdims=True))
            total = jnp.sum(raised, axis=-1, keepdims=True)
            shares = (raised * (1.0 / total)).astype(bf16)
            p_ref[head] = shares
            mixed = mixed + dot(shares, values * masks[half])
        o_ref[:, columns] = mixed.astype(bf16)
        return carry

    lax.fori_loop(0, p_ref.shape[0] // 2, pair, 0)
    middle = wide + dot(o_ref[...], weights[3])
    mid_ref[...] = middle
    h2 = (middle * norm_scale(middle) * gain_ref[1:2, :]).astype(bf16)
    h2_ref[...] = h2
    logits = dot(h2, router_ref[...])
    lane = lax.broadcasted_iota(jnp.int32, (1, 128), 1)
    logits = jnp.where(lane < experts, logits, masked_score)
    raised = jnp.exp(logits - jnp.max(logits, axis=-1, keepdims=True))
    shares = raised / jnp.sum(raised, axis=-1, keepdims=True)
    share_ref[...] = shares
    chosen = route_ref[...] == lax.broadcasted_iota(jnp.int32, shares.shape, 1)
    gate = jnp.sum(jnp.where(chosen, shares, 0.0), axis=-1, keepdims=True)
    gate_ref[...] = gate
    gather = one_hot_rows(place_ref[...], slots)
    send_ref[...] = dot(gather, h2).astype(bf16)
    if second:
        grad_out = (gate * cot_ref[...].astype(f32)).astype(bf16)
        grad_send_ref[...] = dot(gather, grad_out).astype(bf16)


def heads_backward_kernel(second, layout, core_ref, *refs):
    blocks, refs = laid_out(layout, refs)
    (
        q_ref, k_ref, v_ref, p_ref, mid_ref, h2_ref, share_ref, gate_ref, dy_ref, dback_ref,
        out_ref, gain_ref, route_ref, place_ref,
    ), refs = refs[:14], refs[14:]
    (
        token_ref, dx1_ref, low_ref, dq_ref, dk_ref, dv_ref, router_grad_ref, gain_grad_ref,
        line_grad_ref,
    ), refs = refs[:9], refs[9:]
    if second:
        (y_ref,), refs = refs[:1], refs[1:]
    weights, router_ref, do_ref, sems = refs
    zero_token(token_ref)
    copies = weight_copies(core_ref, int(second), (3, 1), blocks, weights, router_ref, sems)
    rows = q_ref.shape[0]
    slots = dback_ref.shape[0]
    dy = dy_ref[...].astype(f32)
    gate = gate_ref[...]
    middle = mid_ref[...]
    scatter = one_hot_columns(place_ref[...], slots)
    if second:
        combined = dot(one_hot_columns(out_ref[...], slots), dback_ref[...])
        y_ref[...] = (middle + gate * combined).astype(bf16)
    else:
        combined = out_ref[...].astype(f32)
    grad_gate = jnp.sum(dy * combined, axis=-1, keepdims=True)
    shares = share_ref[...]
    chosen = route_ref[...] == lax.broadcasted_iota(jnp.int32, shares.shape, 1)
    grad_logits = (grad_gate * gate * (chosen.astype(f32) - shares)).astype(bf16)
    router_grad_ref[...] = dot_lead(grad_logits, h2_ref[...])[: router_grad_ref.shape[0]]
    for copy in copies:
        copy.wait()
    grad_two = dot(scatter, dback_ref[...]) + dot_last(grad_logits, router_ref[...])
    grad_middle, gain_two = norm_backward(middle, gain_ref[1:2, :], grad_two)
    gain_grad_ref[...] = gain_two
    grad_middle = grad_middle + dy
    dx1_ref[...] = grad_middle
    low = grad_middle.astype(bf16)
    low_ref[...] = low
    do_ref[...] = dot_last(low, weights[0]).astype(bf16)
    masks = head_masks()
    flip = (
        lax.broadcasted_iota(jnp.int32, (128, 128), 0)
        + lax.broadcasted_iota(jnp.int32, (128, 128), 1)
        == 127
    )
    flip = flip.astype(f32).astype(bf16)

    def pair(p, carry):
        columns = pl.ds(pl.multiple_of(p * 128, 128), 128)
        queries, keys, values = q_ref[:, columns], k_ref[:, columns], v_ref[:, columns]
        grad_mixed = do_ref[:, columns]
        dq = jnp.zeros((rows, 128), f32)
        dk = jnp.zeros((rows, 128), f32)
        dv = jnp.zeros((rows, 128), f32)
        for half in range(2):
            head = 2 * p + half
            own_mixed = grad_mixed * masks[half]
            low_shares = p_ref[head]
            shares = low_shares.astype(f32)
            grad_shares = dot_last(own_mixed, values)
            mean = jnp.sum(shares * grad_shares, axis=-1, keepdims=True)
            grad_scores = (shares * (grad_shares - mean)).astype(bf16)
            dv = dv + dot_lead(low_shares, own_mixed)
            dq = dq + dot(grad_scores, keys * masks[half])
            dk = dk + dot_lead(grad_scores, queries * masks[half])
            line_grad_ref[pl.ds(head, 1), :] = diagonal_line(
                grad_scores, flip, line_grad_ref.shape[1]
            )
        dq_ref[:, columns] = (dq * 0.125).astype(bf16)
        dk_ref[:, columns] = (dk * 0.125).astype(bf16)
        dv_ref[:, columns] = dv.astype(bf16)
        return carry

    lax.fori_loop(0, p_ref.shape[0] // 2, pair, 0)


def input_backward_kernel(second, layout, core_ref, *refs):
    blocks, refs = laid_out(layout, refs)
    (x_ref, dx1_ref, dq_ref, dk_ref, dv_ref, gain_ref), refs = refs[:6], refs[6:]
    if second:
        (gate_next_ref, place_next_ref), refs = refs[:2], refs[2:]
    (token_ref, dx_ref, gain_grad_ref), refs = refs[:3], refs[3:]
    if second:
        (low_out_ref, grad_send_ref), refs = refs[:2], refs[2:]
    weights, sems = refs
    zero_token(token_ref)
    copies = weight_copies(core_ref, int(second), (0, 3), blocks, weights, None, sems)
    for copy in copies:
        copy.wait()
    wide = x_ref[...].astype(f32)
    grad_one = (
        dot_last(dq_ref[...], weights[0])
        + dot_last(dk_ref[...], weights[1])
        + dot_last(dv_ref[...], weights[2])
    )
    grad_inputs, gain_one = norm_backward(wide, gain_ref[0:1, :], grad_one)
    grad_inputs = grad_inputs + dx1_ref[...]
    dx_ref[...] = grad_inputs
    gain_grad_ref[...] = gain_one
    if second:
        low = grad_inputs.astype(bf16)
        low_out_ref[...] = low
        grad_out = (gate_next_ref[...] * low.astype(f32)).astype(bf16)
        gather = one_hot_rows(place_next_ref[...], grad_send_ref.shape[0])
        grad_send_ref[...] = dot(gather, grad_out).astype(bf16)


def weight_backward_kernel(core_ref, x_ref, gain_ref, o_ref, low_ref, dq_ref, dk_ref, dv_ref, *refs):
    token_ref, keep_ref, give_ref = refs
    zero_token(token_ref)
    core = core_ref[0]

    def put(matrix, value):
        value = value.astype(bf16)

        @pl.when(core == matrix // 2)
        def _():
            keep_ref[matrix % 2] = value

        @pl.when(core != matrix // 2)
        def _():
            give_ref[matrix % 2] = value

    wide = x_ref[...].astype(f32)
    h1 = (wide * norm_scale(wide) * gain_ref[0:1, :]).astype(bf16)
    put(0, dot_lead(h1, dq_ref[...]))
    put(1, dot_lead(h1, dk_ref[...]))
    put(2, dot_lead(h1, dv_ref[...]))
    put(3, dot_lead(o_ref[...], low_ref[...]))


def places_of(block, order):
    place = 0
    for bit in order:
        place = 2 * place + ((block >> bit) & 1)
    return place


def fold_first_kernel(orders, device_ref, *refs):
    sums, outs = refs[:4], refs[4:]
    token_ref, outs = outs[0], outs[1:]
    zero_token(token_ref)
    keeps, sends = outs[:pieces], outs[pieces:]
    device = device_ref[0]
    half, rows, step = keeps[0].shape[1:]
    for block in range(2 * half):
        at = pl.ds(pl.multiple_of((device ^ block) * rows, rows), rows)
        for layer in range(2):
            for matrix in range(2):
                total = sums[2 * layer][matrix, at, :].astype(f32)
                total = (total + sums[2 * layer + 1][matrix, at, :].astype(f32)).astype(bf16)
                for p in range(pieces):
                    place = places_of(block, orders[p])
                    target = sends[p] if place >= half else keeps[p]
                    target[2 * layer + matrix, place % half] = total[:, p * step : (p + 1) * step]


def fold_kernel(device_ref, *refs):
    olds, gots, outs = refs[:pieces], refs[pieces : 2 * pieces], refs[2 * pieces :]
    token_ref, outs = outs[0], outs[1:]
    zero_token(token_ref)
    for p in range(pieces):
        total = olds[p][...].astype(f32) + gots[p][...].astype(f32)
        half = total.shape[1] // 2
        outs[p][...] = total[:, :half].astype(bf16)
        outs[pieces + p][...] = total[:, half:].astype(bf16)


def fold_last_kernel(device_ref, *refs):
    olds, gots, (token_ref, out_ref) = refs[:pieces], refs[pieces : 2 * pieces], refs[2 * pieces :]
    zero_token(token_ref)
    for p in range(pieces):
        step = olds[p].shape[3]
        total = olds[p][...].astype(f32) + gots[p][...].astype(f32)
        out_ref[:, :, p * step : (p + 1) * step] = total[:, 0]


def expert_copies(mine, tiles, up_refs, down_refs, up, down, sems, start):
    width = up.shape[2]

    def copies(which):
        found = []
        for j in range(tiles):
            at = pl.ds(j * width, width)
            found.append(
                (
                    pltpu.make_async_copy(up_refs[which].at[:, at], up.at[j], sems.at[0, j]),
                    pltpu.make_async_copy(down_refs[which].at[at, :], down.at[j], sems.at[1, j]),
                )
            )
        return found

    if start:
        for which in range(2):

            @pl.when(mine == 1 - which)
            def _():
                for couple in copies(which):
                    for copy in couple:
                        copy.start()


def expert_wait(j, up_ref, down_ref, up, down, sems):
    width = up.shape[2]
    at = pl.ds(0, width)
    pltpu.make_async_copy(up_ref.at[:, at], up.at[j], sems.at[0, j]).wait()
    pltpu.make_async_copy(down_ref.at[at, :], down.at[j], sems.at[1, j]).wait()


def expert_forward_kernel(
    mine_ref, x_ref, up_own, up_other, down_own, down_other, act_ref, slope_ref, out_ref,
    up, down, total, sems,
):
    j = pl.program_id(0)
    tiles = up.shape[0]

    @pl.when(j == 0)
    def _():
        expert_copies(
            mine_ref[0], tiles, (up_own, up_other), (down_own, down_other), up, down, sems, True
        )
        total[...] = jnp.zeros_like(total)

    expert_wait(j, up_own, down_own, up, down, sems)
    active, slope = gelu_pair(dot(x_ref[...], up[j]))
    active = active.astype(bf16)
    act_ref[...] = active
    slope_ref[...] = slope.astype(bf16)
    total[...] += dot(active, down[j])

    @pl.when(j == tiles - 1)
    def _():
        out_ref[...] = total[...].astype(bf16)


def expert_backward_kernel(
    mine_ref, dout_ref, slope_ref, up_own, up_other, down_own, down_other, dpre_ref, dbuf_ref,
    up, down, total, sems,
):
    j = pl.program_id(0)
    tiles = up.shape[0]

    @pl.when(j == 0)
    def _():
        expert_copies(
            mine_ref[0], tiles, (up_own, up_other), (down_own, down_other), up, down, sems, True
        )
        total[...] = jnp.zeros_like(total)

    expert_wait(j, up_own, down_own, up, down, sems)
    grad_pre = (dot_last(dout_ref[...], down[j]) * slope_ref[...].astype(f32)).astype(bf16)
    dpre_ref[...] = grad_pre
    total[...] += dot_last(grad_pre, up[j])

    @pl.when(j == tiles - 1)
    def _():
        dbuf_ref[...] = total[...].astype(bf16)


def up_grad_kernel(buf_a, buf_b, dpre_a, dpre_b, grad_ref):
    grad_ref[...] = dot_lead(buf_a[...], dpre_a[...]) + dot_lead(buf_b[...], dpre_b[...])


def down_grad_kernel(dout_a, dout_b, act_a, act_b, grad_ref):
    grad_ref[...] = dot_lead(act_a[...], dout_a[...]) + dot_lead(act_b[...], dout_b[...])


def shape(dims, kind=bf16):
    return jax.ShapeDtypeStruct(dims, kind)


def params():
    return pltpu.CompilerParams(vmem_limit_bytes=vmem_bytes)


def cost(us):
    return pl.CostEstimate(flops=int(us * 1e9), bytes_accessed=0, transcendentals=0)


smem = pl.BlockSpec(memory_space=pltpu.SMEM)
vmem = pl.BlockSpec(memory_space=pltpu.VMEM)
anywhere = pl.BlockSpec(memory_space=pl.ANY)


def run(kernel, name, us, inputs, outs, scratch, core, weights=(), after=()):
    def marked(core_ref, *refs):
        at = len(weights) + len(inputs)
        return kernel(core_ref, *refs[:at], *refs[at + len(after) :])

    outs = [shape((1,), jnp.int32)] + list(outs)
    return pl.pallas_call(
        marked,
        out_shape=outs,
        in_specs=[smem]
        + [anywhere] * len(weights)
        + [vmem] * len(inputs)
        + [anywhere] * len(after),
        out_specs=[smem] + [vmem] * (len(outs) - 1),
        scratch_shapes=scratch,
        compiler_params=params(),
        cost_estimate=cost(us),
        name=name,
    )(core, *weights, *inputs, *after)


def weight_scratch(layout, count, width, router):
    copies = sum(len(differ) for piece in layout for differ in piece)
    held = [pltpu.VMEM((count, width, width), bf16)]
    if router:
        copies += sum(len(differ) for differ in layout[0])
        held.append(pltpu.VMEM((width, 128), bf16))
    return held, [pltpu.SemaphoreType.DMA((copies,))]


def run_bias(line, rows):
    heads, wide = line.shape
    return pl.pallas_call(
        bias_kernel,
        out_shape=shape((heads, 128, 2 * rows - 128), f32),
        in_specs=[vmem],
        out_specs=vmem,
        compiler_params=params(),
        cost_estimate=cost(3),
        name="bias_base",
    )(line)


def run_forward(second, layout, core, weights, inputs, slots, experts, heads, after):
    rows, width = inputs[0].shape
    outs = [shape((rows, width))] * 4 + [
        shape((heads, rows, rows)),
        shape((rows, width), f32),
        shape((rows, width)),
        shape((rows, 128), f32),
        shape((rows, 1), f32),
        shape((slots, width)),
    ]
    if second:
        outs += [shape((rows, width)), shape((rows, width)), shape((slots, width))]
    held, sems = weight_scratch(layout, 4, width, True)
    return run(
        functools.partial(forward_kernel, second, experts, layout), "attention_forward", 15, inputs, outs,
        held + [pltpu.VMEM((rows, rows), f32)] + sems, core, weights, after,
    )


def run_heads_backward(second, layout, core, weights, inputs, experts, after):
    rows, width = inputs[0].shape
    heads = inputs[3].shape[0]
    outs = [shape((rows, width), f32)] + [shape((rows, width))] * 4 + [
        shape((experts, width), f32),
        shape((1, width), f32),
        shape((heads, 2 * rows), f32),
    ]
    if second:
        outs += [shape((rows, width))]
    held, sems = weight_scratch(layout, 1, width, True)
    return run(
        functools.partial(heads_backward_kernel, second, layout), "heads_backward", 20, inputs, outs,
        held + [pltpu.VMEM((rows, width), bf16)] + sems, core, weights, after,
    )


def run_input_backward(second, layout, core, weights, inputs, slots, after):
    rows, width = inputs[0].shape
    outs = [shape((rows, width), f32), shape((1, width), f32)]
    if second:
        outs += [shape((rows, width)), shape((slots, width))]
    held, sems = weight_scratch(layout, 3, width, False)
    return run(
        functools.partial(input_backward_kernel, second, layout), "input_backward", 6, inputs, outs,
        held + sems, core, weights, after,
    )


def run_weight_backward(core, inputs, after):
    width = inputs[0].shape[1]
    outs = [shape((2, width, width))] * 2
    return run(weight_backward_kernel, "weight_backward", 6, inputs, outs, [], core, (), after)


def summed_blocks(pairs, little, device, devices, beside, after):
    bits = devices.bit_length() - 1
    _, tall, width = pairs[0].shape
    rows, step = tall // devices, width // pieces
    orders = [order[::-1] for order in bit_orders(bits)]
    me = device.astype(jnp.int32).reshape(1)
    if rows % 16:
        found = unfolded(
            jnp.concatenate(
                [(pairs[i].astype(f32) + pairs[i + 1].astype(f32)).astype(bf16) for i in (0, 2)]
            ),
            devices,
        )
        for at in range(bits):
            found = folded(found, at, device, devices)
            little = little + across(little, at, devices)
        sums = jnp.concatenate([p.reshape(4, rows, -1) for p in found], 2)
        return sums, little, [call(0) for call in beside]
    half = devices // 2
    outs = [shape((4, half, rows, step))] * (2 * pieces)
    found = run(
        functools.partial(fold_first_kernel, orders), "fold_first", 4, pairs, outs, [], me, (), after
    )
    results = []
    for at in range(bits):
        token, found = found[0], found[1:]
        after = ()
        if at < len(beside):
            after = (beside[at](token[0]),)
            results.extend(after)
        keeps = found[:pieces]
        gots = [across(found[pieces + p], orders[p][at], devices) for p in range(pieces)]
        little = little + token.astype(f32)
        little = little + across(little, at, devices)
        half //= 2
        if half:
            outs = [shape((4, half, rows, step))] * (2 * pieces)
            found = run(fold_kernel, "fold", 2, [*keeps, *gots], outs, [], me, (), after)
        else:
            outs = [shape((4, rows, width), f32)]
            found = run(fold_last_kernel, "fold_last", 1, [*keeps, *gots], outs, [], me)
    return found[1], little, results


def run_expert(kernel, mine, tall, middles, ups, downs, n_middle, us, name):
    slots, width = tall.shape
    inner = ups[0].shape[1]
    tiles = 6 if inner % 768 == 0 else 1
    tile = inner // tiles
    whole = pl.BlockSpec((slots, width), lambda j: (0, 0))
    part = pl.BlockSpec((slots, tile), lambda j: (0, j))
    return pl.pallas_call(
        kernel,
        grid=(tiles,),
        out_shape=[shape((slots, inner))] * n_middle + [shape((slots, width))],
        in_specs=[smem, whole] + [part] * len(middles) + [anywhere] * 4,
        out_specs=[part] * n_middle + [whole],
        scratch_shapes=[
            pltpu.VMEM((tiles, width, tile), bf16),
            pltpu.VMEM((tiles, tile, width), bf16),
            pltpu.VMEM((slots, width), f32),
            pltpu.SemaphoreType.DMA((2, tiles)),
        ],
        compiler_params=params(),
        cost_estimate=cost(us),
        name=name,
    )(mine, tall, *middles, *ups, *downs)


def run_up_grad(buf_a, buf_b, dpre_a, dpre_b):
    slots, width = buf_a.shape
    inner = dpre_a.shape[1]
    tile = inner // 6
    whole = pl.BlockSpec((slots, width), lambda j: (0, 0))
    part = pl.BlockSpec((slots, tile), lambda j: (0, j))
    return pl.pallas_call(
        up_grad_kernel,
        grid=(6,),
        out_shape=shape((width, inner), f32),
        in_specs=[whole, whole, part, part],
        out_specs=pl.BlockSpec((width, tile), lambda j: (0, j)),
        compiler_params=params(),
        cost_estimate=cost(10),
        name="up_gradient",
    )(buf_a, buf_b, dpre_a, dpre_b)


def run_down_grad(dout_a, dout_b, act_a, act_b):
    slots, width = dout_a.shape
    inner = act_a.shape[1]
    tile = inner // 6
    whole = pl.BlockSpec((slots, width), lambda j: (0, 0))
    part = pl.BlockSpec((slots, tile), lambda j: (0, j))
    return pl.pallas_call(
        down_grad_kernel,
        grid=(6,),
        out_shape=shape((inner, width), f32),
        in_specs=[whole, whole, part, part],
        out_specs=pl.BlockSpec((tile, width), lambda j: (j, 0)),
        compiler_params=params(),
        cost_estimate=cost(10),
        name="down_gradient",
    )(dout_a, dout_b, act_a, act_b)


def swap(block):
    return lax.ppermute(block, "section", [(0, 1), (1, 0)])


def across(block, bit, devices):
    return lax.ppermute(block, "expert", [(i, i ^ (1 << bit)) for i in range(devices)])


def bit_orders(bits):
    if bits == 4:
        return [(3, 2, 0, 1), (3, 0, 1, 2), (3, 1, 2, 0)]
    names = list(range(bits))
    return [tuple(names[(i + r * bits // pieces) % bits] for i in names) for r in range(pieces)]


def split_lanes(block):
    step = block.shape[-1] // pieces
    return [block[..., p * step : (p + 1) * step] for p in range(pieces)]


def token_of(block):
    value = block[(0,) * block.ndim]
    return (value != value).astype(jnp.int32)


def gathered(shards, device, devices, after):
    bits = devices.bit_length() - 1
    orders = bit_orders(bits)
    rows = shards[0].shape[1]
    if rows % 16:
        found = [p.reshape(p.shape[:1] + (1,) * bits + p.shape[1:]) for p in shards]
        for step in range(bits):
            for p in range(pieces):
                bit = orders[p][step]
                axis = bits - bit
                got = across(found[p], bit, devices)
                high = (device >> bit) & 1 == 1
                found[p] = jnp.where(
                    high,
                    jnp.concatenate([got, found[p]], axis),
                    jnp.concatenate([found[p], got], axis),
                )
        found = [p.reshape(1, p.shape[0], -1, p.shape[-1]) for p in found]
        return [[[0]]] * pieces, False, [*found, *[swap(p) for p in found]]
    me = device.astype(jnp.int32).reshape(1)
    found = [p[None] for p in shards]
    differ = [[0] for _ in shards]
    for step in range(bits - 1):
        gots = [across(found[p], orders[p][step], devices) for p in range(pieces)]
        outs = [shape((2 * p.shape[0],) + p.shape[1:]) for p in found]
        last = after if step == bits - 2 else ()
        found = run(join_kernel, "join", 3, [*found, *gots], outs, [], me, (), last)[1:]
        for p in range(pieces):
            differ[p] = differ[p] + [d ^ (1 << orders[p][step]) for d in differ[p]]
    far = [across(found[p], orders[p][-1], devices) for p in range(pieces)]
    layout = [
        [differ[p], [d ^ (1 << orders[p][-1]) for d in differ[p]]] for p in range(pieces)
    ]
    near_other = [swap(p) for p in found]
    far_other = [swap(p) for p in far]
    arrays = []
    for near, distant in ((found, far), (near_other, far_other)):
        for p in range(pieces):
            arrays += [near[p], distant[p]]
    return layout, True, arrays


def halved(block, bit, bits, lead, device, devices, late=0):
    axis = lead + bits - 1 - bit
    low = lax.index_in_dim(block, 0, axis, keepdims=True)
    high = lax.index_in_dim(block, 1, axis, keepdims=True)
    got = across(jnp.where((device >> bit) & 1 == 1, low, high), bit, devices)
    up = ((device + late) >> bit) & 1 == 1
    return jnp.where(up, high, low).astype(f32) + got.astype(f32)


def folded(found, step, device, devices, late=0):
    bits = devices.bit_length() - 1
    orders = [order[::-1] for order in bit_orders(bits)]
    results = []
    for p in range(pieces):
        value = halved(found[p], orders[p][step], bits, 1, device, devices, late)
        results.append(value if step == bits - 1 else value.astype(bf16))
    return results


def unfolded(total, devices):
    bits = devices.bit_length() - 1
    return [
        p.reshape(p.shape[:1] + (2,) * bits + (p.shape[1] // devices, p.shape[2]))
        for p in split_lanes(total)
    ]


def body(
    block_input,
    cotangent,
    lengths,
    routes,
    norm_gain,
    attention_in,
    attention_out,
    position_bias,
    router,
    expert_up,
    expert_down,
):
    _, rows, width = block_input.shape
    section = lax.axis_index("section")
    device = lax.axis_index("expert")
    devices = lax.axis_size("expert")
    bits = devices.bit_length() - 1
    first = section == 0
    mine = [(section == which).astype(jnp.int32).reshape(1) for which in range(2)]
    experts = router.shape[2]
    shard_rows = router.shape[1]
    buckets, heads = position_bias.shape[1:]
    capacity = max(2, 3 * rows // (2 * experts))
    capacity = -(-capacity // 8) * 8
    slots = experts * capacity

    def both(own, other):
        return (jnp.where(first, own, other), jnp.where(first, other, own))

    def own_micro(block):
        return jnp.where(first, block[0], block[1])

    def other_micro(block):
        return jnp.where(first, block[1], block[0])

    own_shards = jnp.concatenate([attention_in[0], attention_out], axis=0)
    cut = split_lanes(own_shards)
    pad = cut[0].shape[-1] - experts
    cut[0] = jnp.concatenate([cut[0], jnp.pad(router, ((0, 0), (0, 0), (0, pad)))], axis=0)
    small_parts = (
        norm_gain[0].reshape(-1),
        position_bias[0].reshape(-1),
        other_micro(routes[0])[:, 0].astype(f32),
    )
    small = jnp.concatenate(small_parts)
    small = jnp.pad(small, (0, -small.shape[0] % 128)).reshape(-1, 128)
    small_given = swap(small).reshape(-1)
    split_at, at = [], 0
    for part in small_parts:
        at += part.shape[0]
        split_at.append(at)
    gain_other, table_other, route_other, _ = jnp.split(small_given, split_at)
    gains = both(norm_gain[0], gain_other.reshape(2, width))
    tables = both(position_bias[0], table_other.reshape(buckets, heads))
    route_pair = both(own_micro(routes[0])[:, 0], route_other.astype(jnp.int32))

    positions = jnp.arange(rows, dtype=jnp.int32)
    bounds = jnp.cumsum(own_micro(lengths)[0])
    segment = jnp.sum((positions[:, None] >= bounds[None, :]).astype(jnp.int32), axis=1)
    seg_col, seg_row = segment[:, None], segment[None, :]
    offsets = jnp.arange(2 * rows, dtype=jnp.int32) - (rows - 1)
    bucket_hot = (
        bucket_of(offsets)[:, None] == jnp.arange(buckets, dtype=jnp.int32)[None, :]
    ).astype(f32)
    lines = [
        lax.dot_general(table, bucket_hot, (((0,), (1,)), ((), ())), precision=highest)
        for table in tables
    ]
    bases = [run_bias(line, rows) for line in lines]
    before = (positions[:, None] > positions[None, :]).astype(bf16)
    places = []
    for route in route_pair:
        chosen = route[:, None] == jnp.arange(experts, dtype=jnp.int32)[None, :]
        earlier = dot(before, chosen.astype(bf16))
        slot = jnp.sum(jnp.where(chosen, earlier, 0.0), axis=1).astype(jnp.int32)
        places.append(route * capacity + slot)
    route_cols = [route[:, None] for route in route_pair]
    place_cols = [place[:, None] for place in places]
    place_rows = [place[None, :] for place in places]
    layout, apart, weights = gathered(
        cut, device, devices, (*bases, *place_rows, *place_cols, *route_cols, seg_col, seg_row, *gains)
    )
    core = jnp.stack([section, device if apart else jnp.zeros_like(device)]).astype(jnp.int32)
    up_other = swap(expert_up[0, 0])
    down_other = swap(expert_down[0, 0])
    ups, downs = (expert_up[0, 0], up_other), (expert_down[0, 0], down_other)

    def exchanged(block):
        return lax.all_to_all(block, "expert", split_axis=0, concat_axis=0, tiled=True)

    def expert_forward(which, arrived):
        return run_expert(
            expert_forward_kernel, mine[which], arrived, (), ups, downs, 2, 11, "expert_forward"
        )

    def expert_backward(mine, arrived, slope):
        return run_expert(
            expert_backward_kernel, mine, arrived, (slope,), ups, downs, 1, 11,
            "expert_backward",
        )

    def shared_inputs(which):
        return (
            gains[which], bases[which], seg_col, seg_row, route_cols[which],
        )

    inputs = own_micro(block_input)
    cot = own_micro(cotangent)
    token, q0, k0, v0, o0, p0, mid0, h20, share0, gate0, send0 = run_forward(
        False, layout, core, weights, (inputs, *shared_inputs(0), place_rows[0]), slots, experts,
        heads, (),
    )
    buf0 = exchanged(send0)
    act0, slope0, result0 = expert_forward(0, buf0)
    back0 = exchanged(result0)
    _, q1, k1, v1, o1, p1, mid1, h21, share1, gate1, send1, between, combined0, grad_send1 = (
        run_forward(
            True, layout, core, weights,
            (mid0, gate0, place_cols[0], back0, cot, *shared_inputs(1), place_rows[1]),
            slots, experts, heads, (),
        )
    )
    buf1 = exchanged(send1)
    dout1 = exchanged(grad_send1)
    act1, slope1, result1 = expert_forward(1, buf1)
    dpre1, dbuf1 = expert_backward(mine[1], dout1, slope1)
    back1 = exchanged(
        jnp.concatenate(
            [block.reshape(experts, capacity, width) for block in (result1, dbuf1)], axis=1
        ).reshape(2 * slots, width)
    )
    place_out = place_cols[1] + route_cols[1] * capacity
    _, dx11, low1, dq1, dk1, dv1, router_grad1, gain_two1, line_grad1, last = run_heads_backward(
        True, layout, core, weights,
        (q1, k1, v1, p1, mid1, h21, share1, gate1, cot, back1, place_out, gains[1],
         route_cols[1], place_out + capacity),
        experts, (),
    )
    token, dx1, gain_one1, dy0, grad_send0 = run_input_backward(
        True, layout, core, weights,
        (between, dx11, dq1, dk1, dv1, gains[1], gate0, place_rows[0]), slots, (),
    )
    token, keep1, give1 = run_weight_backward(
        core + token[0], (between, gains[1], o1, low1, dq1, dk1, dv1), ()
    )
    dout0 = exchanged(grad_send0)

    given1 = swap(give1)
    dpre0, dbuf0 = expert_backward(mine[0] + token[0], dout0, slope0)
    dback0 = exchanged(dbuf0)
    from_first = [swap(block) for block in (buf1, act1, dout1, dpre1)]
    from_second = [swap(block) for block in (buf0, act0, dout0, dpre0)]

    def up_of(bufs, dpres):
        return run_up_grad(*bufs, *dpres)

    def down_of(douts, acts):
        return run_down_grad(*douts, *acts)

    up_sets = ((buf0, from_second[0], dpre0, from_second[3]), (buf1, from_first[0], dpre1, from_first[3]))
    down_sets = ((dout0, from_second[2], act0, from_second[1]), (dout1, from_first[2], act1, from_first[1]))

    def own_layer(run_grad, sets, token):
        return lax.cond(
            section + token == 0, lambda a, b: run_grad(*a), lambda a, b: run_grad(*b), *sets
        )

    grads = [
        functools.partial(own_layer, run_down_grad, down_sets),
        functools.partial(own_layer, run_up_grad, up_sets),
    ]

    grad_down = grads[0](token_of(dbuf0))
    token, dx10, low0, dq0, dk0, dv0, router_grad0, gain_two0, line_grad0 = run_heads_backward(
        False, layout, core, weights,
        (q0, k0, v0, p0, mid0, h20, share0, gate0, dy0, dback0, combined0, gains[0],
         route_cols[0], place_cols[0]),
        experts, (grad_down,),
    )
    token, keep0, give0 = run_weight_backward(
        core, (inputs, gains[0], o0, low0, dq0, dk0, dv0), ()
    )
    _, dx0, gain_one0 = run_input_backward(
        False, layout, core + token[0], weights, (inputs, dx10, dq0, dk0, dv0, gains[0]), slots, ()
    )

    little = [
        jnp.concatenate(parts, axis=0)
        for parts in (
            (gain_one0, gain_two0, line_grad0, router_grad0),
            (gain_one1, gain_two1, line_grad1, router_grad1),
        )
    ]
    little = jnp.where(first, little[0], little[1]) + swap(jnp.where(first, little[1], little[0]))
    sums, little_sum, (grad_up,) = summed_blocks(
        [keep0, swap(give0), keep1, given1], little, device, devices, grads[1:], (dx0,)
    )
    shared0, shared1 = sums[:2], sums[2:]
    shared_other = swap(jnp.where(first, shared1, shared0))
    queries_keys = jnp.where(first, shared0, shared_other)
    values_out = jnp.where(first, shared_other, shared1)

    grad_table = jnp.dot(little_sum[2 : 2 + heads], bucket_hot, precision=highest).T
    router_sum = lax.dynamic_slice_in_dim(little_sum[2 + heads :], device * shard_rows, shard_rows, 1)

    out_other = swap(jnp.where(first, last, between))
    layer_out = jnp.stack(
        [jnp.where(first, between, out_other), jnp.where(first, out_other, last)]
    )
    grad_other = swap(jnp.where(first, dx1, dx0))
    input_grad = jnp.stack([jnp.where(first, dx0, grad_other), jnp.where(first, grad_other, dx1)])
    return (
        layer_out[None],
        input_grad[None],
        little_sum[:2][None],
        jnp.concatenate([queries_keys, values_out[:1]], axis=0)[None],
        values_out[1][None],
        grad_table[None],
        router_sum.T[None],
        grad_up[None, None],
        grad_down[None, None],
    )


def solution(mesh):
    in_specs = (
        P(None, "expert", None),
        P(None, "expert", None),
        P(None, "expert", None),
        P("section", None, "expert", None),
        P("section", None, None),
        P("section", None, "expert", None),
        P("section", "expert", None),
        P("section", None, None),
        P("section", "expert", None),
        P("section", "expert", None, None),
        P("section", "expert", None, None),
    )
    out_specs = (
        P("section", None, "expert", None),
        P("section", None, "expert", None),
        P("section", None, None),
        P("section", None, "expert", None),
        P("section", "expert", None),
        P("section", None, None),
        P("section", "expert", None),
        P("section", "expert", None, None),
        P("section", "expert", None, None),
    )
    return jax.shard_map(body, mesh=mesh, in_specs=in_specs, out_specs=out_specs, check_vma=False)
```

time: 589 us -> 560 us (0.951)
  starting transfers between devices: 131 us -> 66.8 us
  waiting for transfers between devices: 189 us -> 135 us
  blocking collectives: 31.3 us -> 80.3 us
  Pallas kernels: 182 us -> 219 us
    ppermute x60 -> x28, waiting for transfers between devices: 145 us -> 55.1 us  [across(): lax.ppermute(block, 'expert', [(i, i ^ 1 << bit) for i in range(devices)])]
    all_to_all x1 -> x2, blocking collectives: 31.3 us -> 80.3 us  [exchanged(): lax.all_to_all(block, 'expert', split_axis=0, concat_axis=0, tiled=True)]
    pallas_call x4 -> x18, Pallas kernels: 102 us -> 140 us  [the longest x16 131 us: run(): pl.pallas_call(marked, out_shape=outs, in_specs=[smem] + [anywhere] * len...]
    ppermute x60 -> x28, starting transfers between devices: 70.4 us -> 36.2 us  [across(): lax.ppermute(block, 'expert', [(i, i ^ 1 << bit) for i in range(devices)])]
    all_to_all x7 -> x5, waiting for transfers between devices: 39.3 us -> 64.3 us  [exchanged(): lax.all_to_all(block, 'expert', split_axis=0, concat_axis=0, tiled=True)]
    ppermute x8 -> x0, starting transfers between devices: 19.7 us -> none  [moved(): return lax.ppermute(block, 'section', [(source, 1 - source)])]
    all_to_all x7 -> x5, starting transfers between devices: 38.2 us -> 23.9 us  [exchanged(): lax.all_to_all(block, 'expert', split_axis=0, concat_axis=0, tiled=True)]
    ppermute x17 -> x23, waiting for transfers between devices: 4.96 us -> 15.8 us  [swap(): return lax.ppermute(block, 'section', [(0, 1), (1, 0)])]
  transfers between devices with their start and end apart: 92 -> 56, of which waited for: 38 -> 27; matrix products, arithmetic and copies ran while one was open for 6% -> 5% of each run, Pallas kernels for 28% -> 25%
where the time goes in v2:
time: 560 us; the launch traced here: 551 us
  Pallas kernels  219 us (39%)
  waiting for transfers between devices  135 us (24%)
  blocking collectives  80.3 us (14%)
  starting transfers between devices  66.8 us (12%)
  other arithmetic  21.9 us (4%)
  local copies, waits for them, and re-layouts  17.6 us (3%)
  between operations  7.06 us (1%)
    pallas_call x16, Pallas kernels, run(): pl.pallas_call(marked, out_shape=outs, in_specs=[smem] + [anywhere] * len...  131 us
    all_to_all x2, blocking collectives, exchanged(): lax.all_to_all(block, 'expert', split_axis=0, concat_axis=0, tiled=True)  80.3 us
    all_to_all x5, waiting for transfers between devices, exchanged(): lax.all_to_all(block, 'expert', split_axis=0, concat_axis=0, tiled=True)  64.3 us
    ppermute x28, waiting for transfers between devices, across(): lax.ppermute(block, 'expert', [(i, i ^ 1 << bit) for i in range(devices)])  55.1 us
    pallas_call x4, Pallas kernels, run_expert(): pl.pallas_call(kernel, grid=(tiles,), out_shape=[shape((slots, inner))] *...  53.6 us
    ppermute x28, starting transfers between devices, across(): lax.ppermute(block, 'expert', [(i, i ^ 1 << bit) for i in range(devices)])  36.2 us
    all_to_all x5, starting transfers between devices, exchanged(): lax.all_to_all(block, 'expert', split_axis=0, concat_axis=0, tiled=True)  23.9 us
    ppermute x23, waiting for transfers between devices, swap(): return lax.ppermute(block, 'section', [(0, 1), (1, 0)])  15.8 us
  transfers between devices with their start and end apart: 56, of which 27 were waited for; matrix products, arithmetic and copies ran while one was open for 5% of the time, Pallas kernels for 25%

profile of v2, /device:TPU:0, one launch (start us, length us, event | category | flops | bytes accessed | tf_op | source)
XLA Modules:
  0.0 550.6 jit_solution(2957899760303365978)
XLA Ops:
  16.3 4.8 bias_base.2.refs_6_.refs_14_
  45.1 4.8 bias_base.3.refs_7_.refs_18_
  61.4 14.9 %collective-permute-done.11.refs_3_ = bf16[8,4,48,256]{3,2,1,0:T(8,128)(2,1)S(1)} collective-permute-done((bf16[8,4,48,256]{3,2,1,0:T(8,128)(2,1)}, bf16[8,4,48,256]{3,2,1,0:T(8,128)(2,1)S(1)}, u32[]{:S(2)}, u32[]{:S(2)}) %collective-permute-start.11) | collective-permute-done | bytes 786464 | tf_op jit(solution)/shard_map/ppermute | solution.py:732
  77.0 7.3 %collective-permute-done.10.refs_1_ = bf16[8,5,48,256]{3,2,1,0:T(8,128)(2,1)S(1)} collective-permute-done((bf16[8,5,48,256]{3,2,1,0:T(8,128)(2,1)}, bf16[8,5,48,256]{3,2,1,0:T(8,128)(2,1)S(1)}, u32[]{:S(2)}, u32[]{:S(2)}) %collective-permute-start.10) | collective-permute-done | bytes 983072 | tf_op jit(solution)/shard_map/ppermute | solution.py:732
  86.6 8.0 %collective-permute-done.16.refs_9_ = bf16[8,4,48,256]{3,2,1,0:T(8,128)(2,1)S(1)} collective-permute-done((bf16[8,4,48,256]{3,2,1,0:T(8,128)(2,1)S(1)}, bf16[8,4,48,256]{3,2,1,0:T(8,128)(2,1)S(1)}, u32[]{:S(2)}, u32[]{:S(2)}) %collective-permute-start.16) | collective-permute-done | bytes 786464 | tf_op jit(solution)/shard_map/ppermute | solution.py:728
  97.7 15.8 %attention_forward.2 = (s32[1]{0:T(128)}, bf16[384,768]{1,0:T(8,128)(2,1)}, bf16[384,768]{1,0:T(8,128)(2,1)}, bf16[384,768]{1,0:T(8,128)(2,1)}, bf16[384,768]{1,...) custom-call(s32[2]{0:T(128)} %pad_add_fusion.core_ref, ...), custom_call_target="tpu_custom_call" | custom-call | flops 15000000512 | tf_op jit(solution)/shard_map/attention_forward/pallas_call | solution.py:531
  117.1 23.4 %all-to-all-done = bf16[16,40,768]{2,1,0:T(8,128)(2,1)S(1)} async-done(((bf16[16,40,768]{2,1,0:T(8,128)(2,1)}), bf16[16,40,768]{2,1,0:T(8,128)(2,1)S(1)}, u32[]{:S(2)}, u32[]{:S(2)}) %all-to-all-start) | async-done | bytes 983072 | tf_op jit(solution)/shard_map/all_to_all | solution.py:910
  140.6 13.9 %expert_forward.2 = (bf16[640,3072]{1,0:T(8,128)(2,1)}, bf16[640,3072]{1,0:T(8,128)(2,1)}, bf16[640,768]{1,0:T(8,128)(2,1)}) custom-call(s32[1]{0:T(128)} %bitcast.15.mine_ref, bf16[640,768]{1,0:T(8,128)(2,1)S(1)} %bitcast.100, bf16[768,3072]{1,0:T(8,128)(2,1)} %bitcast.18.up_own, bf16[768,3072]{1,0:T(8,128)(2,1)} %collective-permute-done.19.up_other, ...), custom_call_target="tpu_custom_call" | custom-call | flops 11000000512 | tf_op jit(solution)/shard_map/expert_forward/pallas_call | solution.py:673
  154.5 7.0 %all-to-all-start.1 = ((bf16[16,40,768]{2,1,0:T(8,128)(2,1)}), bf16[16,40,768]{2,1,0:T(8,128)(2,1)S(1)}, u32[]{:S(2)}, u32[]{:S(2)}) async-start(bf16[16,40,768]{2,1,0:T(8,128)(2,1)} %bitcast.115), calls=%async_computation.1 | async-start | bytes 1966080 | tf_op jit(solution)/shard_map/all_to_all | solution.py:910
  162.4 21.5 %all-to-all-done.1 = bf16[16,40,768]{2,1,0:T(8,128)(2,1)S(1)} async-done(((bf16[16,40,768]{2,1,0:T(8,128)(2,1)}), bf16[16,40,768]{2,1,0:T(8,128)(2,1)S(1)}, u32[]{:S(2)}, u32[]{:S(2)}) %all-to-all-start.1) | async-done | bytes 983072 | tf_op jit(solution)/shard_map/all_to_all | solution.py:910
  184.9 17.8 %attention_forward.3 = (s32[1]{0:T(128)}, bf16[384,768]{1,0:T(8,128)(2,1)}, bf16[384,768]{1,0:T(8,128)(2,1)}, bf16[384,768]{1,0:T(8,128)(2,1)}, bf16[384,768]{1,...) custom-call(s32[2]{0:T(128)} %pad_add_fusion.core_ref, ...), custom_call_target="tpu_custom_call" | custom-call | flops 15000000512 | tf_op jit(solution)/shard_map/attention_forward/pallas_call | solution.py:531
  202.7 29.5 %all_to_all.74 = bf16[16,40,768]{2,1,0:T(8,128)(2,1)} all-to-all(bf16[16,40,768]{2,1,0:T(8,128)(2,1)} %bitcast.113), channel_id=1, replica_groups=mesh['section'=2,'expert'=16] {'expert'}, dimensions={0} | all-to-all | bytes 1966080 | tf_op jit(solution)/shard_map/all_to_all | solution.py:910
  236.0 14.9 %expert_forward.3 = (bf16[640,3072]{1,0:T(8,128)(2,1)}, bf16[640,3072]{1,0:T(8,128)(2,1)}, bf16[640,768]{1,0:T(8,128)(2,1)}) custom-call(s32[1]{0:T(128)} %bitcast.23.mine_ref, bf16[640,768]{1,0:T(8,128)(2,1)} %bitcast.25.x_ref, bf16[768,3072]{1,0:T(8,128)(2,1)} %bitcast.18.up_own, bf16[768,3072]{1,0:T(8,128)(2,1)} %collective-permute-done.19.up_other, ...), custom_call_target="tpu_custom_call" | custom-call | flops 11000000512 | tf_op jit(solution)/shard_map/expert_forward/pallas_call | solution.py:673
  250.9 6.8 %all-to-all-done.3 = bf16[16,40,768]{2,1,0:T(8,128)(2,1)S(1)} async-done(((bf16[16,40,768]{2,1,0:T(8,128)(2,1)}), bf16[16,40,768]{2,1,0:T(8,128)(2,1)S(1)}, u32[]{:S(2)}, u32[]{:S(2)}) %all-to-all-start.3) | async-done | bytes 983072 | tf_op jit(solution)/shard_map/all_to_all | solution.py:910
  257.7 12.5 %expert_backward.2 = (bf16[640,3072]{1,0:T(8,128)(2,1)}, bf16[640,768]{1,0:T(8,128)(2,1)}) custom-call(s32[1]{0:T(128)} %bitcast.23.mine_ref, bf16[640,768]{1,0:T(8,128)(2,1)S(1)} %bitcast.103, bf16[640,3072]{1,0:T(8,128)(2,1)} %get-tuple-element.189.slope_ref, bf16[768,3072]{1,0:T(8,128)(2,1)} %bitcast.18.up_own, ...), custom_call_target="tpu_custom_call" | custom-call | flops 11000000512 | tf_op jit(solution)/shard_map/expert_backward/pallas_call | solution.py:673
  271.5 50.8 %all_to_all.75 = bf16[16,80,768]{2,1,0:T(8,128)(2,1)} all-to-all(bf16[16,80,768]{2,1,0:T(8,128)(2,1)S(1)} %pad_maximum_fusion), channel_id=1, replica_groups=mesh['section'=2,'expert'=16] {'expert'}, dimensions={0} | all-to-all | bytes 3932160 | tf_op jit(solution)/shard_map/all_to_all | solution.py:910
  322.3 20.1 %heads_backward.2 = (s32[1]{0:T(128)}, f32[384,768]{1,0:T(8,128)}, bf16[384,768]{1,0:T(8,128)(2,1)}, bf16[384,768]{1,0:T(8,128)(2,1)}, bf16[384,768]{1,0:T(8,128...) custom-call(s32[2]{0:T(128)} %pad_add_fusion.core_ref, ...), custom_call_target="tpu_custom_call" | custom-call | flops 20000000000 | tf_op jit(solution)/shard_map/heads_backward/pallas_call | solution.py:531
  342.4 8.9 %input_backward.2 = (s32[1]{0:T(128)}, f32[384,768]{1,0:T(8,128)}, f32[1,768]{1,0:T(1,128)}, bf16[384,768]{1,0:T(8,128)(2,1)}, bf16[640,768]{1,0:T(8,128)(2,1)}) custom-call(s32[2]{0:T(128)} %pad_add_fusion.core_ref, bf16[8,5,48,256]{3,2,1,0:T(8,128)(2,1)} %get-tuple-element.170.refs_0_, bf16[8,5,48,256]{3,2,1,0:T(8,128)(2,1)} %copy-done.30, ...), custom_call_target="tpu_custom_call" | custom-call | flops 6000000000 | tf_op jit(solution)/shard_map/input_backward/pallas_call | solution.py:531
  356.8 8.9 %weight_backward.2 = (s32[1]{0:T(128)}, bf16[2,768,768]{2,1,0:T(8,128)(2,1)}, bf16[2,768,768]{2,1,0:T(8,128)(2,1)}) custom-call(s32[2]{0:T(128)} %broadcast_add_fusion.2.core_ref, bf16[384,768]{1,0:T(8,128)(2,1)} %get-tuple-element.177.refs_12_.refs_0_, f32[2,768]{1,0:T(2,128)} %get-tuple-element.325.refs_17_.refs_23_.refs_1_, ...), custom_call_target="tpu_custom_call" | custom-call | flops 6000000000 | tf_op jit(solution)/shard_map/weight_backward/pallas_call | solution.py:531
  366.3 10.4 %all-to-all-done.5 = bf16[16,40,768]{2,1,0:T(8,128)(2,1)S(1)} async-done(((bf16[16,40,768]{2,1,0:T(8,128)(2,1)}), bf16[16,40,768]{2,1,0:T(8,128)(2,1)S(1)}, u32[]{:S(2)}, u32[]{:S(2)}) %all-to-all-start.5) | async-done | bytes 983072 | tf_op jit(solution)/shard_map/all_to_all | solution.py:910
  376.7 12.3 %expert_backward.3 = (bf16[640,3072]{1,0:T(8,128)(2,1)}, bf16[640,768]{1,0:T(8,128)(2,1)}) custom-call(s32[1]{0:T(128)S(6)} %add.242.mine_ref, bf16[640,768]{1,0:T(8,128)(2,1)S(1)} %bitcast.106, bf16[640,3072]{1,0:T(8,128)(2,1)} %get-tuple-element.209.slope_ref, bf16[768,3072]{1,0:T(8,128)(2,1)} %bitcast.18.up_own, ...), custom_call_target="tpu_custom_call" | custom-call | flops 11000000512 | tf_op jit(solution)/shard_map/expert_backward/pallas_call | solution.py:673
  388.9 5.9 %all-to-all-start.6 = ((bf16[16,40,768]{2,1,0:T(8,128)(2,1)}), bf16[16,40,768]{2,1,0:T(8,128)(2,1)}, u32[]{:S(2)}, u32[]{:S(2)}) async-start(bf16[16,40,768]{2,1,0:T(8,128)(2,1)} %bitcast.109), calls=%async_computation.6 | async-start | bytes 1966080 | tf_op jit(solution)/shard_map/all_to_all | solution.py:910
  402.1 12.4 %conditional.2 = (f32[3072,768]{1,0:T(8,128)}) conditional(s32[]{:T(128)} %convert_element_type.247, (bf16[640,768]{1,0:T(8,128)(2,1)S(1)}, bf16[640,768]{1,0:T(8,128)(2,1)}, bf16[640,3072]{1,0:T(8,128)(2,1)}, bf16[640,3072]{1,0:T(8,128)(2,1)}) %tuple.53, (bf16[640,768]{1,0:T(8,128)(2,1)S(1)}, bf16[640,768]{1,0:T(8,128)(2,1)}, ...), branch_computations={%region_4.5_spmd, %region_5.6_spmd} | conditional | flops 10000000000 | bytes 8 | solution.py:985
  402.1 12.4 %down_gradient.3 = f32[3072,768]{1,0:T(8,128)} custom-call(bf16[640,768]{1,0:T(8,128)(2,1)S(1)} %get-tuple-element.42.dout_a, bf16[640,768]{1,0:T(8,128)(2,1)} %get-tuple-element.43.dout_b, bf16[640,3072]{1,0:T(8,128)(2,1)} %get-tuple-element.44.act_a, bf16[640,3072]{1,0:T(8,128)(2,1)} %get-tuple-element.45.act_b), custom_call_target="tpu_custom_call" | custom-call | flops 10000000000 | tf_op jit(solution)/shard_map/cond/branch_1_fun/down_gradient/pallas_call | solution.py:715
  416.7 17.3 %heads_backward.3 = (s32[1]{0:T(128)}, f32[384,768]{1,0:T(8,128)}, bf16[384,768]{1,0:T(8,128)(2,1)}, bf16[384,768]{1,0:T(8,128)(2,1)}, bf16[384,768]{1,0:T(8,128...) custom-call(s32[2]{0:T(128)} %pad_add_fusion.core_ref, ...), custom_call_target="tpu_custom_call" | custom-call | flops 20000000000 | tf_op jit(solution)/shard_map/heads_backward/pallas_call | solution.py:531
  434.0 9.1 %weight_backward.3 = (s32[1]{0:T(128)}, bf16[2,768,768]{2,1,0:T(8,128)(2,1)}, bf16[2,768,768]{2,1,0:T(8,128)(2,1)}) custom-call(s32[2]{0:T(128)} %pad_add_fusion.core_ref, bf16[384,768]{1,0:T(8,128)(2,1)} %select_bitcast_fusion.5.refs_12_.refs_0_, f32[2,768]{1,0:T(2,128)} %get-tuple-element.326.refs_16_.refs_13_.refs_23_.refs_1_.refs_17_, ...), custom_call_target="tpu_custom_call" | custom-call | flops 6000000000 | tf_op jit(solution)/shard_map/weight_backward/pallas_call | solution.py:531
  449.1 7.6 %input_backward.3 = (s32[1]{0:T(128)}, f32[384,768]{1,0:T(8,128)}, f32[1,768]{1,0:T(1,128)}) custom-call(s32[2]{0:T(128)} %broadcast_add_fusion.1.core_ref, bf16[8,5,48,256]{3,2,1,0:T(8,128)(2,1)} %get-tuple-element.170.refs_0_, bf16[8,5,48,256]{3,2,1,0:T(8,128)(2,1)} %copy-done.30, bf16[8,4,48,256]{3,2,1,0:T(8,128)(2,1)} %get-tuple-element.171.refs_2_, ...), custom_call_target="tpu_custom_call" | custom-call | flops 6000000000 | tf_op jit(solution)/shard_map/input_backward/pallas_call | solution.py:531
  459.7 6.9 %fold_first.1 = (s32[1]{0:T(128)}, bf16[4,8,48,256]{3,2,1,0:T(8,128)(2,1)}, bf16[4,8,48,256]{3,2,1,0:T(8,128)(2,1)}, bf16[4,8,48,256]{3,2,1,0:T(8,128)(2,1)}, bf...) custom-call(s32[1]{0:T(128)} %bitcast.1.core_ref, ...), custom_call_target="tpu_custom_call" | custom-call | flops 4000000000 | tf_op jit(solution)/shard_map/fold_first/pallas_call | solution.py:531
  478.2 12.4 %conditional.3 = (f32[768,3072]{1,0:T(8,128)}) conditional(s32[]{:T(128)} %convert_element_type.249, (bf16[640,768]{1,0:T(8,128)(2,1)}, bf16[640,768]{1,0:T(8,128)(2,1)}, bf16[640,3072]{1,0:T(8,128)(2,1)}, bf16[640,3072]{1,0:T(8,128)(2,1)}) %tuple.22, (bf16[640,768]{1,0:T(8,128)(2,1)S(1)}, bf16[640,768]{1,0:T(8,128)(2,1)}, ...), branch_computations={%region_6.7_spmd, %region_7.8_spmd} | conditional | flops 10000000000 | bytes 8 | solution.py:985
  478.2 12.4 %up_gradient.3 = f32[768,3072]{1,0:T(8,128)} custom-call(bf16[640,768]{1,0:T(8,128)(2,1)S(1)} %get-tuple-element.50.buf_a, bf16[640,768]{1,0:T(8,128)(2,1)} %get-tuple-element.51.buf_b, bf16[640,3072]{1,0:T(8,128)(2,1)} %get-tuple-element.52.dpre_a, bf16[640,3072]{1,0:T(8,128)(2,1)} %get-tuple-element.53.dpre_b), custom_call_target="tpu_custom_call" | custom-call | flops 10000000000 | tf_op jit(solution)/shard_map/cond/branch_1_fun/up_gradient/pallas_call | solution.py:697
  499.9 7.5 %collective-permute-done.39.refs_3_ = bf16[4,4,48,256]{3,2,1,0:T(8,128)(2,1)S(1)} collective-permute-done((bf16[4,4,48,256]{3,2,1,0:T(8,128)(2,1)}, bf16[4,4,48,256]{3,2,1,0:T(8,128)(2,1)S(1)}, u32[]{:S(2)}, u32[]{:S(2)}) %collective-permute-start.39) | collective-permute-done | bytes 393248 | tf_op jit(solution)/shard_map/ppermute | solution.py:732
  531.6 6.1 %collective-permute-done.46 = f32[30,768]{1,0:T(8,128)S(1)} collective-permute-done((f32[30,768]{1,0:T(8,128)S(1)}, f32[30,768]{1,0:T(8,128)S(1)}, u32[]{:S(2)}, u32[]{:S(2)}) %collective-permute-start.46) | collective-permute-done | bytes 92192 | tf_op jit(solution)/shard_map/ppermute | solution.py:732
  (287 shorter events, 144.0 us)
Async XLA Ops:
  2.5 21.7 %collective-permute-start = (bf16[1,5,48,256]{3,2,1,0:T(8,128)(2,1)S(1)}, bf16[1,5,48,256]{3,2,1,0:T(8,128)(2,1)S(1)}, u32[]{:S(2)}, u32[]{:S(2)}) collective-permute-start(bf16[1,5,48,256]{3,2,1,0:T(8,128)(2,1)S(1)} %fusion.9.refs_0_), channel_id=1, source_target_pairs={{0,8},{1,9},{2,10},{3,11},{4,12},{5,13},{6,14},{7,15},{8,0},{9,1},... | collective-permute-start | bytes 368648 | tf_op jit(solution)/shard_map/ppermute | solution.py:732
  6.6 17.6 %collective-permute-start.1 = (bf16[1,4,48,256]{3,2,1,0:T(8,128)(2,1)S(1)}, bf16[1,4,48,256]{3,2,1,0:T(8,128)(2,1)S(1)}, u32[]{:S(2)}, u32[]{:S(2)}) collective-permute-start(bf16[1,4,48,256]{3,2,1,0:T(8,128)(2,1)S(1)} %get-tuple-element.322.refs_1_), channel_id=1, source_target_pairs={{0,8},{1,9},{2,10},{3,11},{4,12},{5,13},{6,14},{7,15},{8,0},{9,1},... | collective-permute-start | bytes 294920 | tf_op jit(solution)/shard_map/ppermute | solution.py:732
  6.7 17.5 %collective-permute-start.2 = (bf16[1,4,48,256]{3,2,1,0:T(8,128)(2,1)S(1)}, bf16[1,4,48,256]{3,2,1,0:T(8,128)(2,1)S(1)}, u32[]{:S(2)}, u32[]{:S(2)}) collective-permute-start(bf16[1,4,48,256]{3,2,1,0:T(8,128)(2,1)S(1)} %get-tuple-element.320.refs_2_), channel_id=1, source_target_pairs={{0,8},{1,9},{2,10},{3,11},{4,12},{5,13},{6,14},{7,15},{8,0},{9,1},... | collective-permute-start | bytes 294920 | tf_op jit(solution)/shard_map/ppermute | solution.py:732
  41.9 12.5 %collective-permute-start.6 = (bf16[4,5,48,256]{3,2,1,0:T(8,128)(2,1)}, bf16[4,5,48,256]{3,2,1,0:T(8,128)(2,1)S(1)}, u32[]{:S(2)}, u32[]{:S(2)}) collective-permute-start(bf16[4,5,48,256]{3,2,1,0:T(8,128)(2,1)} %get-tuple-element.167.refs_0_), channel_id=1, source_target_pairs={{0,1},{1,0},{2,3},{3,2},{4,5},{5,4},{6,7},{7,6},{8,9},{9,8},{10,11... | collective-permute-start | bytes 1474568 | tf_op jit(solution)/shard_map/ppermute | solution.py:732
  58.5 17.9 %collective-permute-start.11 = (bf16[8,4,48,256]{3,2,1,0:T(8,128)(2,1)}, bf16[8,4,48,256]{3,2,1,0:T(8,128)(2,1)S(1)}, u32[]{:S(2)}, u32[]{:S(2)}) collective-permute-start(bf16[8,4,48,256]{3,2,1,0:T(8,128)(2,1)} %get-tuple-element.171.refs_2_), channel_id=1, source_target_pairs={{0,4},{1,5},{2,6},{3,7},{4,0},{5,1},{6,2},{7,3},{8,12},{9,13},{10,... | collective-permute-start | bytes 2359304 | tf_op jit(solution)/shard_map/ppermute | solution.py:732
  59.0 17.5 %collective-permute-start.12 = (bf16[8,4,48,256]{3,2,1,0:T(8,128)(2,1)}, bf16[8,4,48,256]{3,2,1,0:T(8,128)(2,1)S(1)}, u32[]{:S(2)}, u32[]{:S(2)}) collective-permute-start(bf16[8,4,48,256]{3,2,1,0:T(8,128)(2,1)} %get-tuple-element.172.refs_4_), channel_id=1, source_target_pairs={{0,1},{1,0},{2,3},{3,2},{4,5},{5,4},{6,7},{7,6},{8,9},{9,8},{10,11... | collective-permute-start | bytes 2359304 | tf_op jit(solution)/shard_map/ppermute | solution.py:732
  60.0 16.9 %collective-permute-start.15 = (bf16[8,4,48,256]{3,2,1,0:T(8,128)(2,1)}, bf16[8,4,48,256]{3,2,1,0:T(8,128)(2,1)S(1)}, u32[]{:S(2)}, u32[]{:S(2)}) collective-permute-start(bf16[8,4,48,256]{3,2,1,0:T(8,128)(2,1)} %get-tuple-element.171.refs_2_), channel_id=1, source_target_pairs={{0,16},{16,0},{1,17},{17,1},{2,18},{18,2},{3,19},{19,3},{4,20},{20... | collective-permute-start | bytes 2359304 | tf_op jit(solution)/shard_map/ppermute | solution.py:728
  60.0 24.4 %collective-permute-start.10 = (bf16[8,5,48,256]{3,2,1,0:T(8,128)(2,1)}, bf16[8,5,48,256]{3,2,1,0:T(8,128)(2,1)S(1)}, u32[]{:S(2)}, u32[]{:S(2)}) collective-permute-start(bf16[8,5,48,256]{3,2,1,0:T(8,128)(2,1)} %get-tuple-element.170.refs_0_), channel_id=1, source_target_pairs={{0,2},{1,3},{2,0},{3,1},{4,6},{5,7},{6,4},{7,5},{8,10},{9,11},{10,... | collective-permute-start | bytes 2949128 | tf_op jit(solution)/shard_map/ppermute | solution.py:732
  61.2 23.7 %collective-permute-start.13 = (bf16[8,5,48,256]{3,2,1,0:T(8,128)(2,1)}, bf16[8,5,48,256]{3,2,1,0:T(8,128)(2,1)S(1)}, u32[]{:S(2)}, u32[]{:S(2)}) collective-permute-start(bf16[8,5,48,256]{3,2,1,0:T(8,128)(2,1)} %get-tuple-element.170.refs_0_), channel_id=1, source_target_pairs={{0,16},{16,0},{1,17},{17,1},{2,18},{18,2},{3,19},{19,3},{4,20},{20... | collective-permute-start | bytes 2949128 | tf_op jit(solution)/shard_map/ppermute | solution.py:728
  76.5 64.0 %collective-permute-start.19 = (bf16[768,3072]{1,0:T(8,128)(2,1)}, bf16[768,3072]{1,0:T(8,128)(2,1)}, u32[]{:S(2)}, u32[]{:S(2)}) collective-permute-start(bf16[768,3072]{1,0:T(8,128)(2,1)} %bitcast.18.up_own), channel_id=1, source_target_pairs={{0,16},{16,0},{1,17},{17,1},{2,18},{18,2},{3,19},{19,3},{4,20},{20... | collective-permute-start | bytes 14155784 | tf_op jit(solution)/shard_map/ppermute | solution.py:728
  76.9 63.7 %collective-permute-start.20 = (bf16[3072,768]{1,0:T(8,128)(2,1)}, bf16[3072,768]{1,0:T(8,128)(2,1)}, u32[]{:S(2)}, u32[]{:S(2)}) collective-permute-start(bf16[3072,768]{1,0:T(8,128)(2,1)} %bitcast.19.down_own), channel_id=1, source_target_pairs={{0,16},{16,0},{1,17},{17,1},{2,18},{18,2},{3,19},{19,3},{4,20},{20... | collective-permute-start | bytes 14155784 | tf_op jit(solution)/shard_map/ppermute | solution.py:728
  113.4 27.1 %all-to-all-start = ((bf16[16,40,768]{2,1,0:T(8,128)(2,1)}), bf16[16,40,768]{2,1,0:T(8,128)(2,1)S(1)}, u32[]{:S(2)}, u32[]{:S(2)}) async-start(bf16[16,40,768]{2,1,0:T(8,128)(2,1)} %bitcast.114), calls=%async_computation | async-start | bytes 1966080 | tf_op jit(solution)/shard_map/all_to_all | solution.py:910
  154.5 29.4 %all-to-all-start.1 = ((bf16[16,40,768]{2,1,0:T(8,128)(2,1)}), bf16[16,40,768]{2,1,0:T(8,128)(2,1)S(1)}, u32[]{:S(2)}, u32[]{:S(2)}) async-start(bf16[16,40,768]{2,1,0:T(8,128)(2,1)} %bitcast.115), calls=%async_computation.1 | async-start | bytes 1966080 | tf_op jit(solution)/shard_map/all_to_all | solution.py:910
  232.2 25.5 %all-to-all-start.3 = ((bf16[16,40,768]{2,1,0:T(8,128)(2,1)}), bf16[16,40,768]{2,1,0:T(8,128)(2,1)S(1)}, u32[]{:S(2)}, u32[]{:S(2)}) async-start(bf16[16,40,768]{2,1,0:T(8,128)(2,1)} %bitcast.111), calls=%async_computation.3 | async-start | bytes 1966080 | tf_op jit(solution)/shard_map/all_to_all | solution.py:910
  351.3 25.3 %all-to-all-start.5 = ((bf16[16,40,768]{2,1,0:T(8,128)(2,1)}), bf16[16,40,768]{2,1,0:T(8,128)(2,1)S(1)}, u32[]{:S(2)}, u32[]{:S(2)}) async-start(bf16[16,40,768]{2,1,0:T(8,128)(2,1)} %bitcast.110), calls=%async_computation.5 | async-start | bytes 1966080 | tf_op jit(solution)/shard_map/all_to_all | solution.py:910
  355.0 44.1 %collective-permute-start.23 = (bf16[640,3072]{1,0:T(8,128)(2,1)}, bf16[640,3072]{1,0:T(8,128)(2,1)}, u32[]{:S(2)}, u32[]{:S(2)}) collective-permute-start(bf16[640,3072]{1,0:T(8,128)(2,1)} %get-tuple-element.212), channel_id=1, source_target_pairs={{0,16},{16,0},{1,17},{17,1},{2,18},{18,2},{3,19},{19,3},{4,20},{20... | collective-permute-start | bytes 11796488 | tf_op jit(solution)/shard_map/ppermute | solution.py:728
  355.1 47.0 %collective-permute-start.25 = (bf16[640,3072]{1,0:T(8,128)(2,1)}, bf16[640,3072]{1,0:T(8,128)(2,1)}, u32[]{:S(2)}, u32[]{:S(2)}) collective-permute-start(bf16[640,3072]{1,0:T(8,128)(2,1)} %get-tuple-element.213), channel_id=1, source_target_pairs={{0,16},{16,0},{1,17},{17,1},{2,18},{18,2},{3,19},{19,3},{4,20},{20... | collective-permute-start | bytes 11796488 | tf_op jit(solution)/shard_map/ppermute | solution.py:728
  388.9 27.7 %all-to-all-start.6 = ((bf16[16,40,768]{2,1,0:T(8,128)(2,1)}), bf16[16,40,768]{2,1,0:T(8,128)(2,1)}, u32[]{:S(2)}, u32[]{:S(2)}) async-start(bf16[16,40,768]{2,1,0:T(8,128)(2,1)} %bitcast.109), calls=%async_computation.6 | async-start | bytes 1966080 | tf_op jit(solution)/shard_map/all_to_all | solution.py:910
  395.4 73.3 %collective-permute-start.35 = (bf16[640,3072]{1,0:T(8,128)(2,1)}, bf16[640,3072]{1,0:T(8,128)(2,1)}, u32[]{:S(2)}, u32[]{:S(2)}) collective-permute-start(bf16[640,3072]{1,0:T(8,128)(2,1)} %get-tuple-element.241), channel_id=1, source_target_pairs={{0,16},{16,0},{1,17},{17,1},{2,18},{18,2},{3,19},{19,3},{4,20},{20... | collective-permute-start | bytes 11796488 | tf_op jit(solution)/shard_map/ppermute | solution.py:728
  399.0 57.7 %collective-permute-start.29 = (bf16[2,768,768]{2,1,0:T(8,128)(2,1)}, bf16[2,768,768]{2,1,0:T(8,128)(2,1)}, u32[]{:S(2)}, u32[]{:S(2)}) collective-permute-start(bf16[2,768,768]{2,1,0:T(8,128)(2,1)} %get-tuple-element.233), channel_id=1, source_target_pairs={{0,16},{16,0},{1,17},{17,1},{2,18},{18,2},{3,19},{19,3},{4,20},{20... | collective-permute-start | bytes 7077896 | tf_op jit(solution)/shard_map/ppermute | solution.py:728
  401.6 71.9 %collective-permute-start.37 = (bf16[640,3072]{1,0:T(8,128)(2,1)}, bf16[640,3072]{1,0:T(8,128)(2,1)}, u32[]{:S(2)}, u32[]{:S(2)}) collective-permute-start(bf16[640,3072]{1,0:T(8,128)(2,1)} %get-tuple-element.242), channel_id=1, source_target_pairs={{0,16},{16,0},{1,17},{17,1},{2,18},{18,2},{3,19},{19,3},{4,20},{20... | collective-permute-start | bytes 11796488 | tf_op jit(solution)/shard_map/ppermute | solution.py:728
  443.1 15.1 %collective-permute-start.28 = (bf16[2,768,768]{2,1,0:T(8,128)(2,1)}, bf16[2,768,768]{2,1,0:T(8,128)(2,1)S(1)}, u32[]{:S(2)}, u32[]{:S(2)}) collective-permute-start(bf16[2,768,768]{2,1,0:T(8,128)(2,1)} %get-tuple-element.231), channel_id=1, source_target_pairs={{0,16},{16,0},{1,17},{17,1},{2,18},{18,2},{3,19},{19,3},{4,20},{20... | collective-permute-start | bytes 7077896 | tf_op jit(solution)/shard_map/ppermute | solution.py:728
  448.7 17.9 %collective-permute-start.34 = (bf16[640,768]{1,0:T(8,128)(2,1)}, bf16[640,768]{1,0:T(8,128)(2,1)}, u32[]{:S(2)}, u32[]{:S(2)}) collective-permute-start(bf16[640,768]{1,0:T(8,128)(2,1)} %bitcast.25.x_ref), channel_id=1, source_target_pairs={{0,16},{16,0},{1,17},{17,1},{2,18},{18,2},{3,19},{19,3},{4,20},{20... | collective-permute-start | bytes 2949128 | tf_op jit(solution)/shard_map/ppermute | solution.py:728
  456.7 14.1 %collective-permute-start.21 = (bf16[384,768]{1,0:T(8,128)(2,1)S(1)}, bf16[384,768]{1,0:T(8,128)(2,1)S(1)}, u32[]{:S(2)}, u32[]{:S(2)}) collective-permute-start(bf16[384,768]{1,0:T(8,128)(2,1)S(1)} %broadcast_select_fusion.1), channel_id=1, source_target_pairs={{0,16},{16,0},{1,17},{17,1},{2,18},{18,2},{3,19},{19,3},{4,20},{20... | collective-permute-start | bytes 1769480 | tf_op jit(solution)/shard_map/ppermute | solution.py:728
  458.2 39.5 %collective-permute-start.26 = (f32[384,768]{1,0:T(8,128)}, f32[384,768]{1,0:T(8,128)S(1)}, u32[]{:S(2)}, u32[]{:S(2)}) collective-permute-start(f32[384,768]{1,0:T(8,128)} %broadcast_select_fusion), channel_id=1, source_target_pairs={{0,16},{16,0},{1,17},{17,1},{2,18},{18,2},{3,19},{19,3},{4,20},{20... | collective-permute-start | bytes 3538952 | tf_op jit(solution)/shard_map/ppermute | solution.py:728
  466.7 23.9 %collective-permute-start.31 = (bf16[4,8,48,256]{3,2,1,0:T(8,128)(2,1)}, bf16[4,8,48,256]{3,2,1,0:T(8,128)(2,1)}, u32[]{:S(2)}, u32[]{:S(2)}) collective-permute-start(bf16[4,8,48,256]{3,2,1,0:T(8,128)(2,1)} %get-tuple-element.238), channel_id=1, source_target_pairs={{0,2},{1,3},{2,0},{3,1},{4,6},{5,7},{6,4},{7,5},{8,10},{9,11},{10,... | collective-permute-start | bytes 2359304 | tf_op jit(solution)/shard_map/ppermute | solution.py:732
  468.7 21.9 %collective-permute-start.32 = (bf16[4,8,48,256]{3,2,1,0:T(8,128)(2,1)}, bf16[4,8,48,256]{3,2,1,0:T(8,128)(2,1)}, u32[]{:S(2)}, u32[]{:S(2)}) collective-permute-start(bf16[4,8,48,256]{3,2,1,0:T(8,128)(2,1)} %get-tuple-element.239), channel_id=1, source_target_pairs={{0,4},{1,5},{2,6},{3,7},{4,0},{5,1},{6,2},{7,3},{8,12},{9,13},{10,... | collective-permute-start | bytes 2359304 | tf_op jit(solution)/shard_map/ppermute | solution.py:732
  471.6 20.7 %collective-permute-start.33 = (bf16[4,8,48,256]{3,2,1,0:T(8,128)(2,1)}, bf16[4,8,48,256]{3,2,1,0:T(8,128)(2,1)}, u32[]{:S(2)}, u32[]{:S(2)}) collective-permute-start(bf16[4,8,48,256]{3,2,1,0:T(8,128)(2,1)} %get-tuple-element.240), channel_id=1, source_target_pairs={{0,1},{1,0},{2,3},{3,2},{4,5},{5,4},{6,7},{7,6},{8,9},{9,8},{10,11... | collective-permute-start | bytes 2359304 | tf_op jit(solution)/shard_map/ppermute | solution.py:732
  476.0 22.5 %collective-permute-start.30 = (f32[30,768]{1,0:T(8,128)S(1)}, f32[30,768]{1,0:T(8,128)S(1)}, u32[]{:S(2)}, u32[]{:S(2)}) collective-permute-start(f32[30,768]{1,0:T(8,128)S(1)} %add_add_fusion.3), channel_id=1, source_target_pairs={{0,1},{1,0},{2,3},{3,2},{4,5},{5,4},{6,7},{7,6},{8,9},{9,8},{10,11... | collective-permute-start | bytes 276488 | tf_op jit(solution)/shard_map/ppermute | solution.py:732
  498.6 16.8 %collective-permute-start.38 = (f32[30,768]{1,0:T(8,128)S(1)}, f32[30,768]{1,0:T(8,128)S(1)}, u32[]{:S(2)}, u32[]{:S(2)}) collective-permute-start(f32[30,768]{1,0:T(8,128)S(1)} %add_add_fusion.2), channel_id=1, source_target_pairs={{0,2},{1,3},{2,0},{3,1},{4,6},{5,7},{6,4},{7,5},{8,10},{9,11},{10,... | collective-permute-start | bytes 276488 | tf_op jit(solution)/shard_map/ppermute | solution.py:732
  524.1 13.6 %collective-permute-start.46 = (f32[30,768]{1,0:T(8,128)S(1)}, f32[30,768]{1,0:T(8,128)S(1)}, u32[]{:S(2)}, u32[]{:S(2)}) collective-permute-start(f32[30,768]{1,0:T(8,128)S(1)} %add_add_fusion), channel_id=1, source_target_pairs={{0,8},{1,9},{2,10},{3,11},{4,12},{5,13},{6,14},{7,15},{8,0},{9,1},... | collective-permute-start | bytes 276488 | tf_op jit(solution)/shard_map/ppermute | solution.py:732
  527.2 12.6 %collective-permute-start.47 = (bf16[4,1,48,256]{3,2,1,0:T(8,128)(2,1)S(1)}, bf16[4,1,48,256]{3,2,1,0:T(8,128)(2,1)S(1)}, u32[]{:S(2)}, u32[]{:S(2)}) collective-permute-start(bf16[4,1,48,256]{3,2,1,0:T(8,128)(2,1)S(1)} %copy-done.55), channel_id=1, source_target_pairs={{0,8},{1,9},{2,10},{3,11},{4,12},{5,13},{6,14},{7,15},{8,0},{9,1},... | collective-permute-start | bytes 294920 | tf_op jit(solution)/shard_map/ppermute | solution.py:732
  (83 other events, 852.2 us)

commit v3 on v2

--- a/solution.py
+++ b/solution.py
@@ -163,22 +163,22 @@
 
 def forward_kernel(second, experts, layout, core_ref, *refs):
     blocks, refs = laid_out(layout, refs)
+    base_hbm, refs = refs[0], refs[1:]
     if second:
         (before_ref, gate_before_ref, place_before_ref, back_ref, cot_ref), refs = refs[:5], refs[5:]
     else:
         (x_ref,), refs = refs[:1], refs[1:]
-    (gain_ref, base_ref, seg_col_ref, seg_row_ref, route_ref, place_ref), refs = (
-        refs[:6],
-        refs[6:],
-    )
+    (gain_ref, seg_col_ref, seg_row_ref, route_ref, place_ref), refs = refs[:5], refs[5:]
     (
-        token_ref, q_ref, k_ref, v_ref, o_ref, p_ref, mid_ref, h2_ref, share_ref, gate_ref, send_ref,
+        token_ref, q_ref, k_ref, v_ref, o_ref, p_hbm, mid_ref, h2_ref, share_ref, gate_ref, send_ref,
     ), refs = refs[:11], refs[11:]
     if second:
         (x_out_ref, combined_ref, grad_send_ref), refs = refs[:3], refs[3:]
-    weights, router_ref, mask_ref, sems = refs
+    weights, router_ref, mask_ref, base_ref, p_ref, part_sems, sems = refs
     zero_token(token_ref)
     copies = weight_copies(core_ref, int(second), (0, 4), blocks, weights, router_ref, sems)
+    base_copy = pltpu.make_async_copy(base_hbm, base_ref, part_sems.at[0])
+    base_copy.start()
     slots = send_ref.shape[0]
     rows = q_ref.shape[0]
     if second:
@@ -198,6 +198,11 @@
     k_ref[...] = dot(h1, weights[1]).astype(bf16)
     v_ref[...] = dot(h1, weights[2]).astype(bf16)
     masks = head_masks()
+    base_copy.wait()
+
+    def leaving(p):
+        both = pl.ds(2 * p, 2)
+        return pltpu.make_async_copy(p_ref.at[both], p_hbm.at[both], part_sems.at[1 + p])
 
     def pair(p, carry):
         columns = pl.ds(pl.multiple_of(p * 128, 128), 128)
@@ -213,6 +218,7 @@
             p_ref[head] = shares
             mixed = mixed + dot(shares, values * masks[half])
         o_ref[:, columns] = mixed.astype(bf16)
+        leaving(p).start()
         return carry
 
     lax.fori_loop(0, p_ref.shape[0] // 2, pair, 0)
@@ -234,23 +240,33 @@
     if second:
         grad_out = (gate * cot_ref[...].astype(f32)).astype(bf16)
         grad_send_ref[...] = dot(gather, grad_out).astype(bf16)
+    for p in range(p_ref.shape[0] // 2):
+        leaving(p).wait()
 
 
 def heads_backward_kernel(second, layout, core_ref, *refs):
     blocks, refs = laid_out(layout, refs)
+    p_hbm, refs = refs[0], refs[1:]
     (
-        q_ref, k_ref, v_ref, p_ref, mid_ref, h2_ref, share_ref, gate_ref, dy_ref, dback_ref,
+        q_ref, k_ref, v_ref, mid_ref, h2_ref, share_ref, gate_ref, dy_ref, dback_ref,
         out_ref, gain_ref, route_ref, place_ref,
-    ), refs = refs[:14], refs[14:]
+    ), refs = refs[:13], refs[13:]
     (
         token_ref, dx1_ref, low_ref, dq_ref, dk_ref, dv_ref, router_grad_ref, gain_grad_ref,
         line_grad_ref,
     ), refs = refs[:9], refs[9:]
     if second:
         (y_ref,), refs = refs[:1], refs[1:]
-    weights, router_ref, do_ref, sems = refs
+    weights, router_ref, do_ref, p_ref, part_sems, sems = refs
     zero_token(token_ref)
+
+    def arriving(p):
+        both = pl.ds(2 * p, 2)
+        return pltpu.make_async_copy(p_hbm.at[both], p_ref.at[both], part_sems.at[p])
+
     copies = weight_copies(core_ref, int(second), (3, 1), blocks, weights, router_ref, sems)
+    for p in range(p_ref.shape[0] // 2):
+        arriving(p).start()
     rows = q_ref.shape[0]
     slots = dback_ref.shape[0]
     dy = dy_ref[...].astype(f32)
@@ -286,6 +302,7 @@
     flip = flip.astype(f32).astype(bf16)
 
     def pair(p, carry):
+        arriving(p).wait()
         columns = pl.ds(pl.multiple_of(p * 128, 128), 128)
         queries, keys, values = q_ref[:, columns], k_ref[:, columns], v_ref[:, columns]
         grad_mixed = do_ref[:, columns]
@@ -520,9 +537,10 @@
 smem = pl.BlockSpec(memory_space=pltpu.SMEM)
 vmem = pl.BlockSpec(memory_space=pltpu.VMEM)
 anywhere = pl.BlockSpec(memory_space=pl.ANY)
-
-
-def run(kernel, name, us, inputs, outs, scratch, core, weights=(), after=()):
+hbm = pl.BlockSpec(memory_space=pltpu.HBM)
+
+
+def run(kernel, name, us, inputs, outs, scratch, core, weights=(), after=(), apart=()):
     def marked(core_ref, *refs):
         at = len(weights) + len(inputs)
         return kernel(core_ref, *refs[:at], *refs[at + len(after) :])
@@ -535,7 +553,7 @@
         + [anywhere] * len(weights)
         + [vmem] * len(inputs)
         + [anywhere] * len(after),
-        out_specs=[smem] + [vmem] * (len(outs) - 1),
+        out_specs=[smem] + [hbm if at in apart else vmem for at in range(len(outs) - 1)],
         scratch_shapes=scratch,
         compiler_params=params(),
         cost_estimate=cost(us),
@@ -580,13 +598,15 @@
     held, sems = weight_scratch(layout, 4, width, True)
     return run(
         functools.partial(forward_kernel, second, experts, layout), "attention_forward", 15, inputs, outs,
-        held + [pltpu.VMEM((rows, rows), f32)] + sems, core, weights, after,
+        held + [pltpu.VMEM((rows, rows), f32)]
+        + [pltpu.VMEM((heads, 128, 2 * rows - 128), f32), pltpu.VMEM((heads, rows, rows), bf16)]
+        + [pltpu.SemaphoreType.DMA((1 + heads // 2,))] + sems, core, weights, after, (4,),
     )
 
 
 def run_heads_backward(second, layout, core, weights, inputs, experts, after):
     rows, width = inputs[0].shape
-    heads = inputs[3].shape[0]
+    heads = weights[-1].shape[0]
     outs = [shape((rows, width), f32)] + [shape((rows, width))] * 4 + [
         shape((experts, width), f32),
         shape((1, width), f32),
@@ -597,7 +617,8 @@
     held, sems = weight_scratch(layout, 1, width, True)
     return run(
         functools.partial(heads_backward_kernel, second, layout), "heads_backward", 20, inputs, outs,
-        held + [pltpu.VMEM((rows, width), bf16)] + sems, core, weights, after,
+        held + [pltpu.VMEM((rows, width), bf16), pltpu.VMEM((heads, rows, rows), bf16)]
+        + [pltpu.SemaphoreType.DMA((heads // 2,))] + sems, core, weights, after,
     )
 
 
@@ -663,18 +684,23 @@
     return found[1], little, results
 
 
-def run_expert(kernel, mine, tall, middles, ups, downs, n_middle, us, name):
+def run_expert(kernel, mine, tall, middles, ups, downs, n_middle, us, name, after=()):
     slots, width = tall.shape
     inner = ups[0].shape[1]
     tiles = 6 if inner % 768 == 0 else 1
     tile = inner // tiles
     whole = pl.BlockSpec((slots, width), lambda j: (0, 0))
     part = pl.BlockSpec((slots, tile), lambda j: (0, j))
+
+    def marked(*refs):
+        at = 6 + len(middles)
+        return kernel(*refs[:at], *refs[at + len(after) :])
+
     return pl.pallas_call(
-        kernel,
+        marked,
         grid=(tiles,),
         out_shape=[shape((slots, inner))] * n_middle + [shape((slots, width))],
-        in_specs=[smem, whole] + [part] * len(middles) + [anywhere] * 4,
+        in_specs=[smem, whole] + [part] * len(middles) + [anywhere] * (4 + len(after)),
         out_specs=[part] * n_middle + [whole],
         scratch_shapes=[
             pltpu.VMEM((tiles, width, tile), bf16),
@@ -685,7 +711,7 @@
         compiler_params=params(),
         cost_estimate=cost(us),
         name=name,
-    )(mine, tall, *middles, *ups, *downs)
+    )(mine, tall, *middles, *ups, *downs, *after)
 
 
 def run_up_grad(buf_a, buf_b, dpre_a, dpre_b):
@@ -726,6 +752,10 @@
 
 def swap(block):
     return lax.ppermute(block, "section", [(0, 1), (1, 0)])
+
+
+def moved(block, source):
+    return lax.ppermute(block, "section", [(source, 1 - source)])
 
 
 def across(block, bit, devices):
@@ -767,7 +797,8 @@
                     jnp.concatenate([found[p], got], axis),
                 )
         found = [p.reshape(1, p.shape[0], -1, p.shape[-1]) for p in found]
-        return [[[0]]] * pieces, False, [*found, *[swap(p) for p in found]]
+        passed = [[moved(p, source) for p in found] for source in range(2)]
+        return [[[0]]] * pieces, False, [[*found, *other] for other in passed]
     me = device.astype(jnp.int32).reshape(1)
     found = [p[None] for p in shards]
     differ = [[0] for _ in shards]
@@ -782,12 +813,8 @@
     layout = [
         [differ[p], [d ^ (1 << orders[p][-1]) for d in differ[p]]] for p in range(pieces)
     ]
-    near_other = [swap(p) for p in found]
-    far_other = [swap(p) for p in far]
-    arrays = []
-    for near, distant in ((found, far), (near_other, far_other)):
-        for p in range(pieces):
-            arrays += [near[p], distant[p]]
+    own = [block for couple in zip(found, far) for block in couple]
+    arrays = [[*own, *[moved(block, source) for block in own]] for source in range(2)]
     return layout, True, arrays
 
 
@@ -899,7 +926,7 @@
     place_cols = [place[:, None] for place in places]
     place_rows = [place[None, :] for place in places]
     layout, apart, weights = gathered(
-        cut, device, devices, (*bases, *place_rows, *place_cols, *route_cols, seg_col, seg_row, *gains)
+        cut, device, devices, (place_rows[0], route_cols[0], seg_col, seg_row, gains[0])
     )
     core = jnp.stack([section, device if apart else jnp.zeros_like(device)]).astype(jnp.int32)
     up_other = swap(expert_up[0, 0])
@@ -911,7 +938,8 @@
 
     def expert_forward(which, arrived):
         return run_expert(
-            expert_forward_kernel, mine[which], arrived, (), ups, downs, 2, 11, "expert_forward"
+            expert_forward_kernel, mine[which], arrived, (), ups, downs, 2, 11, "expert_forward",
+            weights[1][len(weights[1]) // 2 :] if which == 0 else (),
         )
 
     def expert_backward(mine, arrived, slope):
@@ -922,13 +950,13 @@
 
     def shared_inputs(which):
         return (
-            gains[which], bases[which], seg_col, seg_row, route_cols[which],
+            gains[which], seg_col, seg_row, route_cols[which],
         )
 
     inputs = own_micro(block_input)
     cot = own_micro(cotangent)
     token, q0, k0, v0, o0, p0, mid0, h20, share0, gate0, send0 = run_forward(
-        False, layout, core, weights, (inputs, *shared_inputs(0), place_rows[0]), slots, experts,
+        False, layout, core, [*weights[0], bases[0]], (inputs, *shared_inputs(0), place_rows[0]), slots, experts,
         heads, (),
     )
     buf0 = exchanged(send0)
@@ -936,7 +964,7 @@
     back0 = exchanged(result0)
     _, q1, k1, v1, o1, p1, mid1, h21, share1, gate1, send1, between, combined0, grad_send1 = (
         run_forward(
-            True, layout, core, weights,
+            True, layout, core, [*weights[1], bases[1]],
             (mid0, gate0, place_cols[0], back0, cot, *shared_inputs(1), place_rows[1]),
             slots, experts, heads, (),
         )
@@ -952,13 +980,13 @@
     )
     place_out = place_cols[1] + route_cols[1] * capacity
     _, dx11, low1, dq1, dk1, dv1, router_grad1, gain_two1, line_grad1, last = run_heads_backward(
-        True, layout, core, weights,
-        (q1, k1, v1, p1, mid1, h21, share1, gate1, cot, back1, place_out, gains[1],
+        True, layout, core, [*weights[1], p1],
+        (q1, k1, v1, mid1, h21, share1, gate1, cot, back1, place_out, gains[1],
          route_cols[1], place_out + capacity),
         experts, (),
     )
     token, dx1, gain_one1, dy0, grad_send0 = run_input_backward(
-        True, layout, core, weights,
+        True, layout, core, weights[1],
         (between, dx11, dq1, dk1, dv1, gains[1], gate0, place_rows[0]), slots, (),
     )
     token, keep1, give1 = run_weight_backward(
@@ -993,8 +1021,8 @@
 
     grad_down = grads[0](token_of(dbuf0))
     token, dx10, low0, dq0, dk0, dv0, router_grad0, gain_two0, line_grad0 = run_heads_backward(
-        False, layout, core, weights,
-        (q0, k0, v0, p0, mid0, h20, share0, gate0, dy0, dback0, combined0, gains[0],
+        False, layout, core, [*weights[0], p0],
+        (q0, k0, v0, mid0, h20, share0, gate0, dy0, dback0, combined0, gains[0],
          route_cols[0], place_cols[0]),
         experts, (grad_down,),
     )
@@ -1002,7 +1030,7 @@
         core, (inputs, gains[0], o0, low0, dq0, dk0, dv0), ()
     )
     _, dx0, gain_one0 = run_input_backward(
-        False, layout, core + token[0], weights, (inputs, dx10, dq0, dk0, dv0, gains[0]), slots, ()
+        False, layout, core + token[0], weights[0], (inputs, dx10, dq0, dk0, dv0, gains[0]), slots, ()
     )
 
     little = [

time: 560 us -> 554 us (0.989)
  waiting for transfers between devices: 135 us -> 111 us
  starting transfers between devices: 66.8 us -> 86.9 us
    all_to_all x5, waiting for transfers between devices: 64.3 us -> 42.4 us  [exchanged(): lax.all_to_all(block, 'expert', split_axis=0, concat_axis=0, tiled=True)]
    ppermute x0 -> x12, starting transfers between devices: none -> 18.4 us  [moved(): return lax.ppermute(block, 'section', [(source, 1 - source)])]
    ppermute x23 -> x17, waiting for transfers between devices: 15.8 us -> 6.68 us  [swap(): return lax.ppermute(block, 'section', [(0, 1), (1, 0)])]
    ppermute x0 -> x12, waiting for transfers between devices: none -> 7.08 us  [moved(): return lax.ppermute(block, 'section', [(source, 1 - source)])]
    unnamed x122 -> x118, local copies, waits for them, and re-layouts: 12 us -> 10.3 us
  transfers between devices with their start and end apart: 56 -> 62, of which waited for: 27 -> 31; matrix products, arithmetic and copies ran while one was open for 5% -> 5% of each run, Pallas kernels for 25% -> 25%
where the time goes in v3:
time: 554 us; the launch traced here: 543 us
  Pallas kernels  217 us (39%)
  waiting for transfers between devices  111 us (20%)
  starting transfers between devices  86.9 us (16%)
  blocking collectives  80.4 us (15%)
  other arithmetic  21.6 us (4%)
  local copies, waits for them, and re-layouts  15.8 us (3%)
  between operations  7.24 us (1%)
    pallas_call x16, Pallas kernels, run(): pl.pallas_call(marked, out_shape=outs, in_specs=[smem] + [anywhere] * len...  129 us
    all_to_all x2, blocking collectives, exchanged(): lax.all_to_all(block, 'expert', split_axis=0, concat_axis=0, tiled=True)  80.4 us
    ppermute x28, waiting for transfers between devices, across(): lax.ppermute(block, 'expert', [(i, i ^ 1 << bit) for i in range(devices)])  55.3 us
    pallas_call x4, Pallas kernels, run_expert(): pl.pallas_call(marked, grid=(tiles,), out_shape=[shape((slots, inner))] *...  53.7 us
    all_to_all x5, waiting for transfers between devices, exchanged(): lax.all_to_all(block, 'expert', split_axis=0, concat_axis=0, tiled=True)  42.4 us
    ppermute x28, starting transfers between devices, across(): lax.ppermute(block, 'expert', [(i, i ^ 1 << bit) for i in range(devices)])  35.9 us
    all_to_all x5, starting transfers between devices, exchanged(): lax.all_to_all(block, 'expert', split_axis=0, concat_axis=0, tiled=True)  26.7 us
    ppermute x12, starting transfers between devices, moved(): return lax.ppermute(block, 'section', [(source, 1 - source)])  18.4 us
  transfers between devices with their start and end apart: 62, of which 31 were waited for; matrix products, arithmetic and copies ran while one was open for 5% of the time, Pallas kernels for 25%

profile of v3, /device:TPU:0, one launch (start us, length us, event | category | flops | bytes accessed | tf_op | source)
XLA Modules:
  0.0 543.2 jit_solution(14656180826242293194)
XLA Ops:
  41.5 5.7 %collective-permute-done.7.refs_4_ = bf16[4,4,48,256]{3,2,1,0:T(8,128)(2,1)S(1)} collective-permute-done((bf16[4,4,48,256]{3,2,1,0:T(8,128)(2,1)}, bf16[4,4,48,256]{3,2,1,0:T(8,128)(2,1)S(1)}, u32[]{:S(2)}, u32[]{:S(2)}) %collective-permute-start.7) | collective-permute-done | bytes 393248 | tf_op jit(solution)/shard_map/ppermute | solution.py:762
  58.1 11.8 %collective-permute-done.11.refs_3_ = bf16[8,4,48,256]{3,2,1,0:T(8,128)(2,1)} collective-permute-done((bf16[8,4,48,256]{3,2,1,0:T(8,128)(2,1)}, bf16[8,4,48,256]{3,2,1,0:T(8,128)(2,1)}, u32[]{:S(2)}, u32[]{:S(2)}) %collective-permute-start.11) | collective-permute-done | bytes 786464 | tf_op jit(solution)/shard_map/ppermute | solution.py:762
  85.5 4.8 bias_base.3.refs_12_
  90.6 15.4 %attention_forward.2 = (s32[1]{0:T(128)}, bf16[384,768]{1,0:T(8,128)(2,1)}, bf16[384,768]{1,0:T(8,128)(2,1)}, bf16[384,768]{1,0:T(8,128)(2,1)}, bf16[384,768]{1,...) custom-call(s32[2]{0:T(128)} %pad_add_fusion.core_ref, ...), custom_call_target="tpu_custom_call" | custom-call | flops 15000000512 | tf_op jit(solution)/shard_map/attention_forward/pallas_call | solution.py:549
  106.0 7.2 %all-to-all-start = ((bf16[16,40,768]{2,1,0:T(8,128)(2,1)}), bf16[16,40,768]{2,1,0:T(8,128)(2,1)S(1)}, u32[]{:S(2)}, u32[]{:S(2)}) async-start(bf16[16,40,768]{2,1,0:T(8,128)(2,1)} %bitcast.110), calls=%async_computation | async-start | bytes 1966080 | tf_op jit(solution)/shard_map/all_to_all | solution.py:937
  127.9 8.2 %all-to-all-done = bf16[16,40,768]{2,1,0:T(8,128)(2,1)S(1)} async-done(((bf16[16,40,768]{2,1,0:T(8,128)(2,1)}), bf16[16,40,768]{2,1,0:T(8,128)(2,1)S(1)}, u32[]{:S(2)}, u32[]{:S(2)}) %all-to-all-start) | async-done | bytes 983072 | tf_op jit(solution)/shard_map/all_to_all | solution.py:937
  136.1 13.9 %expert_forward.2 = (bf16[640,3072]{1,0:T(8,128)(2,1)}, bf16[640,3072]{1,0:T(8,128)(2,1)}, bf16[640,768]{1,0:T(8,128)(2,1)}) custom-call(s32[1]{0:T(128)} %bitcast.15.refs_0_, bf16[640,768]{1,0:T(8,128)(2,1)S(1)} %bitcast.100, bf16[768,3072]{1,0:T(8,128)(2,1)} %bitcast.122, bf16[768,3072]{1,0:T(8,128)(2,1)} %collective-permute-done.25.refs_3_.refs_4_, ...), custom_call_target="tpu_custom_call" | custom-call | flops 11000000512 | tf_op jit(solution)/shard_map/expert_forward/pallas_call | solution.py:699
  150.1 6.3 %all-to-all-start.1 = ((bf16[16,40,768]{2,1,0:T(8,128)(2,1)}), bf16[16,40,768]{2,1,0:T(8,128)(2,1)S(1)}, u32[]{:S(2)}, u32[]{:S(2)}) async-start(bf16[16,40,768]{2,1,0:T(8,128)(2,1)} %bitcast.115), calls=%async_computation.1 | async-start | bytes 1966080 | tf_op jit(solution)/shard_map/all_to_all | solution.py:937
  158.3 4.8 bias_base.2.refs_12_
  163.1 15.0 %all-to-all-done.1 = bf16[16,40,768]{2,1,0:T(8,128)(2,1)S(1)} async-done(((bf16[16,40,768]{2,1,0:T(8,128)(2,1)}), bf16[16,40,768]{2,1,0:T(8,128)(2,1)S(1)}, u32[]{:S(2)}, u32[]{:S(2)}) %all-to-all-start.1) | async-done | bytes 983072 | tf_op jit(solution)/shard_map/all_to_all | solution.py:937
  179.1 17.6 %attention_forward.3 = (s32[1]{0:T(128)}, bf16[384,768]{1,0:T(8,128)(2,1)}, bf16[384,768]{1,0:T(8,128)(2,1)}, bf16[384,768]{1,0:T(8,128)(2,1)}, bf16[384,768]{1,...) custom-call(s32[2]{0:T(128)} %pad_add_fusion.core_ref, ...), custom_call_target="tpu_custom_call" | custom-call | flops 15000000512 | tf_op jit(solution)/shard_map/attention_forward/pallas_call | solution.py:549
  196.7 29.6 %all_to_all.74 = bf16[16,40,768]{2,1,0:T(8,128)(2,1)} all-to-all(bf16[16,40,768]{2,1,0:T(8,128)(2,1)} %bitcast.114), channel_id=1, replica_groups=mesh['section'=2,'expert'=16] {'expert'}, dimensions={0} | all-to-all | bytes 1966080 | tf_op jit(solution)/shard_map/all_to_all | solution.py:937
  230.1 14.9 %expert_forward.3 = (bf16[640,3072]{1,0:T(8,128)(2,1)}, bf16[640,3072]{1,0:T(8,128)(2,1)}, bf16[640,768]{1,0:T(8,128)(2,1)}) custom-call(s32[1]{0:T(128)} %bitcast.23.refs_0_, bf16[640,768]{1,0:T(8,128)(2,1)} %bitcast.25.refs_1_, bf16[768,3072]{1,0:T(8,128)(2,1)} %bitcast.123, bf16[768,3072]{1,0:T(8,128)(2,1)} %collective-permute-done.25.refs_3_.refs_4_, ...), custom_call_target="tpu_custom_call" | custom-call | flops 11000000512 | tf_op jit(solution)/shard_map/expert_forward/pallas_call | solution.py:699
  245.0 6.7 %all-to-all-done.3 = bf16[16,40,768]{2,1,0:T(8,128)(2,1)S(1)} async-done(((bf16[16,40,768]{2,1,0:T(8,128)(2,1)}), bf16[16,40,768]{2,1,0:T(8,128)(2,1)S(1)}, u32[]{:S(2)}, u32[]{:S(2)}) %all-to-all-start.3) | async-done | bytes 983072 | tf_op jit(solution)/shard_map/all_to_all | solution.py:937
  251.7 12.4 %expert_backward.2 = (bf16[640,3072]{1,0:T(8,128)(2,1)}, bf16[640,768]{1,0:T(8,128)(2,1)}) custom-call(s32[1]{0:T(128)} %bitcast.23.refs_0_, bf16[640,768]{1,0:T(8,128)(2,1)S(1)} %bitcast.103, bf16[640,3072]{1,0:T(8,128)(2,1)} %get-tuple-element.189.refs_2_, bf16[768,3072]{1,0:T(8,128)(2,1)} %bitcast.124, ...), custom_call_target="tpu_custom_call" | custom-call | flops 11000000512 | tf_op jit(solution)/shard_map/expert_backward/pallas_call | solution.py:699
  265.5 50.8 %all_to_all.75 = bf16[16,80,768]{2,1,0:T(8,128)(2,1)} all-to-all(bf16[16,80,768]{2,1,0:T(8,128)(2,1)S(1)} %pad_maximum_fusion), channel_id=1, replica_groups=mesh['section'=2,'expert'=16] {'expert'}, dimensions={0} | all-to-all | bytes 3932160 | tf_op jit(solution)/shard_map/all_to_all | solution.py:937
  316.3 19.2 %heads_backward.2 = (s32[1]{0:T(128)}, f32[384,768]{1,0:T(8,128)}, bf16[384,768]{1,0:T(8,128)(2,1)}, bf16[384,768]{1,0:T(8,128)(2,1)}, bf16[384,768]{1,0:T(8,128...) custom-call(s32[2]{0:T(128)} %pad_add_fusion.core_ref, ...), custom_call_target="tpu_custom_call" | custom-call | flops 20000000000 | tf_op jit(solution)/shard_map/heads_backward/pallas_call | solution.py:549
  335.5 9.0 %input_backward.2 = (s32[1]{0:T(128)}, f32[384,768]{1,0:T(8,128)}, f32[1,768]{1,0:T(1,128)}, bf16[384,768]{1,0:T(8,128)(2,1)}, bf16[640,768]{1,0:T(8,128)(2,1)}) custom-call(s32[2]{0:T(128)} %pad_add_fusion.core_ref, bf16[8,5,48,256]{3,2,1,0:T(8,128)(2,1)} %get-tuple-element.170.refs_0_, bf16[8,5,48,256]{3,2,1,0:T(8,128)(2,1)} %copy-done.26, ...), custom_call_target="tpu_custom_call" | custom-call | flops 6000000000 | tf_op jit(solution)/shard_map/input_backward/pallas_call | solution.py:549
  350.0 8.9 %weight_backward.2 = (s32[1]{0:T(128)}, bf16[2,768,768]{2,1,0:T(8,128)(2,1)}, bf16[2,768,768]{2,1,0:T(8,128)(2,1)}) custom-call(s32[2]{0:T(128)} %broadcast_add_fusion.2.core_ref, bf16[384,768]{1,0:T(8,128)(2,1)} %get-tuple-element.177.refs_12_.refs_0_, f32[2,768]{1,0:T(2,128)} %get-tuple-element.325.refs_18_.refs_23_.refs_17_.refs_1_, ...), custom_call_target="tpu_custom_call" | custom-call | flops 6000000000 | tf_op jit(solution)/shard_map/weight_backward/pallas_call | solution.py:549
  359.6 10.3 %all-to-all-done.5 = bf16[16,40,768]{2,1,0:T(8,128)(2,1)S(1)} async-done(((bf16[16,40,768]{2,1,0:T(8,128)(2,1)}), bf16[16,40,768]{2,1,0:T(8,128)(2,1)S(1)}, u32[]{:S(2)}, u32[]{:S(2)}) %all-to-all-start.5) | async-done | bytes 983072 | tf_op jit(solution)/shard_map/all_to_all | solution.py:937
  369.8 12.4 %expert_backward.3 = (bf16[640,3072]{1,0:T(8,128)(2,1)}, bf16[640,768]{1,0:T(8,128)(2,1)}) custom-call(s32[1]{0:T(128)S(6)} %add.238.refs_0_, bf16[640,768]{1,0:T(8,128)(2,1)S(1)} %bitcast.106, bf16[640,3072]{1,0:T(8,128)(2,1)} %get-tuple-element.209.refs_2_, bf16[768,3072]{1,0:T(8,128)(2,1)} %bitcast.125, ...), custom_call_target="tpu_custom_call" | custom-call | flops 11000000512 | tf_op jit(solution)/shard_map/expert_backward/pallas_call | solution.py:699
  382.2 5.9 %all-to-all-start.6 = ((bf16[16,40,768]{2,1,0:T(8,128)(2,1)}), bf16[16,40,768]{2,1,0:T(8,128)(2,1)}, u32[]{:S(2)}, u32[]{:S(2)}) async-start(bf16[16,40,768]{2,1,0:T(8,128)(2,1)} %bitcast.109), calls=%async_computation.6 | async-start | bytes 1966080 | tf_op jit(solution)/shard_map/all_to_all | solution.py:937
  395.4 12.4 %conditional.2 = (f32[3072,768]{1,0:T(8,128)}) conditional(s32[]{:T(128)} %convert_element_type.239, (bf16[640,768]{1,0:T(8,128)(2,1)S(1)}, bf16[640,768]{1,0:T(8,128)(2,1)}, bf16[640,3072]{1,0:T(8,128)(2,1)}, bf16[640,3072]{1,0:T(8,128)(2,1)}) %tuple.53, (bf16[640,768]{1,0:T(8,128)(2,1)S(1)}, bf16[640,768]{1,0:T(8,128)(2,1)}, ...), branch_computations={%region_4.5_spmd, %region_5.6_spmd} | conditional | flops 10000000000 | bytes 8 | solution.py:1013
  395.4 12.4 %down_gradient.3 = f32[3072,768]{1,0:T(8,128)} custom-call(bf16[640,768]{1,0:T(8,128)(2,1)S(1)} %get-tuple-element.42.dout_a, bf16[640,768]{1,0:T(8,128)(2,1)} %get-tuple-element.43.dout_b, bf16[640,3072]{1,0:T(8,128)(2,1)} %get-tuple-element.44.act_a, bf16[640,3072]{1,0:T(8,128)(2,1)} %get-tuple-element.45.act_b), custom_call_target="tpu_custom_call" | custom-call | flops 10000000000 | tf_op jit(solution)/shard_map/cond/branch_1_fun/down_gradient/pallas_call | solution.py:741
  410.0 17.0 %heads_backward.3 = (s32[1]{0:T(128)}, f32[384,768]{1,0:T(8,128)}, bf16[384,768]{1,0:T(8,128)(2,1)}, bf16[384,768]{1,0:T(8,128)(2,1)}, bf16[384,768]{1,0:T(8,128...) custom-call(s32[2]{0:T(128)} %pad_add_fusion.core_ref, ...), custom_call_target="tpu_custom_call" | custom-call | flops 20000000000 | tf_op jit(solution)/shard_map/heads_backward/pallas_call | solution.py:549
  427.0 9.0 %weight_backward.3 = (s32[1]{0:T(128)}, bf16[2,768,768]{2,1,0:T(8,128)(2,1)}, bf16[2,768,768]{2,1,0:T(8,128)(2,1)}) custom-call(s32[2]{0:T(128)} %pad_add_fusion.core_ref, bf16[384,768]{1,0:T(8,128)(2,1)} %select_bitcast_fusion.5.refs_13_.refs_0_.refs_12_, f32[2,768]{1,0:T(2,128)} %get-tuple-element.326.refs_10_.refs_14_.refs_23_.refs_1_.refs_17_, ...), custom_call_target="tpu_custom_call" | custom-call | flops 6000000000 | tf_op jit(solution)/shard_map/weight_backward/pallas_call | solution.py:549
  442.0 7.5 %input_backward.3 = (s32[1]{0:T(128)}, f32[384,768]{1,0:T(8,128)}, f32[1,768]{1,0:T(1,128)}) custom-call(s32[2]{0:T(128)} %broadcast_add_fusion.1.core_ref, bf16[8,5,48,256]{3,2,1,0:T(8,128)(2,1)} %get-tuple-element.170.refs_0_, bf16[8,5,48,256]{3,2,1,0:T(8,128)(2,1)} %copy-done.26, bf16[8,4,48,256]{3,2,1,0:T(8,128)(2,1)} %get-tuple-element.171.refs_2_, ...), custom_call_target="tpu_custom_call" | custom-call | flops 6000000000 | tf_op jit(solution)/shard_map/input_backward/pallas_call | solution.py:549
  452.6 6.9 %fold_first.1 = (s32[1]{0:T(128)}, bf16[4,8,48,256]{3,2,1,0:T(8,128)(2,1)}, bf16[4,8,48,256]{3,2,1,0:T(8,128)(2,1)}, bf16[4,8,48,256]{3,2,1,0:T(8,128)(2,1)}, bf...) custom-call(s32[1]{0:T(128)} %bitcast.1.core_ref, ...), custom_call_target="tpu_custom_call" | custom-call | flops 4000000000 | tf_op jit(solution)/shard_map/fold_first/pallas_call | solution.py:549
  471.0 12.4 %conditional.3 = (f32[768,3072]{1,0:T(8,128)}) conditional(s32[]{:T(128)} %convert_element_type.241, (bf16[640,768]{1,0:T(8,128)(2,1)}, bf16[640,768]{1,0:T(8,128)(2,1)}, bf16[640,3072]{1,0:T(8,128)(2,1)}, bf16[640,3072]{1,0:T(8,128)(2,1)}) %tuple.22, (bf16[640,768]{1,0:T(8,128)(2,1)S(1)}, bf16[640,768]{1,0:T(8,128)(2,1)}, ...), branch_computations={%region_6.7_spmd, %region_7.8_spmd} | conditional | flops 10000000000 | bytes 8 | solution.py:1013
  471.0 12.4 %up_gradient.3 = f32[768,3072]{1,0:T(8,128)} custom-call(bf16[640,768]{1,0:T(8,128)(2,1)S(1)} %get-tuple-element.50.buf_a, bf16[640,768]{1,0:T(8,128)(2,1)} %get-tuple-element.51.buf_b, bf16[640,3072]{1,0:T(8,128)(2,1)} %get-tuple-element.52.dpre_a, bf16[640,3072]{1,0:T(8,128)(2,1)} %get-tuple-element.53.dpre_b), custom_call_target="tpu_custom_call" | custom-call | flops 10000000000 | tf_op jit(solution)/shard_map/cond/branch_1_fun/up_gradient/pallas_call | solution.py:723
  492.8 7.5 %collective-permute-done.45.refs_3_ = bf16[4,4,48,256]{3,2,1,0:T(8,128)(2,1)S(1)} collective-permute-done((bf16[4,4,48,256]{3,2,1,0:T(8,128)(2,1)}, bf16[4,4,48,256]{3,2,1,0:T(8,128)(2,1)S(1)}, u32[]{:S(2)}, u32[]{:S(2)}) %collective-permute-start.45) | collective-permute-done | bytes 393248 | tf_op jit(solution)/shard_map/ppermute | solution.py:762
  524.4 6.0 %collective-permute-done.52 = f32[30,768]{1,0:T(8,128)S(1)} collective-permute-done((f32[30,768]{1,0:T(8,128)S(1)}, f32[30,768]{1,0:T(8,128)S(1)}, u32[]{:S(2)}, u32[]{:S(2)}) %collective-permute-start.52) | collective-permute-done | bytes 92192 | tf_op jit(solution)/shard_map/ppermute | solution.py:762
  (294 shorter events, 166.6 us)
Async XLA Ops:
  2.5 18.5 %collective-permute-start = (bf16[1,5,48,256]{3,2,1,0:T(8,128)(2,1)S(1)}, bf16[1,5,48,256]{3,2,1,0:T(8,128)(2,1)S(1)}, u32[]{:S(2)}, u32[]{:S(2)}) collective-permute-start(bf16[1,5,48,256]{3,2,1,0:T(8,128)(2,1)S(1)} %fusion.9.refs_0_), channel_id=1, source_target_pairs={{0,8},{1,9},{2,10},{3,11},{4,12},{5,13},{6,14},{7,15},{8,0},{9,1},... | collective-permute-start | bytes 368648 | tf_op jit(solution)/shard_map/ppermute | solution.py:762
  6.6 13.1 %collective-permute-start.1 = (bf16[1,4,48,256]{3,2,1,0:T(8,128)(2,1)S(1)}, bf16[1,4,48,256]{3,2,1,0:T(8,128)(2,1)S(1)}, u32[]{:S(2)}, u32[]{:S(2)}) collective-permute-start(bf16[1,4,48,256]{3,2,1,0:T(8,128)(2,1)S(1)} %get-tuple-element.322.refs_1_), channel_id=1, source_target_pairs={{0,8},{1,9},{2,10},{3,11},{4,12},{5,13},{6,14},{7,15},{8,0},{9,1},... | collective-permute-start | bytes 294920 | tf_op jit(solution)/shard_map/ppermute | solution.py:762
  6.7 14.3 %collective-permute-start.2 = (bf16[1,4,48,256]{3,2,1,0:T(8,128)(2,1)S(1)}, bf16[1,4,48,256]{3,2,1,0:T(8,128)(2,1)S(1)}, u32[]{:S(2)}, u32[]{:S(2)}) collective-permute-start(bf16[1,4,48,256]{3,2,1,0:T(8,128)(2,1)S(1)} %get-tuple-element.320.refs_2_), channel_id=1, source_target_pairs={{0,8},{1,9},{2,10},{3,11},{4,12},{5,13},{6,14},{7,15},{8,0},{9,1},... | collective-permute-start | bytes 294920 | tf_op jit(solution)/shard_map/ppermute | solution.py:762
  52.6 17.4 %collective-permute-start.11 = (bf16[8,4,48,256]{3,2,1,0:T(8,128)(2,1)}, bf16[8,4,48,256]{3,2,1,0:T(8,128)(2,1)}, u32[]{:S(2)}, u32[]{:S(2)}) collective-permute-start(bf16[8,4,48,256]{3,2,1,0:T(8,128)(2,1)} %get-tuple-element.171.refs_2_), channel_id=1, source_target_pairs={{0,4},{1,5},{2,6},{3,7},{4,0},{5,1},{6,2},{7,3},{8,12},{9,13},{10,... | collective-permute-start | bytes 2359304 | tf_op jit(solution)/shard_map/ppermute | solution.py:762
  53.3 18.0 %collective-permute-start.12 = (bf16[8,4,48,256]{3,2,1,0:T(8,128)(2,1)}, bf16[8,4,48,256]{3,2,1,0:T(8,128)(2,1)}, u32[]{:S(2)}, u32[]{:S(2)}) collective-permute-start(bf16[8,4,48,256]{3,2,1,0:T(8,128)(2,1)} %get-tuple-element.172.refs_4_), channel_id=1, source_target_pairs={{0,1},{1,0},{2,3},{3,2},{4,5},{5,4},{6,7},{7,6},{8,9},{9,8},{10,11... | collective-permute-start | bytes 2359304 | tf_op jit(solution)/shard_map/ppermute | solution.py:762
  54.3 17.1 %collective-permute-start.21 = (bf16[8,4,48,256]{3,2,1,0:T(8,128)(2,1)}, bf16[8,4,48,256]{3,2,1,0:T(8,128)(2,1)S(1)}, u32[]{:S(2)}, u32[]{:S(2)}) collective-permute-start(bf16[8,4,48,256]{3,2,1,0:T(8,128)(2,1)} %get-tuple-element.171.refs_2_), channel_id=1, source_target_pairs={{0,16},{1,17},{2,18},{3,19},{4,20},{5,21},{6,22},{7,23},{8,24},{9,... | collective-permute-start | bytes 2359304 | tf_op jit(solution)/shard_map/ppermute | solution.py:758
  55.6 20.6 %collective-permute-start.10 = (bf16[8,5,48,256]{3,2,1,0:T(8,128)(2,1)}, bf16[8,5,48,256]{3,2,1,0:T(8,128)(2,1)S(1)}, u32[]{:S(2)}, u32[]{:S(2)}) collective-permute-start(bf16[8,5,48,256]{3,2,1,0:T(8,128)(2,1)} %get-tuple-element.170.refs_0_), channel_id=1, source_target_pairs={{0,2},{1,3},{2,0},{3,1},{4,6},{5,7},{6,4},{7,5},{8,10},{9,11},{10,... | collective-permute-start | bytes 2949128 | tf_op jit(solution)/shard_map/ppermute | solution.py:762
  56.8 23.9 %collective-permute-start.19 = (bf16[8,5,48,256]{3,2,1,0:T(8,128)(2,1)}, bf16[8,5,48,256]{3,2,1,0:T(8,128)(2,1)S(1)}, u32[]{:S(2)}, u32[]{:S(2)}) collective-permute-start(bf16[8,5,48,256]{3,2,1,0:T(8,128)(2,1)} %get-tuple-element.170.refs_0_), channel_id=1, source_target_pairs={{0,16},{1,17},{2,18},{3,19},{4,20},{5,21},{6,22},{7,23},{8,24},{9,... | collective-permute-start | bytes 2949128 | tf_op jit(solution)/shard_map/ppermute | solution.py:758
  71.3 64.8 %collective-permute-start.25 = (bf16[768,3072]{1,0:T(8,128)(2,1)}, bf16[768,3072]{1,0:T(8,128)(2,1)}, u32[]{:S(2)}, u32[]{:S(2)}) collective-permute-start(bf16[768,3072]{1,0:T(8,128)(2,1)} %bitcast.121), channel_id=1, source_target_pairs={{0,16},{16,0},{1,17},{17,1},{2,18},{18,2},{3,19},{19,3},{4,20},{20... | collective-permute-start | bytes 14155784 | tf_op jit(solution)/shard_map/ppermute | solution.py:754
  71.4 64.7 %collective-permute-start.26 = (bf16[3072,768]{1,0:T(8,128)(2,1)}, bf16[3072,768]{1,0:T(8,128)(2,1)}, u32[]{:S(2)}, u32[]{:S(2)}) collective-permute-start(bf16[3072,768]{1,0:T(8,128)(2,1)} %bitcast.126), channel_id=1, source_target_pairs={{0,16},{16,0},{1,17},{17,1},{2,18},{18,2},{3,19},{19,3},{4,20},{20... | collective-permute-start | bytes 14155784 | tf_op jit(solution)/shard_map/ppermute | solution.py:754
  76.2 14.4 %collective-permute-start.20 = (bf16[8,5,48,256]{3,2,1,0:T(8,128)(2,1)S(1)}, bf16[8,5,48,256]{3,2,1,0:T(8,128)(2,1)}, u32[]{:S(2)}, u32[]{:S(2)}) collective-permute-start(bf16[8,5,48,256]{3,2,1,0:T(8,128)(2,1)S(1)} %collective-permute-done.10.refs_1_), channel_id=1, source_target_pairs={{0,16},{1,17},{2,18},{3,19},{4,20},{5,21},{6,22},{7,23},{8,24},{9,... | collective-permute-start | bytes 2949128 | tf_op jit(solution)/shard_map/ppermute | solution.py:758
  106.0 30.1 %all-to-all-start = ((bf16[16,40,768]{2,1,0:T(8,128)(2,1)}), bf16[16,40,768]{2,1,0:T(8,128)(2,1)S(1)}, u32[]{:S(2)}, u32[]{:S(2)}) async-start(bf16[16,40,768]{2,1,0:T(8,128)(2,1)} %bitcast.110), calls=%async_computation | async-start | bytes 1966080 | tf_op jit(solution)/shard_map/all_to_all | solution.py:937
  150.1 28.1 %all-to-all-start.1 = ((bf16[16,40,768]{2,1,0:T(8,128)(2,1)}), bf16[16,40,768]{2,1,0:T(8,128)(2,1)S(1)}, u32[]{:S(2)}, u32[]{:S(2)}) async-start(bf16[16,40,768]{2,1,0:T(8,128)(2,1)} %bitcast.115), calls=%async_computation.1 | async-start | bytes 1966080 | tf_op jit(solution)/shard_map/all_to_all | solution.py:937
  226.3 25.4 %all-to-all-start.3 = ((bf16[16,40,768]{2,1,0:T(8,128)(2,1)}), bf16[16,40,768]{2,1,0:T(8,128)(2,1)S(1)}, u32[]{:S(2)}, u32[]{:S(2)}) async-start(bf16[16,40,768]{2,1,0:T(8,128)(2,1)} %bitcast.113), calls=%async_computation.3 | async-start | bytes 1966080 | tf_op jit(solution)/shard_map/all_to_all | solution.py:937
  344.5 25.3 %all-to-all-start.5 = ((bf16[16,40,768]{2,1,0:T(8,128)(2,1)}), bf16[16,40,768]{2,1,0:T(8,128)(2,1)S(1)}, u32[]{:S(2)}, u32[]{:S(2)}) async-start(bf16[16,40,768]{2,1,0:T(8,128)(2,1)} %bitcast.111), calls=%async_computation.5 | async-start | bytes 1966080 | tf_op jit(solution)/shard_map/all_to_all | solution.py:937
  348.2 44.3 %collective-permute-start.29 = (bf16[640,3072]{1,0:T(8,128)(2,1)}, bf16[640,3072]{1,0:T(8,128)(2,1)}, u32[]{:S(2)}, u32[]{:S(2)}) collective-permute-start(bf16[640,3072]{1,0:T(8,128)(2,1)} %get-tuple-element.212), channel_id=1, source_target_pairs={{0,16},{16,0},{1,17},{17,1},{2,18},{18,2},{3,19},{19,3},{4,20},{20... | collective-permute-start | bytes 11796488 | tf_op jit(solution)/shard_map/ppermute | solution.py:754
  348.2 47.1 %collective-permute-start.31 = (bf16[640,3072]{1,0:T(8,128)(2,1)}, bf16[640,3072]{1,0:T(8,128)(2,1)}, u32[]{:S(2)}, u32[]{:S(2)}) collective-permute-start(bf16[640,3072]{1,0:T(8,128)(2,1)} %get-tuple-element.213), channel_id=1, source_target_pairs={{0,16},{16,0},{1,17},{17,1},{2,18},{18,2},{3,19},{19,3},{4,20},{20... | collective-permute-start | bytes 11796488 | tf_op jit(solution)/shard_map/ppermute | solution.py:754
  382.2 27.7 %all-to-all-start.6 = ((bf16[16,40,768]{2,1,0:T(8,128)(2,1)}), bf16[16,40,768]{2,1,0:T(8,128)(2,1)}, u32[]{:S(2)}, u32[]{:S(2)}) async-start(bf16[16,40,768]{2,1,0:T(8,128)(2,1)} %bitcast.109), calls=%async_computation.6 | async-start | bytes 1966080 | tf_op jit(solution)/shard_map/all_to_all | solution.py:937
  388.7 72.8 %collective-permute-start.41 = (bf16[640,3072]{1,0:T(8,128)(2,1)}, bf16[640,3072]{1,0:T(8,128)(2,1)}, u32[]{:S(2)}, u32[]{:S(2)}) collective-permute-start(bf16[640,3072]{1,0:T(8,128)(2,1)} %get-tuple-element.241), channel_id=1, source_target_pairs={{0,16},{16,0},{1,17},{17,1},{2,18},{18,2},{3,19},{19,3},{4,20},{20... | collective-permute-start | bytes 11796488 | tf_op jit(solution)/shard_map/ppermute | solution.py:754
  392.3 57.2 %collective-permute-start.35 = (bf16[2,768,768]{2,1,0:T(8,128)(2,1)}, bf16[2,768,768]{2,1,0:T(8,128)(2,1)}, u32[]{:S(2)}, u32[]{:S(2)}) collective-permute-start(bf16[2,768,768]{2,1,0:T(8,128)(2,1)} %get-tuple-element.233), channel_id=1, source_target_pairs={{0,16},{16,0},{1,17},{17,1},{2,18},{18,2},{3,19},{19,3},{4,20},{20... | collective-permute-start | bytes 7077896 | tf_op jit(solution)/shard_map/ppermute | solution.py:754
  394.9 71.4 %collective-permute-start.43 = (bf16[640,3072]{1,0:T(8,128)(2,1)}, bf16[640,3072]{1,0:T(8,128)(2,1)}, u32[]{:S(2)}, u32[]{:S(2)}) collective-permute-start(bf16[640,3072]{1,0:T(8,128)(2,1)} %get-tuple-element.242), channel_id=1, source_target_pairs={{0,16},{16,0},{1,17},{17,1},{2,18},{18,2},{3,19},{19,3},{4,20},{20... | collective-permute-start | bytes 11796488 | tf_op jit(solution)/shard_map/ppermute | solution.py:754
  436.0 15.1 %collective-permute-start.34 = (bf16[2,768,768]{2,1,0:T(8,128)(2,1)}, bf16[2,768,768]{2,1,0:T(8,128)(2,1)S(1)}, u32[]{:S(2)}, u32[]{:S(2)}) collective-permute-start(bf16[2,768,768]{2,1,0:T(8,128)(2,1)} %get-tuple-element.231), channel_id=1, source_target_pairs={{0,16},{16,0},{1,17},{17,1},{2,18},{18,2},{3,19},{19,3},{4,20},{20... | collective-permute-start | bytes 7077896 | tf_op jit(solution)/shard_map/ppermute | solution.py:754
  441.6 17.9 %collective-permute-start.40 = (bf16[640,768]{1,0:T(8,128)(2,1)}, bf16[640,768]{1,0:T(8,128)(2,1)}, u32[]{:S(2)}, u32[]{:S(2)}) collective-permute-start(bf16[640,768]{1,0:T(8,128)(2,1)} %bitcast.25.refs_1_), channel_id=1, source_target_pairs={{0,16},{16,0},{1,17},{17,1},{2,18},{18,2},{3,19},{19,3},{4,20},{20... | collective-permute-start | bytes 2949128 | tf_op jit(solution)/shard_map/ppermute | solution.py:754
  449.6 14.1 %collective-permute-start.27 = (bf16[384,768]{1,0:T(8,128)(2,1)S(1)}, bf16[384,768]{1,0:T(8,128)(2,1)S(1)}, u32[]{:S(2)}, u32[]{:S(2)}) collective-permute-start(bf16[384,768]{1,0:T(8,128)(2,1)S(1)} %broadcast_select_fusion.1), channel_id=1, source_target_pairs={{0,16},{16,0},{1,17},{17,1},{2,18},{18,2},{3,19},{19,3},{4,20},{20... | collective-permute-start | bytes 1769480 | tf_op jit(solution)/shard_map/ppermute | solution.py:754
  451.1 39.4 %collective-permute-start.32 = (f32[384,768]{1,0:T(8,128)}, f32[384,768]{1,0:T(8,128)S(1)}, u32[]{:S(2)}, u32[]{:S(2)}) collective-permute-start(f32[384,768]{1,0:T(8,128)} %broadcast_select_fusion), channel_id=1, source_target_pairs={{0,16},{16,0},{1,17},{17,1},{2,18},{18,2},{3,19},{19,3},{4,20},{20... | collective-permute-start | bytes 3538952 | tf_op jit(solution)/shard_map/ppermute | solution.py:754
  459.5 23.9 %collective-permute-start.37 = (bf16[4,8,48,256]{3,2,1,0:T(8,128)(2,1)}, bf16[4,8,48,256]{3,2,1,0:T(8,128)(2,1)}, u32[]{:S(2)}, u32[]{:S(2)}) collective-permute-start(bf16[4,8,48,256]{3,2,1,0:T(8,128)(2,1)} %get-tuple-element.238), channel_id=1, source_target_pairs={{0,2},{1,3},{2,0},{3,1},{4,6},{5,7},{6,4},{7,5},{8,10},{9,11},{10,... | collective-permute-start | bytes 2359304 | tf_op jit(solution)/shard_map/ppermute | solution.py:762
  461.5 21.9 %collective-permute-start.38 = (bf16[4,8,48,256]{3,2,1,0:T(8,128)(2,1)}, bf16[4,8,48,256]{3,2,1,0:T(8,128)(2,1)}, u32[]{:S(2)}, u32[]{:S(2)}) collective-permute-start(bf16[4,8,48,256]{3,2,1,0:T(8,128)(2,1)} %get-tuple-element.239), channel_id=1, source_target_pairs={{0,4},{1,5},{2,6},{3,7},{4,0},{5,1},{6,2},{7,3},{8,12},{9,13},{10,... | collective-permute-start | bytes 2359304 | tf_op jit(solution)/shard_map/ppermute | solution.py:762
  464.5 20.7 %collective-permute-start.39 = (bf16[4,8,48,256]{3,2,1,0:T(8,128)(2,1)}, bf16[4,8,48,256]{3,2,1,0:T(8,128)(2,1)}, u32[]{:S(2)}, u32[]{:S(2)}) collective-permute-start(bf16[4,8,48,256]{3,2,1,0:T(8,128)(2,1)} %get-tuple-element.240), channel_id=1, source_target_pairs={{0,1},{1,0},{2,3},{3,2},{4,5},{5,4},{6,7},{7,6},{8,9},{9,8},{10,11... | collective-permute-start | bytes 2359304 | tf_op jit(solution)/shard_map/ppermute | solution.py:762
  468.8 22.6 %collective-permute-start.36 = (f32[30,768]{1,0:T(8,128)S(1)}, f32[30,768]{1,0:T(8,128)S(1)}, u32[]{:S(2)}, u32[]{:S(2)}) collective-permute-start(f32[30,768]{1,0:T(8,128)S(1)} %add_add_fusion.4), channel_id=1, source_target_pairs={{0,1},{1,0},{2,3},{3,2},{4,5},{5,4},{6,7},{7,6},{8,9},{9,8},{10,11... | collective-permute-start | bytes 276488 | tf_op jit(solution)/shard_map/ppermute | solution.py:762
  491.4 16.9 %collective-permute-start.44 = (f32[30,768]{1,0:T(8,128)S(1)}, f32[30,768]{1,0:T(8,128)S(1)}, u32[]{:S(2)}, u32[]{:S(2)}) collective-permute-start(f32[30,768]{1,0:T(8,128)S(1)} %add_add_fusion.3), channel_id=1, source_target_pairs={{0,2},{1,3},{2,0},{3,1},{4,6},{5,7},{6,4},{7,5},{8,10},{9,11},{10,... | collective-permute-start | bytes 276488 | tf_op jit(solution)/shard_map/ppermute | solution.py:762
  517.0 13.5 %collective-permute-start.52 = (f32[30,768]{1,0:T(8,128)S(1)}, f32[30,768]{1,0:T(8,128)S(1)}, u32[]{:S(2)}, u32[]{:S(2)}) collective-permute-start(f32[30,768]{1,0:T(8,128)S(1)} %add_add_fusion.1), channel_id=1, source_target_pairs={{0,8},{1,9},{2,10},{3,11},{4,12},{5,13},{6,14},{7,15},{8,0},{9,1},... | collective-permute-start | bytes 276488 | tf_op jit(solution)/shard_map/ppermute | solution.py:762
  520.1 12.4 %collective-permute-start.53 = (bf16[4,1,48,256]{3,2,1,0:T(8,128)(2,1)S(1)}, bf16[4,1,48,256]{3,2,1,0:T(8,128)(2,1)S(1)}, u32[]{:S(2)}, u32[]{:S(2)}) collective-permute-start(bf16[4,1,48,256]{3,2,1,0:T(8,128)(2,1)S(1)} %copy-done.53), channel_id=1, source_target_pairs={{0,8},{1,9},{2,10},{3,11},{4,12},{5,13},{6,14},{7,15},{8,0},{9,1},... | collective-permute-start | bytes 294920 | tf_op jit(solution)/shard_map/ppermute | solution.py:762
  (87 other events, 925.6 us)

commit v4 on v3

--- a/solution.py
+++ b/solution.py
@@ -16,6 +16,8 @@
 f32 = jnp.float32
 bf16 = jnp.bfloat16
 vmem_bytes = 56 * 2**20
+small_bytes = 22 * 2**20
+small_kernels = ("fold_first", "fold", "fold_last", "join")
 pieces = 3
 
 
@@ -526,8 +528,8 @@
     return jax.ShapeDtypeStruct(dims, kind)
 
 
-def params():
-    return pltpu.CompilerParams(vmem_limit_bytes=vmem_bytes)
+def params(limit=vmem_bytes):
+    return pltpu.CompilerParams(vmem_limit_bytes=limit)
 
 
 def cost(us):
@@ -555,7 +557,7 @@
         + [anywhere] * len(after),
         out_specs=[smem] + [hbm if at in apart else vmem for at in range(len(outs) - 1)],
         scratch_shapes=scratch,
-        compiler_params=params(),
+        compiler_params=params(small_bytes if name in small_kernels else vmem_bytes),
         cost_estimate=cost(us),
         name=name,
     )(core, *weights, *inputs, *after)
@@ -868,8 +870,8 @@
     experts = router.shape[2]
     shard_rows = router.shape[1]
     buckets, heads = position_bias.shape[1:]
-    capacity = max(2, 3 * rows // (2 * experts))
-    capacity = -(-capacity // 8) * 8
+    most = max(2, 3 * rows // (2 * experts))
+    capacity = -(-most // 8) * 8
     slots = experts * capacity
 
     def both(own, other):
@@ -975,14 +977,14 @@
     dpre1, dbuf1 = expert_backward(mine[1], dout1, slope1)
     back1 = exchanged(
         jnp.concatenate(
-            [block.reshape(experts, capacity, width) for block in (result1, dbuf1)], axis=1
-        ).reshape(2 * slots, width)
-    )
-    place_out = place_cols[1] + route_cols[1] * capacity
+            [block.reshape(experts, capacity, width)[:, :most] for block in (result1, dbuf1)], axis=1
+        ).reshape(2 * experts * most, width)
+    )
+    place_out = place_cols[1] + route_cols[1] * (2 * most - capacity)
     _, dx11, low1, dq1, dk1, dv1, router_grad1, gain_two1, line_grad1, last = run_heads_backward(
         True, layout, core, [*weights[1], p1],
         (q1, k1, v1, mid1, h21, share1, gate1, cot, back1, place_out, gains[1],
-         route_cols[1], place_out + capacity),
+         route_cols[1], place_out + most),
         experts, (),
     )
     token, dx1, gain_one1, dy0, grad_send0 = run_input_backward(

time: 554 us -> 531 us (0.958)
  Pallas kernels: 217 us -> 201 us
  waiting for transfers between devices: 111 us -> 105 us
    pallas_call x16, Pallas kernels: 129 us -> 112 us  [run(): pl.pallas_call(marked, out_shape=outs, in_specs=[smem] + [anywhere] * len...]
    unnamed x118 -> x112, local copies, waits for them, and re-layouts: 10.3 us -> 12.4 us
  transfers between devices with their start and end apart: 62 -> 62, of which waited for: 31 -> 30; matrix products, arithmetic and copies ran while one was open for 5% -> 6% of each run, Pallas kernels for 25% -> 24%
where the time goes in v4:
time: 531 us; the launch traced here: 520 us
  Pallas kernels  201 us (38%)
  waiting for transfers between devices  105 us (20%)
  starting transfers between devices  85.2 us (16%)
  blocking collectives  76.6 us (14%)
  other arithmetic  25.5 us (5%)
  local copies, waits for them, and re-layouts  16.7 us (3%)
  between operations  7.34 us (1%)
    pallas_call x16, Pallas kernels, run(): pl.pallas_call(marked, out_shape=outs, in_specs=[smem] + [anywhere] * len...  112 us
    all_to_all x2, blocking collectives, exchanged(): lax.all_to_all(block, 'expert', split_axis=0, concat_axis=0, tiled=True)  76.6 us
    pallas_call x4, Pallas kernels, run_expert(): pl.pallas_call(marked, grid=(tiles,), out_shape=[shape((slots, inner))] *...  54 us
    ppermute x28, waiting for transfers between devices, across(): lax.ppermute(block, 'expert', [(i, i ^ 1 << bit) for i in range(devices)])  51.8 us
    all_to_all x5, waiting for transfers between devices, exchanged(): lax.all_to_all(block, 'expert', split_axis=0, concat_axis=0, tiled=True)  41.8 us
    ppermute x28, starting transfers between devices, across(): lax.ppermute(block, 'expert', [(i, i ^ 1 << bit) for i in range(devices)])  36.7 us
    all_to_all x5, starting transfers between devices, exchanged(): lax.all_to_all(block, 'expert', split_axis=0, concat_axis=0, tiled=True)  26.2 us
    ppermute x12, starting transfers between devices, moved(): return lax.ppermute(block, 'section', [(source, 1 - source)])  18.4 us
  transfers between devices with their start and end apart: 62, of which 30 were waited for; matrix products, arithmetic and copies ran while one was open for 6% of the time, Pallas kernels for 24%

profile of v4, /device:TPU:0, one launch (start us, length us, event | category | flops | bytes accessed | tf_op | source)
XLA Modules:
  0.0 520.2 jit_solution(15541285750697558497)
XLA Ops:
  15.2 4.5 collective-permute-done.1.refs_4_
  35.3 6.0 %collective-permute-done.7.refs_4_ = bf16[4,4,48,256]{3,2,1,0:T(8,128)(2,1)S(1)} collective-permute-done((bf16[4,4,48,256]{3,2,1,0:T(8,128)(2,1)S(1)}, bf16[4,4,48,256]{3,2,1,0:T(8,128)(2,1)S(1)}, u32[]{:S(2)}, u32[]{:S(2)}) %collective-permute-start.7) | collective-permute-done | bytes 393248 | tf_op jit(solution)/shard_map/ppermute | solution.py:764
  53.6 10.9 %collective-permute-done.11.refs_3_ = bf16[8,4,48,256]{3,2,1,0:T(8,128)(2,1)} collective-permute-done((bf16[8,4,48,256]{3,2,1,0:T(8,128)(2,1)S(1)}, bf16[8,4,48,256]{3,2,1,0:T(8,128)(2,1)}, u32[]{:S(2)}, u32[]{:S(2)}) %collective-permute-start.11) | collective-permute-done | bytes 786464 | tf_op jit(solution)/shard_map/ppermute | solution.py:764
  66.5 5.7 %collective-permute-done.10.refs_1_ = bf16[8,5,48,256]{3,2,1,0:T(8,128)(2,1)} collective-permute-done((bf16[8,5,48,256]{3,2,1,0:T(8,128)(2,1)S(1)}, bf16[8,5,48,256]{3,2,1,0:T(8,128)(2,1)}, u32[]{:S(2)}, u32[]{:S(2)}) %collective-permute-start.10) | collective-permute-done | bytes 983072 | tf_op jit(solution)/shard_map/ppermute | solution.py:764
  82.5 4.8 bias_base.3.refs_12_
  87.4 15.6 %attention_forward.2 = (s32[1]{0:T(128)}, bf16[384,768]{1,0:T(8,128)(2,1)}, bf16[384,768]{1,0:T(8,128)(2,1)}, bf16[384,768]{1,0:T(8,128)(2,1)}, bf16[384,768]{1,...) custom-call(s32[2]{0:T(128)} %pad_add_fusion.core_ref, ...), custom_call_target="tpu_custom_call" | custom-call | flops 15000000512 | tf_op jit(solution)/shard_map/attention_forward/pallas_call | solution.py:551
  103.0 6.1 %all-to-all-start = ((bf16[16,40,768]{2,1,0:T(8,128)(2,1)}), bf16[16,40,768]{2,1,0:T(8,128)(2,1)S(1)}, u32[]{:S(2)}, u32[]{:S(2)}) async-start(bf16[16,40,768]{2,1,0:T(8,128)(2,1)} %bitcast.111), calls=%async_computation | async-start | bytes 1966080 | tf_op jit(solution)/shard_map/all_to_all | solution.py:939
  123.6 8.0 %all-to-all-done = bf16[16,40,768]{2,1,0:T(8,128)(2,1)S(1)} async-done(((bf16[16,40,768]{2,1,0:T(8,128)(2,1)}), bf16[16,40,768]{2,1,0:T(8,128)(2,1)S(1)}, u32[]{:S(2)}, u32[]{:S(2)}) %all-to-all-start) | async-done | bytes 983072 | tf_op jit(solution)/shard_map/all_to_all | solution.py:939
  131.6 13.9 %expert_forward.2 = (bf16[640,3072]{1,0:T(8,128)(2,1)}, bf16[640,3072]{1,0:T(8,128)(2,1)}, bf16[640,768]{1,0:T(8,128)(2,1)}) custom-call(s32[1]{0:T(128)} %bitcast.15.refs_0_, bf16[640,768]{1,0:T(8,128)(2,1)S(1)} %bitcast.104, bf16[768,3072]{1,0:T(8,128)(2,1)} %bitcast.121, bf16[768,3072]{1,0:T(8,128)(2,1)} %collective-permute-done.25.refs_3_.refs_4_, ...), custom_call_target="tpu_custom_call" | custom-call | flops 11000000512 | tf_op jit(solution)/shard_map/expert_forward/pallas_call | solution.py:701
  145.6 6.2 %all-to-all-start.1 = ((bf16[16,40,768]{2,1,0:T(8,128)(2,1)}), bf16[16,40,768]{2,1,0:T(8,128)(2,1)S(1)}, u32[]{:S(2)}, u32[]{:S(2)}) async-start(bf16[16,40,768]{2,1,0:T(8,128)(2,1)} %bitcast.116), calls=%async_computation.1 | async-start | bytes 1966080 | tf_op jit(solution)/shard_map/all_to_all | solution.py:939
  153.8 4.8 bias_base.2.refs_12_
  158.6 15.0 %all-to-all-done.1 = bf16[16,40,768]{2,1,0:T(8,128)(2,1)S(1)} async-done(((bf16[16,40,768]{2,1,0:T(8,128)(2,1)}), bf16[16,40,768]{2,1,0:T(8,128)(2,1)S(1)}, u32[]{:S(2)}, u32[]{:S(2)}) %all-to-all-start.1) | async-done | bytes 983072 | tf_op jit(solution)/shard_map/all_to_all | solution.py:939
  174.6 17.5 %attention_forward.3 = (s32[1]{0:T(128)}, bf16[384,768]{1,0:T(8,128)(2,1)}, bf16[384,768]{1,0:T(8,128)(2,1)}, bf16[384,768]{1,0:T(8,128)(2,1)}, bf16[384,768]{1,...) custom-call(s32[2]{0:T(128)} %pad_add_fusion.core_ref, ...), custom_call_target="tpu_custom_call" | custom-call | flops 15000000512 | tf_op jit(solution)/shard_map/attention_forward/pallas_call | solution.py:551
  192.2 29.6 %all_to_all.74 = bf16[16,40,768]{2,1,0:T(8,128)(2,1)} all-to-all(bf16[16,40,768]{2,1,0:T(8,128)(2,1)} %bitcast.115), channel_id=1, replica_groups=mesh['section'=2,'expert'=16] {'expert'}, dimensions={0} | all-to-all | bytes 1966080 | tf_op jit(solution)/shard_map/all_to_all | solution.py:939
  225.5 14.9 %expert_forward.3 = (bf16[640,3072]{1,0:T(8,128)(2,1)}, bf16[640,3072]{1,0:T(8,128)(2,1)}, bf16[640,768]{1,0:T(8,128)(2,1)}) custom-call(s32[1]{0:T(128)} %bitcast.23.refs_0_, bf16[640,768]{1,0:T(8,128)(2,1)} %bitcast.25.refs_1_, bf16[768,3072]{1,0:T(8,128)(2,1)} %bitcast.122, bf16[768,3072]{1,0:T(8,128)(2,1)} %collective-permute-done.25.refs_3_.refs_4_, ...), custom_call_target="tpu_custom_call" | custom-call | flops 11000000512 | tf_op jit(solution)/shard_map/expert_forward/pallas_call | solution.py:701
  240.4 6.8 %all-to-all-done.3 = bf16[16,40,768]{2,1,0:T(8,128)(2,1)S(1)} async-done(((bf16[16,40,768]{2,1,0:T(8,128)(2,1)}), bf16[16,40,768]{2,1,0:T(8,128)(2,1)S(1)}, u32[]{:S(2)}, u32[]{:S(2)}) %all-to-all-start.3) | async-done | bytes 983072 | tf_op jit(solution)/shard_map/all_to_all | solution.py:939
  247.2 12.4 %expert_backward.2 = (bf16[640,3072]{1,0:T(8,128)(2,1)}, bf16[640,768]{1,0:T(8,128)(2,1)}) custom-call(s32[1]{0:T(128)} %bitcast.23.refs_0_, bf16[640,768]{1,0:T(8,128)(2,1)S(1)} %bitcast.107, bf16[640,3072]{1,0:T(8,128)(2,1)} %get-tuple-element.189.refs_2_, bf16[768,3072]{1,0:T(8,128)(2,1)} %bitcast.123, ...), custom_call_target="tpu_custom_call" | custom-call | flops 11000000512 | tf_op jit(solution)/shard_map/expert_backward/pallas_call | solution.py:701
  261.2 47.0 %all_to_all.75 = bf16[16,72,768]{2,1,0:T(8,128)(2,1)} all-to-all(bf16[16,72,768]{2,1,0:T(8,128)(2,1)S(1)} %pad_maximum_fusion), channel_id=1, replica_groups=mesh['section'=2,'expert'=16] {'expert'}, dimensions={0} | all-to-all | bytes 3538944 | tf_op jit(solution)/shard_map/all_to_all | solution.py:939
  308.2 19.1 %heads_backward.2 = (s32[1]{0:T(128)}, f32[384,768]{1,0:T(8,128)}, bf16[384,768]{1,0:T(8,128)(2,1)}, bf16[384,768]{1,0:T(8,128)(2,1)}, bf16[384,768]{1,0:T(8,128...) custom-call(s32[2]{0:T(128)} %pad_add_fusion.core_ref, ...), custom_call_target="tpu_custom_call" | custom-call | flops 20000000000 | tf_op jit(solution)/shard_map/heads_backward/pallas_call | solution.py:551
  327.3 8.9 %input_backward.2 = (s32[1]{0:T(128)}, f32[384,768]{1,0:T(8,128)}, f32[1,768]{1,0:T(1,128)}, bf16[384,768]{1,0:T(8,128)(2,1)}, bf16[640,768]{1,0:T(8,128)(2,1)}) custom-call(s32[2]{0:T(128)} %pad_add_fusion.core_ref, bf16[8,5,48,256]{3,2,1,0:T(8,128)(2,1)} %copy-done.8, bf16[8,5,48,256]{3,2,1,0:T(8,128)(2,1)} %collective-permute-done.10.refs_1_, ...), custom_call_target="tpu_custom_call" | custom-call | flops 6000000000 | tf_op jit(solution)/shard_map/input_backward/pallas_call | solution.py:551
  336.2 4.3 all-to-all-start.5
  342.5 8.9 %weight_backward.2 = (s32[1]{0:T(128)}, bf16[2,768,768]{2,1,0:T(8,128)(2,1)}, bf16[2,768,768]{2,1,0:T(8,128)(2,1)}) custom-call(s32[2]{0:T(128)} %broadcast_add_fusion.2.core_ref, bf16[384,768]{1,0:T(8,128)(2,1)} %get-tuple-element.177.refs_12_.refs_0_, f32[2,768]{1,0:T(2,128)} %get-tuple-element.325.refs_18_.refs_23_.refs_17_.refs_1_, ...), custom_call_target="tpu_custom_call" | custom-call | flops 6000000000 | tf_op jit(solution)/shard_map/weight_backward/pallas_call | solution.py:551
  352.0 10.2 %all-to-all-done.5 = bf16[16,40,768]{2,1,0:T(8,128)(2,1)} async-done(((bf16[16,40,768]{2,1,0:T(8,128)(2,1)}), bf16[16,40,768]{2,1,0:T(8,128)(2,1)}, u32[]{:S(2)}, u32[]{:S(2)}) %all-to-all-start.5) | async-done | bytes 983072 | tf_op jit(solution)/shard_map/all_to_all | solution.py:939
  362.2 12.7 %expert_backward.3 = (bf16[640,3072]{1,0:T(8,128)(2,1)}, bf16[640,768]{1,0:T(8,128)(2,1)}) custom-call(s32[1]{0:T(128)S(6)} %add.242.refs_0_, bf16[640,768]{1,0:T(8,128)(2,1)} %bitcast.36.refs_1_, bf16[640,3072]{1,0:T(8,128)(2,1)} %get-tuple-element.209.refs_2_, bf16[768,3072]{1,0:T(8,128)(2,1)} %bitcast.124, ...), custom_call_target="tpu_custom_call" | custom-call | flops 11000000512 | tf_op jit(solution)/shard_map/expert_backward/pallas_call | solution.py:701
  374.8 5.8 %all-to-all-start.6 = ((bf16[16,40,768]{2,1,0:T(8,128)(2,1)}), bf16[16,40,768]{2,1,0:T(8,128)(2,1)}, u32[]{:S(2)}, u32[]{:S(2)}) async-start(bf16[16,40,768]{2,1,0:T(8,128)(2,1)} %bitcast.110), calls=%async_computation.6 | async-start | bytes 1966080 | tf_op jit(solution)/shard_map/all_to_all | solution.py:939
  387.9 12.7 %conditional.2 = (f32[3072,768]{1,0:T(8,128)}) conditional(s32[]{:T(128)} %convert_element_type.239, (bf16[640,768]{1,0:T(8,128)(2,1)S(1)}, bf16[640,768]{1,0:T(8,128)(2,1)}, bf16[640,3072]{1,0:T(8,128)(2,1)}, bf16[640,3072]{1,0:T(8,128)(2,1)}) %tuple.52, (bf16[640,768]{1,0:T(8,128)(2,1)}, bf16[640,768]{1,0:T(8,128)(2,1)}, ...), branch_computations={%region_4.5_spmd, %region_5.6_spmd} | conditional | flops 10000000000 | bytes 8 | solution.py:1015
  387.9 12.7 %down_gradient.3 = f32[3072,768]{1,0:T(8,128)} custom-call(bf16[640,768]{1,0:T(8,128)(2,1)} %get-tuple-element.42.dout_a, bf16[640,768]{1,0:T(8,128)(2,1)} %get-tuple-element.43.dout_b, bf16[640,3072]{1,0:T(8,128)(2,1)} %get-tuple-element.44.act_a, bf16[640,3072]{1,0:T(8,128)(2,1)} %get-tuple-element.45.act_b), custom_call_target="tpu_custom_call" | custom-call | flops 10000000000 | tf_op jit(solution)/shard_map/cond/branch_1_fun/down_gradient/pallas_call | solution.py:743
  402.4 17.0 %heads_backward.3 = (s32[1]{0:T(128)}, f32[384,768]{1,0:T(8,128)}, bf16[384,768]{1,0:T(8,128)(2,1)}, bf16[384,768]{1,0:T(8,128)(2,1)}, bf16[384,768]{1,0:T(8,128...) custom-call(s32[2]{0:T(128)} %pad_add_fusion.core_ref, ...), custom_call_target="tpu_custom_call" | custom-call | flops 20000000000 | tf_op jit(solution)/shard_map/heads_backward/pallas_call | solution.py:551
  419.5 9.1 %weight_backward.3 = (s32[1]{0:T(128)}, bf16[2,768,768]{2,1,0:T(8,128)(2,1)}, bf16[2,768,768]{2,1,0:T(8,128)(2,1)}) custom-call(s32[2]{0:T(128)} %pad_add_fusion.core_ref, bf16[384,768]{1,0:T(8,128)(2,1)} %select_bitcast_fusion.5.refs_13_.refs_0_.refs_12_, f32[2,768]{1,0:T(2,128)} %copy-done.3, bf16[384,768]{1,0:T(8,128)(2,1)} %get-tuple-element.192.refs_2_, ...), custom_call_target="tpu_custom_call" | custom-call | flops 6000000000 | tf_op jit(solution)/shard_map/weight_backward/pallas_call | solution.py:551
  435.2 7.6 %input_backward.3 = (s32[1]{0:T(128)}, f32[384,768]{1,0:T(8,128)}, f32[1,768]{1,0:T(1,128)}) custom-call(s32[2]{0:T(128)} %broadcast_add_fusion.1.core_ref, bf16[8,5,48,256]{3,2,1,0:T(8,128)(2,1)} %copy-done.8, bf16[8,5,48,256]{3,2,1,0:T(8,128)(2,1)} %collective-permute-done.10.refs_1_, bf16[8,4,48,256]{3,2,1,0:T(8,128)(2,1)} %copy-done.10, ...), custom_call_target="tpu_custom_call" | custom-call | flops 6000000000 | tf_op jit(solution)/shard_map/input_backward/pallas_call | solution.py:551
  461.7 12.7 %conditional.3 = (f32[768,3072]{1,0:T(8,128)}) conditional(s32[]{:T(128)} %convert_element_type.241, (bf16[640,768]{1,0:T(8,128)(2,1)}, bf16[640,768]{1,0:T(8,128)(2,1)}, bf16[640,3072]{1,0:T(8,128)(2,1)}, bf16[640,3072]{1,0:T(8,128)(2,1)}) %tuple.22, (bf16[640,768]{1,0:T(8,128)(2,1)}, bf16[640,768]{1,0:T(8,128)(2,1)}, bf16[640,3072]{1,0:T(8,128)(2,1)}, ...), branch_computations={%region_6.7_spmd, %region_7.8_spmd} | conditional | flops 10000000000 | bytes 8 | solution.py:1015
  461.7 12.6 %up_gradient.3 = f32[768,3072]{1,0:T(8,128)} custom-call(bf16[640,768]{1,0:T(8,128)(2,1)} %get-tuple-element.50.buf_a, bf16[640,768]{1,0:T(8,128)(2,1)} %get-tuple-element.51.buf_b, bf16[640,3072]{1,0:T(8,128)(2,1)} %get-tuple-element.52.dpre_a, bf16[640,3072]{1,0:T(8,128)(2,1)} %get-tuple-element.53.dpre_b), custom_call_target="tpu_custom_call" | custom-call | flops 10000000000 | tf_op jit(solution)/shard_map/cond/branch_1_fun/up_gradient/pallas_call | solution.py:725
  (288 shorter events, 154.0 us)
Async XLA Ops:
  2.5 18.5 %collective-permute-start = (bf16[1,5,48,256]{3,2,1,0:T(8,128)(2,1)S(1)}, bf16[1,5,48,256]{3,2,1,0:T(8,128)(2,1)S(1)}, u32[]{:S(2)}, u32[]{:S(2)}) collective-permute-start(bf16[1,5,48,256]{3,2,1,0:T(8,128)(2,1)S(1)} %fusion.10.refs_0_), channel_id=1, source_target_pairs={{0,8},{1,9},{2,10},{3,11},{4,12},{5,13},{6,14},{7,15},{8,0},{9,1},... | collective-permute-start | bytes 368648 | tf_op jit(solution)/shard_map/ppermute | solution.py:764
  6.6 13.1 %collective-permute-start.1 = (bf16[1,4,48,256]{3,2,1,0:T(8,128)(2,1)S(1)}, bf16[1,4,48,256]{3,2,1,0:T(8,128)(2,1)S(1)}, u32[]{:S(2)}, u32[]{:S(2)}) collective-permute-start(bf16[1,4,48,256]{3,2,1,0:T(8,128)(2,1)S(1)} %get-tuple-element.322.refs_1_), channel_id=1, source_target_pairs={{0,8},{1,9},{2,10},{3,11},{4,12},{5,13},{6,14},{7,15},{8,0},{9,1},... | collective-permute-start | bytes 294920 | tf_op jit(solution)/shard_map/ppermute | solution.py:764
  6.7 14.3 %collective-permute-start.2 = (bf16[1,4,48,256]{3,2,1,0:T(8,128)(2,1)S(1)}, bf16[1,4,48,256]{3,2,1,0:T(8,128)(2,1)S(1)}, u32[]{:S(2)}, u32[]{:S(2)}) collective-permute-start(bf16[1,4,48,256]{3,2,1,0:T(8,128)(2,1)S(1)} %get-tuple-element.320.refs_2_), channel_id=1, source_target_pairs={{0,8},{1,9},{2,10},{3,11},{4,12},{5,13},{6,14},{7,15},{8,0},{9,1},... | collective-permute-start | bytes 294920 | tf_op jit(solution)/shard_map/ppermute | solution.py:764
  31.0 11.7 %collective-permute-start.6 = (bf16[4,5,48,256]{3,2,1,0:T(8,128)(2,1)S(1)}, bf16[4,5,48,256]{3,2,1,0:T(8,128)(2,1)S(1)}, u32[]{:S(2)}, u32[]{:S(2)}) collective-permute-start(bf16[4,5,48,256]{3,2,1,0:T(8,128)(2,1)S(1)} %get-tuple-element.167.refs_0_), channel_id=1, source_target_pairs={{0,1},{1,0},{2,3},{3,2},{4,5},{5,4},{6,7},{7,6},{8,9},{9,8},{10,11... | collective-permute-start | bytes 1474568 | tf_op jit(solution)/shard_map/ppermute | solution.py:764
  47.3 17.2 %collective-permute-start.11 = (bf16[8,4,48,256]{3,2,1,0:T(8,128)(2,1)S(1)}, bf16[8,4,48,256]{3,2,1,0:T(8,128)(2,1)}, u32[]{:S(2)}, u32[]{:S(2)}) collective-permute-start(bf16[8,4,48,256]{3,2,1,0:T(8,128)(2,1)S(1)} %get-tuple-element.171.refs_2_), channel_id=1, source_target_pairs={{0,4},{1,5},{2,6},{3,7},{4,0},{5,1},{6,2},{7,3},{8,12},{9,13},{10,... | collective-permute-start | bytes 2359304 | tf_op jit(solution)/shard_map/ppermute | solution.py:764
  48.6 17.3 %collective-permute-start.12 = (bf16[8,4,48,256]{3,2,1,0:T(8,128)(2,1)S(1)}, bf16[8,4,48,256]{3,2,1,0:T(8,128)(2,1)}, u32[]{:S(2)}, u32[]{:S(2)}) collective-permute-start(bf16[8,4,48,256]{3,2,1,0:T(8,128)(2,1)S(1)} %get-tuple-element.172.refs_4_), channel_id=1, source_target_pairs={{0,1},{1,0},{2,3},{3,2},{4,5},{5,4},{6,7},{7,6},{8,9},{9,8},{10,11... | collective-permute-start | bytes 2359304 | tf_op jit(solution)/shard_map/ppermute | solution.py:764
  49.4 16.6 %collective-permute-start.21 = (bf16[8,4,48,256]{3,2,1,0:T(8,128)(2,1)S(1)}, bf16[8,4,48,256]{3,2,1,0:T(8,128)(2,1)S(1)}, u32[]{:S(2)}, u32[]{:S(2)}) collective-permute-start(bf16[8,4,48,256]{3,2,1,0:T(8,128)(2,1)S(1)} %get-tuple-element.171.refs_2_), channel_id=1, source_target_pairs={{0,16},{1,17},{2,18},{3,19},{4,20},{5,21},{6,22},{7,23},{8,24},{9,... | collective-permute-start | bytes 2359304 | tf_op jit(solution)/shard_map/ppermute | solution.py:760
  50.7 21.5 %collective-permute-start.10 = (bf16[8,5,48,256]{3,2,1,0:T(8,128)(2,1)S(1)}, bf16[8,5,48,256]{3,2,1,0:T(8,128)(2,1)}, u32[]{:S(2)}, u32[]{:S(2)}) collective-permute-start(bf16[8,5,48,256]{3,2,1,0:T(8,128)(2,1)S(1)} %get-tuple-element.170.refs_0_), channel_id=1, source_target_pairs={{0,2},{1,3},{2,0},{3,1},{4,6},{5,7},{6,4},{7,5},{8,10},{9,11},{10,... | collective-permute-start | bytes 2949128 | tf_op jit(solution)/shard_map/ppermute | solution.py:764
  52.3 24.4 %collective-permute-start.19 = (bf16[8,5,48,256]{3,2,1,0:T(8,128)(2,1)S(1)}, bf16[8,5,48,256]{3,2,1,0:T(8,128)(2,1)S(1)}, u32[]{:S(2)}, u32[]{:S(2)}) collective-permute-start(bf16[8,5,48,256]{3,2,1,0:T(8,128)(2,1)S(1)} %get-tuple-element.170.refs_0_), channel_id=1, source_target_pairs={{0,16},{1,17},{2,18},{3,19},{4,20},{5,21},{6,22},{7,23},{8,24},{9,... | collective-permute-start | bytes 2949128 | tf_op jit(solution)/shard_map/ppermute | solution.py:760
  65.9 65.7 %collective-permute-start.25 = (bf16[768,3072]{1,0:T(8,128)(2,1)}, bf16[768,3072]{1,0:T(8,128)(2,1)}, u32[]{:S(2)}, u32[]{:S(2)}) collective-permute-start(bf16[768,3072]{1,0:T(8,128)(2,1)} %bitcast.120), channel_id=1, source_target_pairs={{0,16},{16,0},{1,17},{17,1},{2,18},{18,2},{3,19},{19,3},{4,20},{20... | collective-permute-start | bytes 14155784 | tf_op jit(solution)/shard_map/ppermute | solution.py:756
  66.0 65.6 %collective-permute-start.26 = (bf16[3072,768]{1,0:T(8,128)(2,1)}, bf16[3072,768]{1,0:T(8,128)(2,1)}, u32[]{:S(2)}, u32[]{:S(2)}) collective-permute-start(bf16[3072,768]{1,0:T(8,128)(2,1)} %bitcast.125), channel_id=1, source_target_pairs={{0,16},{16,0},{1,17},{17,1},{2,18},{18,2},{3,19},{19,3},{4,20},{20... | collective-permute-start | bytes 14155784 | tf_op jit(solution)/shard_map/ppermute | solution.py:756
  72.2 15.3 %collective-permute-start.20 = (bf16[8,5,48,256]{3,2,1,0:T(8,128)(2,1)}, bf16[8,5,48,256]{3,2,1,0:T(8,128)(2,1)}, u32[]{:S(2)}, u32[]{:S(2)}) collective-permute-start(bf16[8,5,48,256]{3,2,1,0:T(8,128)(2,1)} %collective-permute-done.10.refs_1_), channel_id=1, source_target_pairs={{0,16},{1,17},{2,18},{3,19},{4,20},{5,21},{6,22},{7,23},{8,24},{9,... | collective-permute-start | bytes 2949128 | tf_op jit(solution)/shard_map/ppermute | solution.py:760
  74.5 12.9 %collective-permute-start.22 = (bf16[8,4,48,256]{3,2,1,0:T(8,128)(2,1)}, bf16[8,4,48,256]{3,2,1,0:T(8,128)(2,1)}, u32[]{:S(2)}, u32[]{:S(2)}) collective-permute-start(bf16[8,4,48,256]{3,2,1,0:T(8,128)(2,1)} %collective-permute-done.11.refs_3_), channel_id=1, source_target_pairs={{0,16},{1,17},{2,18},{3,19},{4,20},{5,21},{6,22},{7,23},{8,24},{9,... | collective-permute-start | bytes 2359304 | tf_op jit(solution)/shard_map/ppermute | solution.py:760
  103.0 28.6 %all-to-all-start = ((bf16[16,40,768]{2,1,0:T(8,128)(2,1)}), bf16[16,40,768]{2,1,0:T(8,128)(2,1)S(1)}, u32[]{:S(2)}, u32[]{:S(2)}) async-start(bf16[16,40,768]{2,1,0:T(8,128)(2,1)} %bitcast.111), calls=%async_computation | async-start | bytes 1966080 | tf_op jit(solution)/shard_map/all_to_all | solution.py:939
  145.6 28.0 %all-to-all-start.1 = ((bf16[16,40,768]{2,1,0:T(8,128)(2,1)}), bf16[16,40,768]{2,1,0:T(8,128)(2,1)S(1)}, u32[]{:S(2)}, u32[]{:S(2)}) async-start(bf16[16,40,768]{2,1,0:T(8,128)(2,1)} %bitcast.116), calls=%async_computation.1 | async-start | bytes 1966080 | tf_op jit(solution)/shard_map/all_to_all | solution.py:939
  221.8 25.4 %all-to-all-start.3 = ((bf16[16,40,768]{2,1,0:T(8,128)(2,1)}), bf16[16,40,768]{2,1,0:T(8,128)(2,1)S(1)}, u32[]{:S(2)}, u32[]{:S(2)}) async-start(bf16[16,40,768]{2,1,0:T(8,128)(2,1)} %bitcast.114), calls=%async_computation.3 | async-start | bytes 1966080 | tf_op jit(solution)/shard_map/all_to_all | solution.py:939
  336.2 25.9 %all-to-all-start.5 = ((bf16[16,40,768]{2,1,0:T(8,128)(2,1)}), bf16[16,40,768]{2,1,0:T(8,128)(2,1)}, u32[]{:S(2)}, u32[]{:S(2)}) async-start(bf16[16,40,768]{2,1,0:T(8,128)(2,1)} %bitcast.112), calls=%async_computation.5 | async-start | bytes 1966080 | tf_op jit(solution)/shard_map/all_to_all | solution.py:939
  340.6 44.4 %collective-permute-start.29 = (bf16[640,3072]{1,0:T(8,128)(2,1)}, bf16[640,3072]{1,0:T(8,128)(2,1)}, u32[]{:S(2)}, u32[]{:S(2)}) collective-permute-start(bf16[640,3072]{1,0:T(8,128)(2,1)} %get-tuple-element.212), channel_id=1, source_target_pairs={{0,16},{16,0},{1,17},{17,1},{2,18},{18,2},{3,19},{19,3},{4,20},{20... | collective-permute-start | bytes 11796488 | tf_op jit(solution)/shard_map/ppermute | solution.py:756
  340.7 47.3 %collective-permute-start.31 = (bf16[640,3072]{1,0:T(8,128)(2,1)}, bf16[640,3072]{1,0:T(8,128)(2,1)}, u32[]{:S(2)}, u32[]{:S(2)}) collective-permute-start(bf16[640,3072]{1,0:T(8,128)(2,1)} %get-tuple-element.213), channel_id=1, source_target_pairs={{0,16},{16,0},{1,17},{17,1},{2,18},{18,2},{3,19},{19,3},{4,20},{20... | collective-permute-start | bytes 11796488 | tf_op jit(solution)/shard_map/ppermute | solution.py:756
  374.8 27.6 %all-to-all-start.6 = ((bf16[16,40,768]{2,1,0:T(8,128)(2,1)}), bf16[16,40,768]{2,1,0:T(8,128)(2,1)}, u32[]{:S(2)}, u32[]{:S(2)}) async-start(bf16[16,40,768]{2,1,0:T(8,128)(2,1)} %bitcast.110), calls=%async_computation.6 | async-start | bytes 1966080 | tf_op jit(solution)/shard_map/all_to_all | solution.py:939
  381.2 73.7 %collective-permute-start.41 = (bf16[640,3072]{1,0:T(8,128)(2,1)}, bf16[640,3072]{1,0:T(8,128)(2,1)}, u32[]{:S(2)}, u32[]{:S(2)}) collective-permute-start(bf16[640,3072]{1,0:T(8,128)(2,1)} %get-tuple-element.241), channel_id=1, source_target_pairs={{0,16},{16,0},{1,17},{17,1},{2,18},{18,2},{3,19},{19,3},{4,20},{20... | collective-permute-start | bytes 11796488 | tf_op jit(solution)/shard_map/ppermute | solution.py:756
  384.9 58.0 %collective-permute-start.35 = (bf16[2,768,768]{2,1,0:T(8,128)(2,1)}, bf16[2,768,768]{2,1,0:T(8,128)(2,1)S(1)}, u32[]{:S(2)}, u32[]{:S(2)}) collective-permute-start(bf16[2,768,768]{2,1,0:T(8,128)(2,1)} %get-tuple-element.233), channel_id=1, source_target_pairs={{0,16},{16,0},{1,17},{17,1},{2,18},{18,2},{3,19},{19,3},{4,20},{20... | collective-permute-start | bytes 7077896 | tf_op jit(solution)/shard_map/ppermute | solution.py:756
  387.5 69.5 %collective-permute-start.43 = (bf16[640,3072]{1,0:T(8,128)(2,1)}, bf16[640,3072]{1,0:T(8,128)(2,1)}, u32[]{:S(2)}, u32[]{:S(2)}) collective-permute-start(bf16[640,3072]{1,0:T(8,128)(2,1)} %get-tuple-element.242), channel_id=1, source_target_pairs={{0,16},{16,0},{1,17},{17,1},{2,18},{18,2},{3,19},{19,3},{4,20},{20... | collective-permute-start | bytes 11796488 | tf_op jit(solution)/shard_map/ppermute | solution.py:756
  428.6 18.2 %collective-permute-start.34 = (bf16[2,768,768]{2,1,0:T(8,128)(2,1)}, bf16[2,768,768]{2,1,0:T(8,128)(2,1)S(1)}, u32[]{:S(2)}, u32[]{:S(2)}) collective-permute-start(bf16[2,768,768]{2,1,0:T(8,128)(2,1)} %get-tuple-element.231), channel_id=1, source_target_pairs={{0,16},{16,0},{1,17},{17,1},{2,18},{18,2},{3,19},{19,3},{4,20},{20... | collective-permute-start | bytes 7077896 | tf_op jit(solution)/shard_map/ppermute | solution.py:756
  434.3 16.5 %collective-permute-start.40 = (bf16[640,768]{1,0:T(8,128)(2,1)}, bf16[640,768]{1,0:T(8,128)(2,1)}, u32[]{:S(2)}, u32[]{:S(2)}) collective-permute-start(bf16[640,768]{1,0:T(8,128)(2,1)} %bitcast.25.refs_1_), channel_id=1, source_target_pairs={{0,16},{16,0},{1,17},{17,1},{2,18},{18,2},{3,19},{19,3},{4,20},{20... | collective-permute-start | bytes 2949128 | tf_op jit(solution)/shard_map/ppermute | solution.py:756
  446.8 32.6 %collective-permute-start.32 = (f32[384,768]{1,0:T(8,128)}, f32[384,768]{1,0:T(8,128)}, u32[]{:S(2)}, u32[]{:S(2)}) collective-permute-start(f32[384,768]{1,0:T(8,128)} %broadcast_select_fusion), channel_id=1, source_target_pairs={{0,16},{16,0},{1,17},{17,1},{2,18},{18,2},{3,19},{19,3},{4,20},{20... | collective-permute-start | bytes 3538952 | tf_op jit(solution)/shard_map/ppermute | solution.py:756
  450.8 23.6 %collective-permute-start.37 = (bf16[4,8,48,256]{3,2,1,0:T(8,128)(2,1)}, bf16[4,8,48,256]{3,2,1,0:T(8,128)(2,1)}, u32[]{:S(2)}, u32[]{:S(2)}) collective-permute-start(bf16[4,8,48,256]{3,2,1,0:T(8,128)(2,1)} %get-tuple-element.238), channel_id=1, source_target_pairs={{0,2},{1,3},{2,0},{3,1},{4,6},{5,7},{6,4},{7,5},{8,10},{9,11},{10,... | collective-permute-start | bytes 2359304 | tf_op jit(solution)/shard_map/ppermute | solution.py:764
  452.8 21.6 %collective-permute-start.38 = (bf16[4,8,48,256]{3,2,1,0:T(8,128)(2,1)}, bf16[4,8,48,256]{3,2,1,0:T(8,128)(2,1)}, u32[]{:S(2)}, u32[]{:S(2)}) collective-permute-start(bf16[4,8,48,256]{3,2,1,0:T(8,128)(2,1)} %get-tuple-element.239), channel_id=1, source_target_pairs={{0,4},{1,5},{2,6},{3,7},{4,0},{5,1},{6,2},{7,3},{8,12},{9,13},{10,... | collective-permute-start | bytes 2359304 | tf_op jit(solution)/shard_map/ppermute | solution.py:764
  454.9 20.7 %collective-permute-start.39 = (bf16[4,8,48,256]{3,2,1,0:T(8,128)(2,1)}, bf16[4,8,48,256]{3,2,1,0:T(8,128)(2,1)}, u32[]{:S(2)}, u32[]{:S(2)}) collective-permute-start(bf16[4,8,48,256]{3,2,1,0:T(8,128)(2,1)} %get-tuple-element.240), channel_id=1, source_target_pairs={{0,1},{1,0},{2,3},{3,2},{4,5},{5,4},{6,7},{7,6},{8,9},{9,8},{10,11... | collective-permute-start | bytes 2359304 | tf_op jit(solution)/shard_map/ppermute | solution.py:764
  459.6 22.0 %collective-permute-start.36 = (f32[30,768]{1,0:T(8,128)}, f32[30,768]{1,0:T(8,128)}, u32[]{:S(2)}, u32[]{:S(2)}) collective-permute-start(f32[30,768]{1,0:T(8,128)} %add_add_fusion.3), channel_id=1, source_target_pairs={{0,1},{1,0},{2,3},{3,2},{4,5},{5,4},{6,7},{7,6},{8,9},{9,8},{10,11... | collective-permute-start | bytes 276488 | tf_op jit(solution)/shard_map/ppermute | solution.py:764
  499.3 11.7 %collective-permute-start.52 = (f32[30,768]{1,0:T(8,128)S(1)}, f32[30,768]{1,0:T(8,128)S(1)}, u32[]{:S(2)}, u32[]{:S(2)}) collective-permute-start(f32[30,768]{1,0:T(8,128)S(1)} %add_add_fusion), channel_id=1, source_target_pairs={{0,8},{1,9},{2,10},{3,11},{4,12},{5,13},{6,14},{7,15},{8,0},{9,1},... | collective-permute-start | bytes 276488 | tf_op jit(solution)/shard_map/ppermute | solution.py:764
  502.4 11.5 %collective-permute-start.53 = (bf16[4,1,48,256]{3,2,1,0:T(8,128)(2,1)S(1)}, bf16[4,1,48,256]{3,2,1,0:T(8,128)(2,1)S(1)}, u32[]{:S(2)}, u32[]{:S(2)}) collective-permute-start(bf16[4,1,48,256]{3,2,1,0:T(8,128)(2,1)S(1)} %get-tuple-element.261), channel_id=1, source_target_pairs={{0,8},{1,9},{2,10},{3,11},{4,12},{5,13},{6,14},{7,15},{8,0},{9,1},... | collective-permute-start | bytes 294920 | tf_op jit(solution)/shard_map/ppermute | solution.py:764
  (84 other events, 781.7 us)
